TPU v7x, 128 devices: a whole 4x4x4 slice. The times are simulated.
128 devices in a mesh: dp: 4 (over x), vocab: 32 (over z, y, core).
Axes of the slice: x: 4, y: 4, z: 4, core: 2. Of those that a mesh axis runs over, the one named last changes fastest.
Arguments:
- token_ids: int32 [128, 128], P('dp'), may hold values from 0 to 50256
- seq_lengths: int32 [128], P('dp'), may hold values from 1 to 128, as said below
- loss_positions: int32 [128, 16], P('dp'), may hold values from 0 to 127, as said below
- target_ids: int32 [128, 16], P('dp'), may hold values from 0 to 50256
- block_of_slot: int32 [768], replicated, may hold values from 0 to 767, as said below
- matrices: float32 [768, 128, 128], P(('dp', 'vocab'))
- left_stats: float32 [768, 128, 128], P(('dp', 'vocab'))
- right_stats: float32 [768, 128, 128], P(('dp', 'vocab'))
- left_roots: float32 [768, 128, 128], P(('dp', 'vocab'))
- right_roots: float32 [768, 128, 128], P(('dp', 'vocab'))
- vocab_table: float32 [51200, 1024], P('vocab', 'dp')
- table_m: float32 [51200, 1024], P('vocab', 'dp')
- table_v: float32 [51200, 1024], P('vocab', 'dp')
- positions_table: float32 [128, 1024], replicated, may hold values from -0.6 to 0.6
- pos_m: float32 [128, 1024], replicated
- pos_v: float32 [128, 1024], replicated
- vectors: float32 [14, 1024], replicated
- vectors_m: float32 [14, 1024], replicated
- vectors_v: float32 [14, 1024], replicated
Outputs:
- loss_value: float32 [], replicated
- grad_norm: float32 [], replicated
- matrices_new: float32 [768, 128, 128], P(('dp', 'vocab'))
- left_new: float32 [768, 128, 128], P(('dp', 'vocab'))
- right_new: float32 [768, 128, 128], P(('dp', 'vocab'))
- matrices_grad: float32 [768, 128, 128], P(('dp', 'vocab'))
- vocab_table_new: float32 [51200, 1024], P('vocab', 'dp')
- table_m_new: float32 [51200, 1024], P('vocab', 'dp')
- table_v_new: float32 [51200, 1024], P('vocab', 'dp')
- positions_new: float32 [128, 1024], replicated
- pos_m_new: float32 [128, 1024], replicated
- pos_v_new: float32 [128, 1024], replicated
- vectors_new: float32 [14, 1024], replicated
- vectors_m_new: float32 [14, 1024], replicated
- vectors_v_new: float32 [14, 1024], replicated
Inputs may be any that keep to these rules, and one draw needn't show every extreme that they name: `seq_lengths`: the last sequence has all 128 slots live. `loss_positions`: distinct within each sequence. `block_of_slot`: a permutation of the 768 blocks.
All inputs are finite; a program needn't handle non-finite values.
Results may differ from a plain program's by a relative error of at most 0.014.
Values may be sent and summed in bfloat16 or wider, within the bound.
A program may use at most 256 MiB of HBM per device.

v0:
```python
import jax
import jax.numpy as jnp
from jax import lax
from jax.sharding import PartitionSpec as P

D = 1024
HEADS = 16
HEAD_DIM = 64
FF = 4096
VOCAB_REAL = 50257
LAYERS = 1
BLOCK = 128
STEP = 10


LN_EPS = 1e-05
CLIP_LEVEL = 0.05
BETA_ONE = 0.9
BETA_TWO = 0.999
ADAM_EPS = 1e-08
STAT_DECAY = 0.95
SHAMPOO_RATE = 0.03
TABLE_RATE = 0.15
POS_RATE = 0.05
VECTOR_RATE = 0.25
DECAY_RATE = 0.1
NEG_FILL = -1e30
GELU_C = 0.7978845608028654
HIGH = lax.Precision.HIGHEST


def layer_norm(values, gain_row, shift_row):
    center = values - jnp.mean(values, -1, keepdims=True)
    spread = jnp.mean(center * center, -1, keepdims=True)
    return center * lax.rsqrt(spread + LN_EPS) * gain_row + shift_row


def gelu(values):
    return 0.5 * values * (1.0 + jnp.tanh(GELU_C * (values + 0.044715 * values * values * values)))


def dot_nt(left, right):
    return lax.dot_general(
        left, right, (((1,), (1,)), ((), ())), preferred_element_type=jnp.float32
    )


def dot_tn(left, right):
    return lax.dot_general(
        left, right, (((0,), (0,)), ((), ())), preferred_element_type=jnp.float32
    )


def from_blocks(blocks, height, across):
    block_side = blocks.shape[-1]
    shaped = blocks.reshape(height // block_side, across // block_side, block_side, block_side)
    return shaped.transpose(0, 2, 1, 3).reshape(height, across)


def to_blocks(matrix):
    height, across = matrix.shape
    shaped = matrix.reshape(height // BLOCK, BLOCK, across // BLOCK, BLOCK)
    return shaped.transpose(0, 2, 1, 3).reshape(-1, BLOCK, BLOCK)


def unpack(blocks):
    square = (D // BLOCK) ** 2
    result = [
        (
            from_blocks(blocks[: 3 * square], D, 3 * D),
            from_blocks(blocks[3 * square : 4 * square], D, D),
            from_blocks(blocks[4 * square : 8 * square], D, FF),
            from_blocks(blocks[8 * square :], FF, D),
        )
    ]
    return result


def split_heads(matrix):
    return matrix.reshape(matrix.shape[0], HEADS, HEAD_DIM).transpose(1, 0, 2)


def merge_heads(matrix):
    return matrix.transpose(1, 0, 2).reshape(matrix.shape[1], HEADS * HEAD_DIM)


def masked_scores(q_heads, k_heads, own_length):
    seq_len = q_heads.shape[1]
    query_pos = jnp.arange(seq_len)[:, None]
    key_pos = jnp.arange(seq_len)[None, :]
    allowed = (key_pos <= query_pos) & (key_pos < own_length)
    raw_scores = jnp.einsum(
        "hqd,hkd->hqk", q_heads, k_heads, preferred_element_type=jnp.float32
    ) * HEAD_DIM ** (-0.5)
    return jnp.where(allowed[None], raw_scores, NEG_FILL)


def layer_forward(hidden, own_length, weight_set, vec_rows):
    w_qkv, w_proj, w_fc, w_out = weight_set
    normed_one = layer_norm(hidden, vec_rows[0], vec_rows[1]).astype(jnp.bfloat16)
    qkv_bias = jnp.concatenate([vec_rows[2], jnp.zeros_like(vec_rows[2]), vec_rows[3]])
    qkv_low = (jnp.dot(normed_one, w_qkv, preferred_element_type=jnp.float32) + qkv_bias).astype(
        jnp.bfloat16
    )
    q_heads = split_heads(qkv_low[:, :D])
    k_heads = split_heads(qkv_low[:, D : 2 * D])
    v_heads = split_heads(qkv_low[:, 2 * D :])
    scores = masked_scores(q_heads, k_heads, own_length)
    row_top = jnp.max(scores, -1, keepdims=True)
    exps_all = jnp.exp(scores - row_top)
    exp_total = jnp.sum(exps_all, -1, keepdims=True)
    probs_low = (exps_all / exp_total).astype(jnp.bfloat16)
    log_sums = row_top + jnp.log(exp_total)
    mixed = jnp.einsum("hqk,hkd->hqd", probs_low, v_heads, preferred_element_type=jnp.float32)
    attended = merge_heads(mixed).astype(jnp.bfloat16)
    middle = hidden + jnp.dot(attended, w_proj, preferred_element_type=jnp.float32) + vec_rows[4]
    normed_two = layer_norm(middle, vec_rows[5], vec_rows[6]).astype(jnp.bfloat16)
    pre_act = jnp.dot(normed_two, w_fc, preferred_element_type=jnp.float32) + vec_rows[
        7:11
    ].reshape(-1)
    activated = gelu(pre_act).astype(jnp.bfloat16)
    result = middle + jnp.dot(activated, w_out, preferred_element_type=jnp.float32) + vec_rows[11]
    return (
        result,
        (hidden, normed_one, qkv_low, log_sums, attended, middle, normed_two, pre_act, activated),
    )


def layer_backward(grad_out, own_length, weight_set, vec_rows, layer_cache):
    w_qkv, w_proj, w_fc, w_out = weight_set
    hidden, normed_one, qkv_low, log_sums, attended, middle, normed_two, pre_act, activated = (
        layer_cache
    )
    d_branch = grad_out.astype(jnp.bfloat16)
    g_out = dot_tn(activated, d_branch)
    b_out = jnp.sum(d_branch.astype(jnp.float32), 0)
    d_activated = dot_nt(d_branch, w_out)
    unused_act, gelu_pull = jax.vjp(gelu, pre_act)
    d_pre = gelu_pull(d_activated)[0].astype(jnp.bfloat16)
    g_fc = dot_tn(normed_two, d_pre)
    b_fc = jnp.sum(d_pre.astype(jnp.float32), 0)
    unused_two, norm_pull_two = jax.vjp(layer_norm, middle, vec_rows[5], vec_rows[6])
    d_middle, g_ln_two, b_ln_two = norm_pull_two(dot_nt(d_pre, w_fc))
    d_middle = d_middle + grad_out
    d_proj_in = d_middle.astype(jnp.bfloat16)
    g_proj = dot_tn(attended, d_proj_in)
    b_proj = jnp.sum(d_proj_in.astype(jnp.float32), 0)
    d_attended = split_heads(dot_nt(d_proj_in, w_proj).astype(jnp.bfloat16))
    q_heads = split_heads(qkv_low[:, :D])
    k_heads = split_heads(qkv_low[:, D : 2 * D])
    v_heads = split_heads(qkv_low[:, 2 * D :])
    probs_full = jnp.exp(masked_scores(q_heads, k_heads, own_length) - log_sums)
    d_values = jnp.einsum(
        "hqk,hqd->hkd",
        probs_full.astype(jnp.bfloat16),
        d_attended,
        preferred_element_type=jnp.float32,
    )
    d_probs = jnp.einsum("hqd,hkd->hqk", d_attended, v_heads, preferred_element_type=jnp.float32)
    inner_sum = jnp.sum(probs_full * d_probs, -1, keepdims=True)
    d_scores = (probs_full * (d_probs - inner_sum)).astype(jnp.bfloat16)
    d_queries = jnp.einsum(
        "hqk,hkd->hqd", d_scores, k_heads, preferred_element_type=jnp.float32
    ) * HEAD_DIM ** (-0.5)
    d_keys = jnp.einsum(
        "hqk,hqd->hkd", d_scores, q_heads, preferred_element_type=jnp.float32
    ) * HEAD_DIM ** (-0.5)
    d_qkv = jnp.concatenate(
        [merge_heads(d_queries), merge_heads(d_keys), merge_heads(d_values)], 1
    ).astype(jnp.bfloat16)
    g_qkv = dot_tn(normed_one, d_qkv)
    d_qkv_sums = jnp.sum(d_qkv.astype(jnp.float32), 0)
    unused_one, norm_pull_one = jax.vjp(layer_norm, hidden, vec_rows[0], vec_rows[1])
    d_hidden, g_ln_one, b_ln_one = norm_pull_one(dot_nt(d_qkv, w_qkv))
    d_hidden = d_hidden + d_middle
    vec_grad = jnp.concatenate(
        [
            jnp.stack(
                [
                    g_ln_one,
                    b_ln_one,
                    d_qkv_sums[:D],
                    d_qkv_sums[2 * D :],
                    b_proj,
                    g_ln_two,
                    b_ln_two,
                ]
            ),
            b_fc.reshape(FF // D, D),
            b_out[None],
        ],
        0,
    )
    return (d_hidden, (g_qkv, g_proj, g_fc, g_out), vec_grad)


def adamw(weight, moment_one, moment_two, grad_in, rate, decay):
    new_one = BETA_ONE * moment_one + (1.0 - BETA_ONE) * grad_in
    new_two = BETA_TWO * moment_two + (1.0 - BETA_TWO) * grad_in * grad_in
    hat_one = new_one / (1.0 - BETA_ONE**STEP)
    hat_two = new_two / (1.0 - BETA_TWO**STEP)
    new_weight = weight - rate * (hat_one / (jnp.sqrt(hat_two) + ADAM_EPS) + decay * weight)
    return (new_weight, new_one, new_two)


def per_device(
    token_ids,
    seq_lengths,
    loss_positions,
    target_ids,
    block_of_slot,
    matrices,
    left_stats,
    right_stats,
    left_roots,
    right_roots,
    vocab_table,
    table_m,
    table_v,
    positions_table,
    pos_m,
    pos_v,
    vectors,
    vectors_m,
    vectors_v,
):
    vocab_index = lax.axis_index("vocab")
    vocab_devices = lax.axis_size("vocab")
    all_devices = lax.axis_size("dp") * vocab_devices
    loss_rows = loss_positions.shape[1]
    gathered = lax.all_gather(matrices.astype(jnp.bfloat16), ("dp", "vocab"), axis=0, tiled=True)
    inverse = jnp.argsort(block_of_slot)
    weights = unpack(jnp.take(gathered, inverse, axis=0))
    table_rows = lax.all_gather(vocab_table.astype(jnp.bfloat16), "dp", axis=1, tiled=True)
    local_rows = table_rows.shape[0]
    group_ids = token_ids.reshape(-1) - vocab_index * local_rows
    row_iota = jnp.arange(local_rows, dtype=jnp.int32)

    def one_hot():
        return (group_ids[:, None] == row_iota[None, :]).astype(jnp.bfloat16)

    embedded = lax.psum_scatter(
        jnp.dot(one_hot(), table_rows, preferred_element_type=jnp.float32).astype(jnp.bfloat16),
        "vocab",
        scatter_dimension=0,
        tiled=True,
    ).astype(jnp.float32)
    own_length = lax.dynamic_index_in_dim(seq_lengths, vocab_index, keepdims=False)
    own_positions = lax.dynamic_index_in_dim(loss_positions, vocab_index, keepdims=False)
    hidden = embedded + positions_table
    layer_idx = 0
    hidden, layer_cache = layer_forward(
        hidden, own_length, weights[layer_idx], vectors[12 * layer_idx : 12 * layer_idx + 12]
    )
    caches = [layer_cache]
    final_gain = vectors[12 * LAYERS]
    final_bias = vectors[12 * LAYERS + 1]
    selected = jnp.take(hidden, own_positions, axis=0)
    head_in = layer_norm(selected, final_gain, final_bias).astype(jnp.bfloat16)
    group_in = lax.all_gather(head_in, "vocab", axis=0, tiled=True)
    logits = dot_nt(group_in, table_rows)
    columns = vocab_index * local_rows + row_iota
    live_rows = columns < VOCAB_REAL
    masked = jnp.where(live_rows[None], logits, NEG_FILL)
    target_hits = columns[None, :] == target_ids.reshape(-1)[:, None]
    local_top = jnp.max(masked, -1)
    local_total = jnp.sum(jnp.exp(masked - local_top[:, None]), -1)
    local_pick = jnp.sum(jnp.where(target_hits, logits, 0.0), -1)
    top_all = lax.pmax(local_top, "vocab")
    total_all = lax.psum(local_total * jnp.exp(local_top - top_all), "vocab")
    log_total = top_all + jnp.log(total_all)
    counted_rows = (loss_positions < seq_lengths[:, None]).reshape(-1).astype(jnp.float32)
    weight_rows = counted_rows / (all_devices * loss_rows)
    lse_part = jnp.where(vocab_index == 0, jnp.sum(log_total * counted_rows), 0.0)
    loss_share = lse_part - jnp.sum(local_pick * counted_rows)
    d_logits = (
        (jnp.exp(masked - log_total[:, None]) - target_hits.astype(jnp.float32))
        * weight_rows[:, None]
    ).astype(jnp.bfloat16)
    d_head_in = lax.psum_scatter(
        jnp.dot(d_logits, table_rows, preferred_element_type=jnp.float32),
        "vocab",
        scatter_dimension=0,
        tiled=True,
    )
    table_grad = dot_tn(d_logits, group_in)
    unused_final, final_pull = jax.vjp(layer_norm, selected, final_gain, final_bias)
    d_selected, g_final, b_final = final_pull(d_head_in)
    d_hidden = jnp.zeros_like(hidden).at[own_positions].add(d_selected)
    layer_grads = [None] * LAYERS
    layer_vec = [None] * LAYERS
    for layer_idx in reversed(range(LAYERS)):
        d_hidden, grads_here, vec_here = layer_backward(
            d_hidden,
            own_length,
            weights[layer_idx],
            vectors[12 * layer_idx : 12 * layer_idx + 12],
            caches[layer_idx],
        )
        layer_grads[layer_idx] = grads_here
        layer_vec[layer_idx] = vec_here
    vec_grads = jnp.concatenate(layer_vec + [jnp.stack([g_final, b_final])], 0)
    d_embed = d_hidden.astype(jnp.bfloat16)
    table_grad = table_grad + dot_tn(
        one_hot(), lax.all_gather(d_embed, "vocab", axis=0, tiled=True)
    )
    table_grad_own = lax.psum_scatter(table_grad, "dp", scatter_dimension=1, tiled=True)
    block_parts = []
    layer_idx = 0
    for grad_matrix in layer_grads[layer_idx]:
        block_parts.append(to_blocks(grad_matrix))
    grad_blocks = jnp.concatenate(block_parts, 0)
    owned_grads = lax.psum_scatter(
        jnp.take(grad_blocks, block_of_slot, axis=0),
        ("dp", "vocab"),
        scatter_dimension=0,
        tiled=True,
    )
    squares = jnp.sum(owned_grads * owned_grads) + jnp.sum(table_grad_own * table_grad_own)
    pos_grad, vec_sum, squares_all, loss_value = lax.psum(
        (d_hidden, vec_grads, squares, loss_share), ("dp", "vocab")
    )
    grad_norm = jnp.sqrt(squares_all + jnp.sum(pos_grad * pos_grad) + jnp.sum(vec_sum * vec_sum))
    clip_factor = CLIP_LEVEL / jnp.maximum(grad_norm, CLIP_LEVEL)
    matrices_grad = owned_grads * clip_factor
    left_new = STAT_DECAY * left_stats + (1.0 - STAT_DECAY) * jnp.einsum(
        "bij,bkj->bik", matrices_grad, matrices_grad, precision=HIGH
    )
    right_new = STAT_DECAY * right_stats + (1.0 - STAT_DECAY) * jnp.einsum(
        "bji,bjk->bik", matrices_grad, matrices_grad, precision=HIGH
    )
    left_part = jnp.einsum("bij,bjk->bik", left_roots, matrices_grad, precision=HIGH)
    precond = jnp.einsum("bij,bjk->bik", left_part, right_roots, precision=HIGH)
    matrices_new = matrices - SHAMPOO_RATE * (precond + DECAY_RATE * matrices)
    table_new, table_m_new, table_v_new = adamw(
        vocab_table, table_m, table_v, table_grad_own * clip_factor, TABLE_RATE, DECAY_RATE
    )
    positions_new, pos_m_new, pos_v_new = adamw(
        positions_table, pos_m, pos_v, pos_grad * clip_factor, POS_RATE, DECAY_RATE
    )
    vectors_new, vectors_m_new, vectors_v_new = adamw(
        vectors, vectors_m, vectors_v, vec_sum * clip_factor, VECTOR_RATE, 0.0
    )
    return (
        loss_value,
        grad_norm,
        matrices_new,
        left_new,
        right_new,
        matrices_grad,
        table_new,
        table_m_new,
        table_v_new,
        positions_new,
        pos_m_new,
        pos_v_new,
        vectors_new,
        vectors_m_new,
        vectors_v_new,
    )


def solution(mesh):
    in_specs = (
        P("dp", None),
        P("dp"),
        P("dp", None),
        P("dp", None),
        P(),
        P(("dp", "vocab"), None, None),
        P(("dp", "vocab"), None, None),
        P(("dp", "vocab"), None, None),
        P(("dp", "vocab"), None, None),
        P(("dp", "vocab"), None, None),
        P("vocab", "dp"),
        P("vocab", "dp"),
        P("vocab", "dp"),
        P(),
        P(),
        P(),
        P(),
        P(),
        P(),
    )
    out_specs = (
        P(),
        P(),
        P(("dp", "vocab"), None, None),
        P(("dp", "vocab"), None, None),
        P(("dp", "vocab"), None, None),
        P(("dp", "vocab"), None, None),
        P("vocab", "dp"),
        P("vocab", "dp"),
        P("vocab", "dp"),
        P(),
        P(),
        P(),
        P(),
        P(),
        P(),
    )
    return jax.shard_map(
        per_device, mesh=mesh, in_specs=in_specs, out_specs=out_specs, check_vma=False
    )
```

profile of v0, /device:TPU:1, one launch (start us, length us, event | category | flops | bytes accessed | tf_op | source)
XLA Modules:
  0.0 1266.9 jit_solution(10156596999903190726)
XLA Ops:
  10.6 47.1 %all-gather.5.cloned.1.call-done = bf16[1600,1024]{1,0:T(8,128)(2,1)} async-done(((bf16[1600,256]{1,0:T(8,128)(2,1)}), bf16[1600,1024]{1,0:T(8,128)(2,1)}) %all-gather.5.cloned.1.call-update) | async-done | bytes 3276816 | tf_op jit(solution)/shard_map/all_gather | solution.py:234
  57.7 19.3 %fusion.12 = bf16[4096,1024]{1,0:T(8,128)(2,1)} fusion(bf16[1600,1024]{1,0:T(8,128)(2,1)} %all-gather.5.cloned.1.call-done, s32[4096]{0:T(1024)S(1)} %subtract_bitcast_fusion), kind=kOutput, calls=%fused_computation.22 | convolution fusion | flops 13432520704 | bytes 11681792 | tf_op jit(solution)/shard_map/dot_general | solution.py:243
  79.4 4.4 sort.17
  88.3 104.6 %reduce-scatter.5.cloned.1.call-done = bf16[128,1024]{1,0:T(8,128)(2,1)} async-done(((bf16[4096,1024]{1,0:T(8,128)(2,1)}), bf16[128,1024]{1,0:T(8,128)(2,1)}) %reduce-scatter.5.cloned.1.call-update) | async-done | bytes 262160 | tf_op jit(solution)/shard_map/reduce_scatter | solution.py:242
  194.3 27.4 %gather_fusion = bf16[768,128,128]{2,1,0:T(8,128)(2,1)} fusion(bf16[768,128,128]{2,1,0:T(8,128)(2,1)} %all-gather.7.cloned.1.call-done, s32[1024]{0:T(1024)S(1)} %pad_clamp_fusion.2), kind=kCustom, calls=%fused_computation | custom fusion | bytes 50334720 | tf_op jit(solution)/shard_map/jit(_take)/gather | solution.py:233
  221.7 21.6 %broadcast_select_fusion.1 = bf16[768,128,128]{2,1,0:T(8,128)(2,1)} fusion(bf16[768,128,128]{2,1,0:T(8,128)(2,1)} %gather_fusion, pred[768]{0:T(1024)(128)(4,1)S(1)} %compare_and_fusion.1), kind=kLoop, calls=%fused_computation.9 | loop fusion | flops 12582912 | bytes 50332416 | tf_op jit(solution)/shard_map/jit(_take)/select_n | solution.py:233
  243.3 12.6 fusion.105
  270.3 12.5 copy.70
  282.7 23.1 %copy.71 = bf16[32,8,128,128]{3,1,2,0:T(8,128)(2,1)} copy(bf16[32,8,128,128]{3,2,1,0:T(8,128)(2,1)} %bitcast.192) | data formatting | bytes 16777216 | tf_op jit(solution)/shard_map/reshape | solution.py:56
  305.9 6.7 fusion.23
  318.1 44.0 %all-gather.9.cloned.1.call-done = bf16[512,1024]{1,0:T(8,128)(2,1)} async-done(((bf16[16,1024]{1,0:T(8,128)(2,1)}), bf16[512,1024]{1,0:T(8,128)(2,1)}) %all-gather.9.cloned.1.call-update) | async-done | bytes 1048592 | tf_op jit(solution)/shard_map/all_gather | solution.py:260
  362.1 5.8 select_reduce_fusion
  367.9 62.2 %pmax.7 = f32[512]{0:T(512)S(1)} all-reduce(f32[512]{0:T(512)S(1)} %get-tuple-element.79), channel_id=1, replica_groups=mesh['dp'=4,'vocab'=32] {'vocab'}, use_global_device_ids=true, to_apply=%region_11.12 | all-reduce | flops 512 | bytes 4096 | tf_op jit(solution)/shard_map/pmax | solution.py:269
  432.8 65.2 %psum.35 = f32[512]{0:T(512)S(1)} all-reduce(f32[512]{0:T(512)S(1)} %exponential_multiply_fusion), channel_id=1, replica_groups=mesh['dp'=4,'vocab'=32] {'vocab'}, use_global_device_ids=true, to_apply=%region_13.14 | all-reduce | flops 512 | bytes 4096 | tf_op jit(solution)/shard_map/psum | solution.py:270
  499.6 6.7 fusion.94
  506.3 73.6 %reduce-scatter.7.cloned.1.call-done = f32[16,1024]{1,0:T(8,128)} async-done(((f32[512,1024]{1,0:T(8,128)}), f32[16,1024]{1,0:T(8,128)}) %reduce-scatter.7.cloned.1.call-update) | async-done | bytes 65552 | tf_op jit(solution)/shard_map/reduce_scatter | solution.py:280
  584.0 8.7 convert_reduce_fusion
  592.8 9.1 multiply_reduce_fusion.2
  610.5 6.0 multiply_reduce_fusion.3
  618.6 7.2 fusion.92
  625.8 47.1 %all-gather.11.cloned.1.call-done = bf16[4096,1024]{1,0:T(8,128)(2,1)} async-done(((bf16[128,1024]{1,0:T(8,128)(2,1)}), bf16[4096,1024]{1,0:T(8,128)(2,1)}) %all-gather.11.cloned.1.call-update) | async-done | bytes 8388624 | tf_op jit(solution)/shard_map/all_gather | solution.py:305
  672.9 21.0 %fusion.26 = f32[1600,1024]{1,0:T(8,128)} fusion(f32[1600,1024]{1,0:T(8,128)} %fusion.92, bf16[4096,1024]{1,0:T(8,128)(2,1)} %all-gather.11.cloned.1.call-done, s32[4096]{0:T(1024)S(1)} %copy-done.66), kind=kOutput, calls=%fused_computation.34 | convolution fusion | flops 13429964800 | bytes 21512192 | tf_op jit(solution)/shard_map/dot_general | solution.py:49
  695.0 6.5 convolution_bitcast_fusion.2
  701.5 13.1 %copy.98 = f32[128,8,24,128]{3,2,1,0:T(8,128)} copy(f32[128,8,24,128]{3,1,2,0:T(8,128)} %convolution_bitcast_fusion.2) | data formatting | bytes 25165824
  714.7 11.5 copy.77
  732.9 11.8 copy.79
  752.5 6.8 copy.80
  762.0 34.8 %pad_maximum_fusion = f32[768,128,128]{2,1,0:T(8,128)} fusion(f32[256,128,128]{2,1,0:T(8,128)} %bitcast.189, f32[256,128,128]{2,1,0:T(8,128)} %bitcast.188, f32[64,128,128]{2,1,0:T(8,128)} %bitcast.194, f32[192,128,128]{2,1,0:T(8,128)} %bitcast.190), kind=kLoop, calls=%fused_computation.4 | loop fusion | flops 37748736 | bytes 100663296 | tf_op jit(solution)/shard_map/concatenate | solution.py:312
  796.8 35.4 %gather_fusion.2 = f32[768,128,128]{2,1,0:T(8,128)} fusion(f32[768,128,128]{2,1,0:T(8,128)} %pad_maximum_fusion, s32[1024]{0:T(1024)S(1)} %pad_clamp_fusion), kind=kCustom, calls=%fused_computation.2 | custom fusion | bytes 100666368 | tf_op jit(solution)/shard_map/jit(_take)/gather | solution.py:314
  832.2 34.5 %broadcast_select_fusion = f32[768,128,128]{2,1,0:T(8,128)} fusion(f32[768,128,128]{2,1,0:T(8,128)} %gather_fusion.2, pred[768]{0:T(1024)(128)(4,1)S(1)} %compare_and_fusion), kind=kLoop, calls=%fused_computation.8 | loop fusion | flops 12582912 | bytes 100664064 | tf_op jit(solution)/shard_map/jit(_take)/select_n | solution.py:314
  871.4 302.5 %reduce-scatter.9.cloned.1.call-done = f32[6,128,128]{2,1,0:T(8,128)} async-done(((f32[768,128,128]{2,1,0:T(8,128)}), f32[6,128,128]{2,1,0:T(8,128)}) %reduce-scatter.9.cloned.1.call-update) | async-done | bytes 393232 | tf_op jit(solution)/shard_map/reduce_scatter | solution.py:313
  1178.8 65.3 %all-reduce = (f32[]{:T(128)}, f32[]{:T(128)}, f32[14,1024]{1,0:T(8,128)S(1)}) all-reduce(f32[]{:T(128)S(6)} %sub.127, f32[]{:T(128)S(6)} %add.312, f32[14,1024]{1,0:T(8,128)S(1)} %concatenate.16), channel_id=1, replica_groups=mesh['dp'=4,'vocab'=32] {'dp','vocab'}, use_global_device_ids=true, to_apply=%region_17.18 | all-reduce | flops 14338 | bytes 114704 | tf_op jit(solution)/shard_map/psum | solution.py:320
  (338 shorter events, 85.8 us)
Async XLA Ops:
  8.0 1239.7 %copy-start = (f32[6,128,128]{2,1,0:T(8,128)S(1)}, f32[6,128,128]{2,1,0:T(8,128)}, u32[]{:S(2)}) copy-start(f32[6,128,128]{2,1,0:T(8,128)} %param.27) | copy-start | bytes 1179652
  8.0 49.7 %all-gather.5.cloned.1.call-start = ((), (), s32[]{:S(2)}) async-start(), calls=%async_computation.4 | async-start | bytes 4096000 | tf_op jit(solution)/shard_map/all_gather | solution.py:234
  10.6 182.4 %reduce-scatter.5.cloned.1.call-start = ((), (), s32[]{:S(2)}) async-start(), calls=%async_computation.5 | async-start | bytes 8650752 | tf_op jit(solution)/shard_map/reduce_scatter | solution.py:242
  10.6 66.4 %copy-start.65 = (s32[4096]{0:T(1024)}, s32[4096]{0:T(1024)S(1)}, u32[]{:S(2)}) copy-start(s32[4096]{0:T(1024)S(1)} %subtract_bitcast_fusion) | copy-start | bytes 49156
  77.1 115.9 %copy-start.23 = (f32[128,1024]{1,0:T(8,128)S(1)}, f32[128,1024]{1,0:T(8,128)}, u32[]{:S(2)}) copy-start(f32[128,1024]{1,0:T(8,128)} %param.32) | copy-start | bytes 1572868
  77.1 117.2 %all-gather.7.cloned.1.call-start = ((), (), s32[]{:S(2)}) async-start(), calls=%async_computation.6 | async-start | bytes 25362432 | tf_op jit(solution)/shard_map/all_gather | solution.py:231
  78.7 283.4 %all-gather.9.cloned.1.call-start = ((), (), s32[]{:S(2)}) async-start(), calls=%async_computation.7 | async-start | bytes 1081344 | tf_op jit(solution)/shard_map/all_gather | solution.py:260
  87.1 172.9 %copy-start.46 = (f32[1,1024]{1,0:T(1,128)}, f32[1,1024]{1,0:T(1,128)S(1)}, u32[]{:S(2)}) copy-start(f32[1,1024]{1,0:T(1,128)S(1)} %get-tuple-element.69) | copy-start | bytes 12292
  87.1 218.8 %copy-start.44 = (f32[1,1024]{1,0:T(1,128)}, f32[1,1024]{1,0:T(1,128)S(1)}, u32[]{:S(2)}) copy-start(f32[1,1024]{1,0:T(1,128)S(1)} %get-tuple-element.64) | copy-start | bytes 12292
  87.1 229.9 %copy-start.51 = (f32[1,1024]{1,0:T(1,128)}, f32[1,1024]{1,0:T(1,128)S(1)}, u32[]{:S(2)}) copy-start(f32[1,1024]{1,0:T(1,128)S(1)} %get-tuple-element.62) | copy-start | bytes 12292
  194.0 65.9 %copy-start.72 = (f32[128]{0:T(128)}, f32[128]{0:T(128)S(1)}, u32[]{:S(2)}) copy-start(f32[128]{0:T(128)S(1)} %broadcast_multiply_fusion.3) | copy-start | bytes 1540
  194.3 65.7 %copy-start.82 = (f32[128]{0:T(128)}, f32[128]{0:T(128)S(1)}, u32[]{:S(2)}) copy-start(f32[128]{0:T(128)S(1)} %fusion.87) | copy-start | bytes 1540
  270.0 35.9 %copy-start.75 = (f32[128]{0:T(128)}, f32[128]{0:T(128)S(1)}, u32[]{:S(2)}) copy-start(f32[128]{0:T(128)S(1)} %broadcast_multiply_fusion.2) | copy-start | bytes 1540
  270.3 35.6 %copy-start.85 = (f32[128]{0:T(128)}, f32[128]{0:T(128)S(1)}, u32[]{:S(2)}) copy-start(f32[128]{0:T(128)S(1)} %fusion.88) | copy-start | bytes 1540
  317.7 262.3 %reduce-scatter.7.cloned.1.call-start = ((), (), s32[]{:S(2)}) async-start(), calls=%async_computation.8 | async-start | bytes 2162688 | tf_op jit(solution)/shard_map/reduce_scatter | solution.py:280
  318.0 181.5 %copy-start.78 = (s32[512]{0:T(512)}, s32[512]{0:T(512)S(1)}, u32[]{:S(2)}) copy-start(s32[512]{0:T(512)S(1)} %eq.21) | copy-start | bytes 6148
  318.0 181.5 %copy-start.80 = (pred[1600]{0:T(1024)(128)(4,1)}, pred[1600]{0:T(1024)(128)(4,1)S(1)}, u32[]{:S(2)}) copy-start(pred[1600]{0:T(1024)(128)(4,1)S(1)} %broadcast_compare_fusion.1) | copy-start | bytes 4804
  318.0 181.5 %copy-start.55 = (s32[1600]{0:T(1024)}, s32[1600]{0:T(1024)S(1)}, u32[]{:S(2)}) copy-start(s32[1600]{0:T(1024)S(1)} %iota_add_fusion) | copy-start | bytes 19204
  367.9 130.2 %copy-start.100 = (s32[32]{0:T(128)S(1)}, s32[32]{0:T(128)}, u32[]{:S(2)}) copy-start(s32[32]{0:T(128)} %param.20) | copy-start | bytes 388
  499.5 80.4 %copy-start.52 = (f32[1,1024]{1,0:T(1,128)S(1)}, f32[1,1024]{1,0:T(1,128)}, u32[]{:S(2)}) copy-start(f32[1,1024]{1,0:T(1,128)} %copy-done.51) | copy-start | bytes 12292
  506.3 166.7 %all-gather.11.cloned.1.call-start = ((), (), s32[]{:S(2)}) async-start(), calls=%async_computation.10 | async-start | bytes 8650752 | tf_op jit(solution)/shard_map/all_gather | solution.py:305
  618.5 54.4 %copy-start.66 = (s32[4096]{0:T(1024)S(1)}, s32[4096]{0:T(1024)}, u32[]{:S(2)}) copy-start(s32[4096]{0:T(1024)} %copy-done.65) | copy-start | bytes 49156
  618.5 250.4 %reduce-scatter.11.cloned.1.call-start = ((), (), s32[]{:S(2)}) async-start(), calls=%async_computation.11 | async-start | bytes 8192000 | tf_op jit(solution)/shard_map/reduce_scatter | solution.py:307
  694.0 479.9 %reduce-scatter.9.cloned.1.call-start = ((), (), s32[]{:S(2)}) async-start(), calls=%async_computation.9 | async-start | bytes 50724864 | tf_op jit(solution)/shard_map/reduce_scatter | solution.py:313
  866.8 381.5 %copy-start.39 = (f32[6,128,128]{2,1,0:T(8,128)S(1)}, f32[6,128,128]{2,1,0:T(8,128)}, u32[]{:S(2)}) copy-start(f32[6,128,128]{2,1,0:T(8,128)} %param.26) | copy-start | bytes 1179652
  866.8 310.2 %all-reduce.3.cloned.1.call-start = ((), (), s32[]{:S(2)}) async-start(), calls=%async_computation.12 | async-start | bytes 1048576 | tf_op jit(solution)/shard_map/psum | solution.py:320
  868.6 381.2 %copy-start.40 = (f32[6,128,128]{2,1,0:T(8,128)S(1)}, f32[6,128,128]{2,1,0:T(8,128)}, u32[]{:S(2)}) copy-start(f32[6,128,128]{2,1,0:T(8,128)} %param.25) | copy-start | bytes 1179652
  871.4 380.2 %copy-start.43 = (f32[14,1024]{1,0:T(8,128)S(1)}, f32[14,1024]{1,0:T(8,128)}, u32[]{:S(2)}) copy-start(f32[14,1024]{1,0:T(8,128)} %param.35) | copy-start | bytes 172036
  871.4 380.2 %copy-start.49 = (f32[14,1024]{1,0:T(8,128)S(1)}, f32[14,1024]{1,0:T(8,128)}, u32[]{:S(2)}) copy-start(f32[14,1024]{1,0:T(8,128)} %param.36) | copy-start | bytes 172036
  871.4 380.2 %copy-start.50 = (f32[14,1024]{1,0:T(8,128)S(1)}, f32[14,1024]{1,0:T(8,128)}, u32[]{:S(2)}) copy-start(f32[14,1024]{1,0:T(8,128)} %param.37) | copy-start | bytes 172036
  871.4 380.9 %copy-start.29 = (f32[6,128,128]{2,1,0:T(8,128)S(1)}, f32[6,128,128]{2,1,0:T(8,128)}, u32[]{:S(2)}) copy-start(f32[6,128,128]{2,1,0:T(8,128)} %param.24) | copy-start | bytes 1179652
  871.4 380.9 %copy-start.41 = (f32[6,128,128]{2,1,0:T(8,128)S(1)}, f32[6,128,128]{2,1,0:T(8,128)}, u32[]{:S(2)}) copy-start(f32[6,128,128]{2,1,0:T(8,128)} %param.28) | copy-start | bytes 1179652
  (85 other events, 423.8 us)
Sparse Core Ops, SparseCore 0:
  11.1 46.5 all-gather.4
  77.2 115.6 reduce-scatter.4
  317.8 44.2 all-gather.8
  506.4 73.5 reduce-scatter.6
  618.6 54.2 all-gather.10
  694.1 65.1 reduce-scatter.10
  866.9 307.0 reduce-scatter.8
Sparse Core Ops, SparseCore 1:
  81.7 104.4 all-gather.6
  873.3 144.2 all-reduce.2
where the time goes:
time: 1270 us
  waiting for transfers between devices  619 us (49%)
  blocking collectives  193 us (15%)
  local copies, waits for them, and re-layouts  184 us (14%)
  other arithmetic  128 us (10%)
  matrix products  119 us (9%)
  between operations  23 us (2%)
    reduce_scatter x1, waiting for transfers between devices, per_device(): lax.psum_scatter(jnp.take(grad_blocks, block_of_slot, axis=0), ('dp', 'vo...  303 us
    reduce_scatter x1, waiting for transfers between devices, per_device(): lax.psum_scatter(jnp.dot(one_hot(), table_rows, preferred_element_type=jn...  105 us
    reduce_scatter x1, waiting for transfers between devices, per_device(): lax.psum_scatter(jnp.dot(d_logits, table_rows, preferred_element_type=jnp...  73.6 us
    psum x1, blocking collectives, per_device(): lax.psum((d_hidden, vec_grads, squares, loss_share), ('dp', 'vocab'))  65.3 us
    psum x1, blocking collectives, per_device(): total_all = lax.psum(local_total * jnp.exp(local_top - top_all), 'vocab')  65.2 us
    pmax x1, blocking collectives, per_device(): top_all = lax.pmax(local_top, 'vocab')  62.2 us
    all_gather x1, waiting for transfers between devices, per_device(): lax.all_gather(d_embed, 'vocab', axis=0, tiled=True)  47.1 us
    all_gather x1, waiting for transfers between devices, per_device(): lax.all_gather(vocab_table.astype(jnp.bfloat16), 'dp', axis=1, tiled=True)  47.1 us
  transfers between devices with their start and end apart: 9, of which 6 were waited for; matrix products, arithmetic and copies ran while one was open for 15% of the time, Pallas kernels for 0%

commit v1 on v0

v1 whole, which is shorter than its diff:
```python
import jax
import jax.numpy as jnp
import numpy as np
from jax import lax
from jax.experimental import pallas as pl
from jax.experimental.pallas import tpu as pltpu
from jax.sharding import PartitionSpec as P

D = 1024
HEADS = 16
HEAD_DIM = 64
FF = 4096
VOCAB_REAL = 50257
LAYERS = 1
BLOCK = 128
STEP = 10


LN_EPS = 1e-05
CLIP_LEVEL = 0.05
BETA_ONE = 0.9
BETA_TWO = 0.999
ADAM_EPS = 1e-08
STAT_DECAY = 0.95
SHAMPOO_RATE = 0.03
TABLE_RATE = 0.15
POS_RATE = 0.05
VECTOR_RATE = 0.25
DECAY_RATE = 0.1
NEG_FILL = -1e30
GELU_C = 0.7978845608028654
HIGH = lax.Precision.HIGHEST


def gelu(values):
    return 0.5 * values * (1.0 + jnp.tanh(GELU_C * (values + 0.044715 * values * values * values)))


def dot_nt(left, right):
    return lax.dot_general(
        left, right, (((1,), (1,)), ((), ())), preferred_element_type=jnp.float32
    )


def dot_tn(left, right):
    return lax.dot_general(
        left, right, (((0,), (0,)), ((), ())), preferred_element_type=jnp.float32
    )


def adamw(weight, moment_one, moment_two, grad_in, rate, decay):
    new_one = BETA_ONE * moment_one + (1.0 - BETA_ONE) * grad_in
    new_two = BETA_TWO * moment_two + (1.0 - BETA_TWO) * grad_in * grad_in
    hat_one = new_one / (1.0 - BETA_ONE**STEP)
    hat_two = new_two / (1.0 - BETA_TWO**STEP)
    new_weight = weight - rate * (hat_one / (jnp.sqrt(hat_two) + ADAM_EPS) + decay * weight)
    return (new_weight, new_one, new_two)


TABLE_CHUNKS = 20
MESH_IDS = pl.DeviceIdType.MESH
ANY = pl.BlockSpec(memory_space=pl.ANY)
VMEM = pl.BlockSpec(memory_space=pltpu.VMEM)
N_DP = 4
N_VOCAB = 32
SIDE = 4
X, Y, Z, CORE = range(4)
ORDERS = ((X, Y, Z), (Y, Z, X), (Z, X, Y))
SLOTS = 6


def coordinates():
    across = lax.axis_index("dp")
    inner = lax.axis_index("vocab")
    return (across, (inner // 2) % SIDE, inner // (2 * SIDE), inner % 2)


def moved(place, axis, step):
    shifted = list(place)
    shifted[axis] = (place[axis] + step) % (2 if axis == CORE else SIDE)
    return tuple(shifted)


def device_of(place):
    return (place[X], (place[Z] * SIDE + place[Y]) * 2 + place[CORE])


def greet(place, axes, far_axes):
    barrier = pltpu.get_barrier_semaphore()
    others = [moved(place, CORE, 1)]
    for axis in axes:
        others += [moved(place, axis, 1), moved(place, axis, -1)]
    for axis in far_axes:
        others.append(moved(place, axis, 2))
    for other in others:
        pl.semaphore_signal(
            barrier, inc=1, device_id=device_of(other), device_id_type=MESH_IDS
        )
    pl.semaphore_wait(barrier, len(others))


class Wires:
    def __init__(self, send_sems, recv_sems):
        self.send_sems, self.recv_sems, self.used = send_sems, recv_sems, 0
        self.sent = []

    def send(self, source, target, place):
        copy = pltpu.make_async_remote_copy(
            src_ref=source,
            dst_ref=target,
            send_sem=self.send_sems.at[self.used],
            recv_sem=self.recv_sems.at[self.used],
            device_id=device_of(place),
            device_id_type=MESH_IDS,
        )
        self.used += 1
        copy.start()
        self.sent.append(copy)
        return copy

    def drain(self):
        for copy in self.sent:
            copy.wait_send()


def add_blocks(target, sources, count):
    @pl.loop(0, count)
    def _(i):
        total = target[i].astype(jnp.float32)
        for source in sources:
            total += source[i].astype(jnp.float32)
        target[i] = total.astype(target.dtype)


class RingGather:
    def __init__(self, wires, place, axis, piece, half):
        self.wires, self.place, self.axis = wires, place, axis
        self.piece, self.half = piece, half
        self.mine = place[axis]

    def start(self):
        mine = self.piece(self.mine)
        self.up = self.wires.send(mine, mine, moved(self.place, self.axis, 1))
        self.down = self.wires.send(mine, mine, moved(self.place, self.axis, -1))

    def forward(self):
        self.up.wait_recv()
        lower = self.half((self.mine + 3) % SIDE, 0)
        self.far_up = self.wires.send(lower, lower, moved(self.place, self.axis, 1))
        self.down.wait_recv()
        upper = self.half((self.mine + 1) % SIDE, 1)
        self.far_down = self.wires.send(upper, upper, moved(self.place, self.axis, -1))

    def finish(self):
        self.far_up.wait_recv()
        self.far_down.wait_recv()


class DirectGather:
    def __init__(self, wires, place, axis, piece):
        self.wires, self.place, self.axis, self.piece = wires, place, axis, piece

    def start(self):
        mine = self.piece(self.place[self.axis])
        self.copies = [
            self.wires.send(mine, mine, moved(self.place, self.axis, step)) for step in (1, 2, 3)
        ]

    def finish(self):
        for copy in self.copies:
            copy.wait_recv()


class RingReduce:
    def __init__(self, wires, place, axis, piece, half, count, half_in, whole_in):
        self.wires, self.place, self.axis = wires, place, axis
        self.piece, self.half, self.count = piece, half, count
        self.half_in, self.whole_in = half_in, whole_in
        self.mine = place[axis]

    def start(self):
        far = (self.mine + 2) % SIDE
        up, down = moved(self.place, self.axis, 1), moved(self.place, self.axis, -1)
        self.far_up = self.wires.send(self.half(far, 0), self.half_in.at[0], up)
        self.far_down = self.wires.send(self.half(far, 1), self.half_in.at[1], down)

    def forward(self):
        after, before = (self.mine + 1) % SIDE, (self.mine + 3) % SIDE
        up, down = moved(self.place, self.axis, 1), moved(self.place, self.axis, -1)
        self.far_up.wait_recv()
        add_blocks(self.half(after, 0), [self.half_in.at[0]], self.count // 2)
        self.up = self.wires.send(self.piece(after), self.whole_in.at[0], up)
        self.far_down.wait_recv()
        add_blocks(self.half(before, 1), [self.half_in.at[1]], self.count // 2)
        self.down = self.wires.send(self.piece(before), self.whole_in.at[1], down)

    def arrive(self):
        self.up.wait_recv()
        self.down.wait_recv()

    def finish(self):
        self.arrive()
        add_blocks(
            self.piece(self.mine), [self.whole_in.at[0], self.whole_in.at[1]], self.count
        )


class DirectReduce:
    def __init__(self, wires, place, axis, piece, count, landing):
        self.wires, self.place, self.axis = wires, place, axis
        self.piece, self.count, self.landing = piece, count, landing

    def start(self):
        mine = self.place[self.axis]
        self.copies = [
            self.wires.send(
                self.piece((mine + step) % SIDE),
                self.landing.at[step - 1],
                moved(self.place, self.axis, step),
            )
            for step in (1, 2, 3)
        ]

    def arrive(self):
        for copy in self.copies:
            copy.wait_recv()

    def finish(self):
        self.arrive()
        add_blocks(
            self.piece(self.place[self.axis]),
            [self.landing.at[step] for step in range(3)],
            self.count,
        )


def block_ring(place, part, phase, at):
    first_axis, second_axis, third_axis = ORDERS[part]
    k1, k2, k3 = place[first_axis], place[second_axis], place[third_axis]
    if phase == 0:
        return (
            lambda j: at(k3, 8 * k2 + 2 * j, 2),
            lambda j, h: at(k3, 8 * k2 + 2 * j + h, 1),
        )
    if phase == 1:
        return (lambda j: at(k3, 8 * j, 8), lambda j, h: at(k3, 8 * j + 4 * h, 4))
    return (lambda j: at(j, 0, 32), lambda j, h: at(j, 16 * h, 16))


def start_kernel(
    ids_ref,
    own_ref,
    table_ref,
    positions_ref,
    full_ref,
    table_full_ref,
    hidden_ref,
    table_pad,
    ids_all,
    parts,
    sibling_in,
    half_in,
    whole_in,
    landing,
    ready,
    arrived,
    send_sems,
    recv_sems,
    local_sems,
):
    place = coordinates()
    core = place[CORE]
    across = place[X]
    sibling = moved(place, CORE, 1)
    wires = Wires(send_sems, recv_sems)
    own_copies = []
    for part in range(3):
        k1, k2, k3 = (place[axis] for axis in ORDERS[part])
        own_copies.append(
            pltpu.make_async_copy(
                own_ref.at[part],
                full_ref.at[part, core, k3, pl.ds(8 * k2 + 2 * k1, 2)],
                local_sems.at[part],
            )
        )
    own_copies.append(
        pltpu.make_async_copy(table_ref, table_full_ref.at[across], local_sems.at[3])
    )
    for copy in own_copies:
        copy.start()
    ids_all[across] = ids_ref[...]
    greet(place, (X, Y, Z), (X, Y, Z))
    ids_ring = DirectGather(wires, place, X, lambda j: ids_all.at[j])
    ids_ring.start()
    rings = []
    for phase in range(3):
        row = []
        for part in range(3):
            piece, half = block_ring(
                place,
                part,
                phase,
                lambda k3, first, count, part=part: full_ref.at[
                    part, core, k3, pl.ds(first, count)
                ],
            )
            row.append(RingGather(wires, place, ORDERS[part][phase], piece, half))
        rings.append(row)
    for copy, ring in zip(own_copies, rings[0]):
        copy.wait()
        ring.start()
    own_copies[3].wait()
    table_ring = RingGather(
        wires,
        place,
        X,
        lambda j: table_full_ref.at[j],
        lambda j, h: table_full_ref.at[j, pl.ds(800 * h, 800)],
    )
    rows = table_ref.shape[0]
    table_pad[pl.ds(0, rows)] = table_ref[...]
    padding = table_pad.shape[0] - rows
    table_pad[pl.ds(rows, padding)] = jnp.zeros((padding, table_pad.shape[1]), jnp.bfloat16)
    base = (lax.axis_index("vocab") * rows).astype(jnp.float32)
    tiles = table_pad.shape[0] // 128
    lane = lax.broadcasted_iota(jnp.int32, (128, 128), 1).astype(jnp.float32)

    def look_up(group):
        part = group // 2

        @pl.loop(0, 8)
        def _(quad):
            hot_rows = []
            for which in range(4):
                ids = ids_all[group, pl.ds(4 * quad + which, 1), :].astype(jnp.float32) - base
                column = jnp.transpose(jnp.broadcast_to(ids, (128, 128)))
                hot_rows.append(
                    jnp.concatenate(
                        [
                            jnp.where(column == lane + 128.0 * tile, 1.0, 0.0).astype(jnp.bfloat16)
                            for tile in range(tiles)
                        ],
                        1,
                    )
                )
            found = jnp.dot(
                jnp.concatenate(hot_rows, 0), table_pad[...], preferred_element_type=jnp.float32
            ).astype(jnp.bfloat16)
            at_z = quad // 2
            for which in range(4):
                at_y = 2 * (quad % 2) + which // 2
                first, second = (at_z, at_y) if part == 0 else (at_y, at_z)
                parts[part, which % 2, first, 2 * second + group % 2] = found[
                    128 * which : 128 * which + 128
                ]

    def to_sibling(part):
        return wires.send(parts.at[part, 1 - core], sibling_in.at[part], sibling)

    lookup_axes = ((Z, Y), (Y, Z))
    lookup_rings, lookup_ends = [], []
    for part in range(2):
        first_axis, second_axis = lookup_axes[part]
        lookup_rings.append(
            RingReduce(
                wires,
                place,
                first_axis,
                lambda j, part=part: parts.at[part, core, j],
                lambda j, h, part=part: parts.at[part, core, j, pl.ds(4 * h, 4)],
                8,
                half_in.at[part],
                whole_in.at[part],
            )
        )
        lookup_ends.append(
            DirectReduce(
                wires,
                place,
                second_axis,
                lambda j, part=part, k=place[first_axis]: parts.at[part, core, k, pl.ds(2 * j, 2)],
                2,
                landing.at[part],
            )
        )
    ids_ring.finish()
    for ring in rings[0]:
        ring.forward()
    for ring, later in zip(rings[0], rings[1]):
        ring.finish()
        later.start()
    look_up(0)
    for ring in rings[1]:
        ring.forward()
    look_up(1)
    siblings = [to_sibling(0)]
    for ring, later in zip(rings[1], rings[2]):
        ring.finish()
        later.start()
    table_ring.start()
    block_siblings = []
    for part in range(3):
        own = full_ref.at[part, core, place[ORDERS[part][2]]]
        block_siblings.append(wires.send(own, own, sibling))
    look_up(2)
    look_up(3)
    siblings.append(to_sibling(1))

    def add_sibling(part):
        siblings[part].wait_recv()
        for j in range(4):
            add_blocks(parts.at[part, core, j], [sibling_in.at[part, j]], 8)
        lookup_rings[part].start()

    add_sibling(0)
    add_sibling(1)
    table_ring.forward()
    for ring in lookup_rings:
        ring.forward()
    for ring in rings[2]:
        ring.forward()
    for part in range(3):
        k3 = place[ORDERS[part][2]]
        for step in (1, 3):
            piece = full_ref.at[part, core, (k3 + step) % SIDE]
            block_siblings.append(wires.send(piece, piece, sibling))
    for ring, end in zip(lookup_rings, lookup_ends):
        ring.finish()
        end.start()
    for part in range(2):
        end = lookup_ends[part]
        end.arrive()
        first_axis, second_axis = lookup_axes[part]
        for which in range(2):
            total = parts[part, core, place[first_axis], 2 * place[second_axis] + which].astype(
                jnp.float32
            )
            for step in range(3):
                total += landing[part, step, which].astype(jnp.float32)
            ready[2 * part + which] = total.astype(jnp.bfloat16)
    swaps = []
    for step in (1, 2, 3):
        there = moved(place, X, step)
        swaps.append(wires.send(ready.at[there[X]], arrived.at[across], there))
    arrived[across] = ready[across]
    for copy in swaps:
        copy.wait_recv()
    for source in range(4):
        columns = pl.ds(256 * source, 256)
        hidden_ref[:, columns] = (
            arrived[source].astype(jnp.float32) + positions_ref[:, columns]
        )
    table_ring.finish()
    for part in range(3):
        rings[2][part].finish()
        far = full_ref.at[part, core, (place[ORDERS[part][2]] + 2) % SIDE]
        block_siblings.append(wires.send(far, far, sibling))
    for copy in block_siblings:
        copy.wait_recv()
    wires.drain()


def start_call(token_ids, own_blocks, table_low, positions_table):
    rows, width = table_low.shape
    padded = -(-rows // 128) * 128
    bf16 = jnp.bfloat16
    return pl.pallas_call(
        start_kernel,
        name="gather_and_look_up",
        out_shape=(
            jax.ShapeDtypeStruct((3, 2, SIDE, 32, BLOCK, BLOCK), bf16),
            jax.ShapeDtypeStruct((N_DP, rows, width), bf16),
            jax.ShapeDtypeStruct(positions_table.shape, jnp.float32),
        ),
        in_specs=[VMEM, ANY, VMEM, VMEM],
        out_specs=(ANY, ANY, VMEM),
        scratch_shapes=[
            pltpu.VMEM((padded, width), bf16),
            pltpu.VMEM((N_DP,) + token_ids.shape, jnp.int32),
            pltpu.VMEM((2, 2, SIDE, 8, 128, width), bf16),
            pltpu.VMEM((2, SIDE, 8, 128, width), bf16),
            pltpu.VMEM((2, 2, 4, 128, width), bf16),
            pltpu.VMEM((2, 2, 8, 128, width), bf16),
            pltpu.VMEM((2, 3, 2, 128, width), bf16),
            pltpu.VMEM((N_DP, 128, width), bf16),
            pltpu.VMEM((N_DP, 128, width), bf16),
            pltpu.SemaphoreType.DMA((80,)),
            pltpu.SemaphoreType.DMA((80,)),
            pltpu.SemaphoreType.DMA((4,)),
        ],
        compiler_params=pltpu.CompilerParams(
            collective_id=1, has_side_effects=True, vmem_limit_bytes=60 << 20
        ),
    )(token_ids, own_blocks, table_low, positions_table)


def head_kernel(
    head_in_ref,
    table_ref,
    target_ref,
    counted_ref,
    d_head_ref,
    table_grad_ref,
    loss_ref,
    pieces,
    rows_in,
    logits,
    d_logits,
    stats,
    stats_in,
    d_rows,
    d_sibling,
    d_first,
    d_second,
    send_sems,
    recv_sems,
):
    place = coordinates()
    core = place[CORE]
    sibling = moved(place, CORE, 1)
    wires = Wires(send_sems, recv_sems)
    own, width = head_in_ref.shape
    half_width = width // 2
    feature_axes = ((Y, Z), (Z, Y))
    for part in range(2):
        near, far = (place[axis] for axis in feature_axes[part])
        pieces[part, core, far, near] = head_in_ref[
            :, part * half_width : (part + 1) * half_width
        ]
    greet(place, (Y, Z), (Y, Z))
    first_rings, second_rings = [], []
    for part in range(2):
        near_axis, far_axis = feature_axes[part]
        first_rings.append(
            DirectGather(
                wires,
                place,
                near_axis,
                lambda j, part=part, k=place[far_axis]: pieces.at[part, core, k, j],
            )
        )
        second_rings.append(
            DirectGather(wires, place, far_axis, lambda j, part=part: pieces.at[part, core, j])
        )
    for ring in first_rings:
        ring.start()
    for ring, later in zip(first_rings, second_rings):
        ring.finish()
        later.start()
    crossing = []
    for part in range(2):
        second_rings[part].finish()
        mine = pieces.at[part, core]
        crossing.append(wires.send(mine, mine, sibling))
    for copy in crossing:
        copy.wait_recv()
    for index in range(32):
        at_z, at_y, at_core = index // 8, index // 2 % SIDE, index % 2
        rows_in[own * index : own * (index + 1), :half_width] = pieces[0, at_core, at_z, at_y]
        rows_in[own * index : own * (index + 1), half_width:] = pieces[1, at_core, at_y, at_z]

    groups, rows, group_width = table_ref.shape
    count = rows_in.shape[0]
    chunk = rows // 4
    base = lax.axis_index("vocab") * rows
    row_iota = lax.broadcasted_iota(jnp.int32, (chunk, count), 0)
    target = target_ref[...]
    counted = counted_ref[...]

    def logit_chunk(index, top):
        at = pl.ds(pl.multiple_of(index * chunk, chunk), chunk)
        total = jnp.zeros((chunk, count), jnp.float32)
        for group in range(groups):
            total += lax.dot_general(
                table_ref[group, at],
                rows_in[:, group * group_width : (group + 1) * group_width],
                (((1,), (1,)), ((), ())),
                preferred_element_type=jnp.float32,
            )
        total = jnp.where(row_iota + (base + index * chunk) < VOCAB_REAL, total, NEG_FILL)
        logits[at] = total
        return jnp.maximum(top, jnp.max(total, 0, keepdims=True))

    local_top = lax.fori_loop(
        0, 4, logit_chunk, jnp.full((1, count), NEG_FILL, jnp.float32)
    )

    def exp_chunk(index, carry):
        total, pick = carry
        at = pl.ds(pl.multiple_of(index * chunk, chunk), chunk)
        values = logits[at]
        hits = row_iota + (base + index * chunk) == target
        pick += jnp.sum(jnp.where(hits, values, 0.0), 0, keepdims=True)
        values = jnp.exp(values - local_top)
        logits[at] = values
        return total + jnp.sum(values, 0, keepdims=True), pick

    zero_row = jnp.zeros((1, count), jnp.float32)
    local_total, pick = lax.fori_loop(0, 4, exp_chunk, (zero_row, zero_row))
    lanes = count // 4
    top = jnp.concatenate([local_top[:, lanes * i : lanes * (i + 1)] for i in range(4)], 0)
    total = jnp.concatenate([local_total[:, lanes * i : lanes * (i + 1)] for i in range(4)], 0)
    for phase, (axis, steps) in enumerate(((CORE, (1,)), (Y, (1, 2, 3)), (Z, (1, 2, 3)))):
        stats[phase] = jnp.concatenate([top, total], 0)
        copies = [
            wires.send(stats.at[phase], stats_in.at[phase, step - 1], moved(place, axis, step))
            for step in steps
        ]
        for copy in copies:
            copy.wait_recv()
        tops, totals = [top], [total]
        for step in steps:
            received = stats_in[phase, step - 1]
            tops.append(received[:4])
            totals.append(received[4:])
        top = tops[0]
        for other in tops[1:]:
            top = jnp.maximum(top, other)
        total = sum(part * jnp.exp(part_top - top) for part, part_top in zip(totals, tops))
    log_total = top + jnp.log(total)
    log_total = jnp.concatenate([log_total[i : i + 1] for i in range(4)], 1)
    first_device = (lax.axis_index("vocab") == 0).astype(jnp.float32)
    loss_ref[...] = (first_device * log_total - pick) * counted
    weight = counted / (N_DP * N_VOCAB * own)
    scale = jnp.exp(local_top - log_total) * weight

    @pl.loop(0, 4)
    def _(index):
        at = pl.ds(pl.multiple_of(index * chunk, chunk), chunk)
        hits = row_iota + (base + index * chunk) == target
        d_logits[at] = (logits[at] * scale - jnp.where(hits, weight, 0.0)).astype(jnp.bfloat16)

    for side in range(2):
        lowered = d_logits[:, 256 * side : 256 * (side + 1)]
        for group in range(groups):
            rows_grad = lax.dot_general(
                lowered,
                table_ref[group],
                (((0,), (0,)), ((), ())),
                preferred_element_type=jnp.float32,
            ).astype(jnp.bfloat16)
            part, column = group // 2, group % 2 * group_width
            for index in range(16):
                inner = 16 * side + index
                at_z, at_y, at_core = inner // 8, inner // 2 % SIDE, inner % 2
                first, second = (at_z, at_y) if part == 0 else (at_y, at_z)
                d_rows[part, at_core, first, second, :, column : column + group_width] = (
                    rows_grad[own * index : own * (index + 1)]
                )
    crossing = [
        wires.send(d_rows.at[part, 1 - core], d_sibling.at[part], sibling) for part in range(2)
    ]
    reduce_axes = ((Z, Y), (Y, Z))
    first_rings, second_rings = [], []
    for part in range(2):
        first_axis, second_axis = reduce_axes[part]
        crossing[part].wait_recv()
        for j in range(4):
            add_blocks(d_rows.at[part, core, j], [d_sibling.at[part, j]], 4)
        first_rings.append(
            DirectReduce(
                wires,
                place,
                first_axis,
                lambda j, part=part: d_rows.at[part, core, j],
                4,
                d_first.at[part],
            )
        )
        second_rings.append(
            DirectReduce(
                wires,
                place,
                second_axis,
                lambda j, part=part, k=place[first_axis]: d_rows.at[part, core, k, j],
                1,
                d_second.at[part],
            )
        )
        first_rings[part].start()

    def table_grad_chunk(index):
        at = pl.ds(pl.multiple_of(index * chunk, chunk), chunk)
        blocks_in_chunk = chunk // table_grad_ref.shape[2]
        for group in range(groups):
            product = jnp.dot(
                d_logits[at],
                rows_in[:, group * group_width : (group + 1) * group_width],
                preferred_element_type=jnp.float32,
            ).astype(jnp.bfloat16)
            table_grad_ref[group, pl.ds(index * blocks_in_chunk, blocks_in_chunk)] = (
                product.reshape((blocks_in_chunk,) + table_grad_ref.shape[2:])
            )

    @pl.loop(0, 2)
    def _(index):
        table_grad_chunk(index)

    for ring, later in zip(first_rings, second_rings):
        ring.finish()
        later.start()

    @pl.loop(2, 4)
    def _(index):
        table_grad_chunk(index)

    for part in range(2):
        second_rings[part].arrive()
        first_axis, second_axis = reduce_axes[part]
        total = d_rows[part, core, place[first_axis], place[second_axis]].astype(jnp.float32)
        for step in range(3):
            total += d_second[part, step].astype(jnp.float32)
        d_head_ref[:, part * half_width : (part + 1) * half_width] = total
    wires.drain()


def head_call(head_in, table_full, target_row, counted_row):
    groups, rows, group_width = table_full.shape
    own, width = head_in.shape
    count = target_row.shape[1]
    half = width // 2
    bf16 = jnp.bfloat16
    return pl.pallas_call(
        head_kernel,
        name="head",
        out_shape=(
            jax.ShapeDtypeStruct((own, width), jnp.float32),
            jax.ShapeDtypeStruct((groups, TABLE_CHUNKS, rows // TABLE_CHUNKS, group_width), bf16),
            jax.ShapeDtypeStruct((1, count), jnp.float32),
        ),
        in_specs=[VMEM] * 4,
        out_specs=(VMEM,) * 3,
        scratch_shapes=[
            pltpu.VMEM((2, 2, SIDE, SIDE, own, half), bf16),
            pltpu.VMEM((count, width), bf16),
            pltpu.VMEM((rows, count), jnp.float32),
            pltpu.VMEM((rows, count), bf16),
            pltpu.VMEM((3, 8, count // 4), jnp.float32),
            pltpu.VMEM((3, 3, 8, count // 4), jnp.float32),
            pltpu.VMEM((2, 2, SIDE, SIDE, own, half), bf16),
            pltpu.VMEM((2, SIDE, SIDE, own, half), bf16),
            pltpu.VMEM((2, 3, SIDE, own, half), bf16),
            pltpu.VMEM((2, 3, own, half), bf16),
            pltpu.SemaphoreType.DMA((40,)),
            pltpu.SemaphoreType.DMA((40,)),
        ],
        compiler_params=pltpu.CompilerParams(
            collective_id=2, has_side_effects=True, vmem_limit_bytes=60 << 20
        ),
    )(head_in, table_full, target_row, counted_row)


def finish_kernel(
    grads_ref,
    small_ref,
    head_grad_ref,
    d_embed_ref,
    ids_ref,
    loss_ref,
    grads_out_ref,
    table_grad_ref,
    final_ref,
    sums,
    sibling_in,
    half_a,
    whole_a,
    half_b,
    whole_b,
    half_c,
    whole_c,
    small_sums,
    small_sibling,
    small_a,
    small_b,
    small_c,
    table_sums,
    table_half,
    table_whole,
    embeds,
    ids_all,
    send_sems,
    recv_sems,
    local_sems,
):
    place = coordinates()
    core = place[CORE]
    across = place[X]
    sibling = moved(place, CORE, 1)
    wires = Wires(send_sems, recv_sems)
    loads = []

    def load(source, target):
        copy = pltpu.make_async_copy(source, target, local_sems.at[len(loads)])
        copy.start()
        loads.append(copy)
        return copy

    third = [place[ORDERS[part][2]] for part in range(3)]
    table_load = load(head_grad_ref, table_sums)
    block_loads = {}
    for step in (2, 1, 3, 0):
        for part in range(3):
            j = (third[part] + step) % SIDE
            block_loads[part, step] = load(grads_ref.at[part, core, j], sums.at[part, j])
    small_load = load(small_ref.at[core], small_sums)

    width = table_grad_ref.shape[1]
    embed_axes = ((Y, Z), (Z, Y))
    source_part = across // 2
    near = place[Y] * (1 - source_part) + place[Z] * source_part
    far = place[Z] * (1 - source_part) + place[Y] * source_part
    landing = embeds.at[source_part, core, far, 2 * near + across % 2]
    own_columns = pl.ds(pl.multiple_of(across * width, width), width)
    landing[...] = d_embed_ref[:, own_columns]
    ids_all[across] = ids_ref[...]
    greet(place, (X, Y, Z), (X, Y, Z))
    swaps = []
    for step in (1, 2, 3):
        there = moved(place, X, step)
        columns = pl.ds(pl.multiple_of(there[X] * width, width), width)
        swaps.append(wires.send(d_embed_ref.at[:, columns], landing, there))
    ids_ring = DirectGather(wires, place, X, lambda j: ids_all.at[j])
    ids_ring.start()
    small_crossing = wires.send(small_ref.at[1 - core], small_sibling, sibling)
    crossings = {}
    for step in (2, 1, 3, 0):
        for part in range(3):
            j = (third[part] + step) % SIDE
            crossings[part, step] = wires.send(
                grads_ref.at[part, 1 - core, j], sibling_in.at[part, j], sibling
            )

    embed_first, embed_second = [], []
    for part in range(2):
        near_axis, far_axis = embed_axes[part]
        embed_first.append(
            DirectGather(
                wires,
                place,
                near_axis,
                lambda j, part=part, k=place[far_axis]: embeds.at[part, core, k, pl.ds(2 * j, 2)],
            )
        )
        embed_second.append(
            RingGather(
                wires,
                place,
                far_axis,
                lambda j, part=part: embeds.at[part, core, j],
                lambda j, h, part=part: embeds.at[part, core, j, pl.ds(4 * h, 4)],
            )
        )
    table_ring = RingReduce(
        wires,
        place,
        X,
        lambda j: table_sums.at[j],
        lambda j, h: table_sums.at[j, pl.ds(TABLE_CHUNKS // 2 * h, TABLE_CHUNKS // 2)],
        TABLE_CHUNKS,
        table_half,
        table_whole,
    )
    rings = []
    for phase, (half_in, whole_in) in enumerate(
        ((half_c, whole_c), (half_b, whole_b), (half_a, whole_a))
    ):
        row = []
        for part in range(3):
            piece, half = block_ring(
                place,
                part,
                phase,
                lambda k3, first, count, part=part: sums.at[part, k3, pl.ds(first, count)],
            )
            row.append(
                RingReduce(
                    wires,
                    place,
                    ORDERS[part][phase],
                    piece,
                    half,
                    (2, 8, 32)[phase],
                    half_in.at[part],
                    whole_in.at[part],
                )
            )
        rings.append(row)
    small_rings = [
        DirectReduce(wires, place, Z, lambda j: small_sums.at[j], 16, small_a),
        DirectReduce(
            wires, place, Y, lambda j: small_sums.at[place[Z], pl.ds(4 * j, 4)], 4, small_b
        ),
        DirectReduce(
            wires, place, X, lambda j: small_sums.at[place[Z], pl.ds(4 * place[Y] + j, 1)], 1, small_c
        ),
    ]

    for copy in swaps:
        copy.wait_recv()
    for ring in embed_first:
        ring.start()
    table_load.wait()
    table_ring.start()

    def add_crossing(part, step):
        j = (third[part] + step) % SIDE
        block_loads[part, step].wait()
        crossings[part, step].wait_recv()
        add_blocks(sums.at[part, j], [sibling_in.at[part, j]], 32)

    small_load.wait()
    small_crossing.wait_recv()
    for j in range(4):
        add_blocks(small_sums.at[j], [small_sibling.at[j]], 16)
    for ring, later in zip(embed_first, embed_second):
        ring.finish()
        later.start()
    small_rings[0].start()
    for part in range(3):
        add_crossing(part, 2)
        rings[2][part].start()
    for ring in embed_second:
        ring.forward()
    for part in range(3):
        add_crossing(part, 1)
        add_crossing(part, 3)
    embed_siblings = []
    for part in range(2):
        k = place[embed_axes[part][1]]
        for step in (0, 1, 3):
            piece = embeds.at[part, core, (k + step) % SIDE]
            embed_siblings.append(wires.send(piece, piece, sibling))
    table_ring.forward()
    for ring in rings[2]:
        ring.forward()
    for part in range(3):
        add_crossing(part, 0)
    for part in range(2):
        embed_second[part].finish()
        k = place[embed_axes[part][1]]
        piece = embeds.at[part, core, (k + 2) % SIDE]
        embed_siblings.append(wires.send(piece, piece, sibling))
    ids_ring.finish()
    small_rings[0].finish()
    small_rings[1].start()

    rows = table_grad_ref.shape[0]
    chunk = rows // 4
    base = lax.axis_index("vocab") * rows
    row_iota = lax.broadcasted_iota(jnp.int32, (chunk, 512), 0)

    @pl.loop(0, 4)
    def _(index):
        at = pl.ds(pl.multiple_of(index * chunk, chunk), chunk)
        table_grad_ref[at] = jnp.zeros((chunk, width), jnp.float32)

    def scatter_rows(part, at_core):
        @pl.loop(0, 8)
        def _(index):
            at_far, pair = index // 2, index % 2
            values = embeds[part, at_core, at_far, pl.ds(4 * pair, 4)].reshape(512, width)
            ids = []
            for which in range(4):
                at_near = 2 * pair + which // 2
                at_z, at_y = (at_far, at_near) if part == 0 else (at_near, at_far)
                inner = (at_z * SIDE + at_y) * 2 + at_core
                ids.append(ids_all[2 * part + which % 2, pl.ds(inner, 1), :])
            ids = jnp.concatenate(ids, 1) - base

            @pl.loop(0, 4)
            def _(row):
                at = pl.ds(pl.multiple_of(row * chunk, chunk), chunk)
                hot = jnp.where(row_iota + row * chunk == ids, 1.0, 0.0).astype(jnp.bfloat16)
                table_grad_ref[at] += jnp.dot(hot, values, preferred_element_type=jnp.float32)

    scatter_rows(0, core)
    table_ring.arrive()
    table_block = rows // TABLE_CHUNKS

    @pl.loop(0, TABLE_CHUNKS)
    def _(index):
        at = pl.ds(pl.multiple_of(index * table_block, table_block), table_block)
        table_grad_ref[at] += (
            table_sums[across, index].astype(jnp.float32)
            + table_whole[0, index].astype(jnp.float32)
            + table_whole[1, index].astype(jnp.float32)
        )

    scatter_rows(1, core)
    small_rings[1].finish()
    small_rings[2].start()
    for ring, later in zip(rings[2], rings[1]):
        ring.finish()
        later.start()
    for copy in embed_siblings:
        copy.wait_recv()
    scatter_rows(0, 1 - core)
    for ring in rings[1]:
        ring.forward()
    scatter_rows(1, 1 - core)
    for ring, later in zip(rings[1], rings[0]):
        ring.finish()
        later.start()
    small_rings[2].finish()
    table_squares = jnp.zeros((1, width), jnp.float32)
    for index in range(4):
        values = table_grad_ref[index * chunk : (index + 1) * chunk]
        table_squares += jnp.sum(values * values, 0, keepdims=True)
    squares = table_squares[:, :128] + table_squares[:, 128:]
    for ring in rings[0]:
        ring.forward()
    for part in range(3):
        rings[0][part].arrive()
        k1, k2, k3 = (place[axis] for axis in ORDERS[part])
        for which in range(2):
            total = sums[part, k3, 8 * k2 + 2 * k1 + which].astype(jnp.float32)
            for side in range(2):
                total += whole_c[part, side, which].astype(jnp.float32)
            grads_out_ref[part, which] = total
            squares += jnp.sum(total * total, 0, keepdims=True)
    loss = sum(loss_ref[:, 128 * index : 128 * (index + 1)] for index in range(4))
    own_small = small_sums[place[Z], 4 * place[Y] + across].astype(jnp.float32)
    final_ref[0, core, place[Z], place[Y], across] = own_small[:8]
    final_ref[1, core, across, place[Z], place[Y]] = jnp.concatenate(
        [own_small[8:9], squares, loss, jnp.zeros((5, 128), jnp.float32)], 0
    )
    lead = [(0, core), (1, core)]
    orders = (((X, Y, Z)), (Y, Z, X))
    for phase in range(3):
        gathers = []
        for part in range(2):
            first_axis, second_axis, third_axis = orders[part]
            keys = (place[third_axis], place[second_axis])[: 2 - phase]
            gathers.append(
                DirectGather(
                    wires,
                    place,
                    orders[part][phase],
                    lambda j, key=lead[part] + keys: final_ref.at[key + (j,)],
                )
            )
        for gather in gathers:
            gather.start()
        for gather in gathers:
            gather.finish()
    copies = []
    for part in range(2):
        mine = final_ref.at[part, core]
        copies.append(wires.send(mine, mine, sibling))
    for copy in copies:
        copy.wait_recv()
    wires.drain()


def finish_call(grads, small, head_grad, d_embed, token_ids, loss_row):
    bf16 = jnp.bfloat16
    groups, chunks, chunk_rows, width = head_grad.shape
    rows = chunks * chunk_rows
    block = (BLOCK, BLOCK)
    return pl.pallas_call(
        finish_kernel,
        name="reduce_and_scatter",
        out_shape=(
            jax.ShapeDtypeStruct((3, 2) + block, jnp.float32),
            jax.ShapeDtypeStruct((rows, width), jnp.float32),
            jax.ShapeDtypeStruct((2, 2, SIDE, SIDE, SIDE, 8, 128), jnp.float32),
        ),
        in_specs=[ANY, ANY, ANY, VMEM, VMEM, VMEM],
        out_specs=(VMEM,) * 3,
        scratch_shapes=[
            pltpu.VMEM((3, SIDE, 32) + block, bf16),
            pltpu.VMEM((3, SIDE, 32) + block, bf16),
            pltpu.VMEM((3, 2, 16) + block, bf16),
            pltpu.VMEM((3, 2, 32) + block, bf16),
            pltpu.VMEM((3, 2, 4) + block, bf16),
            pltpu.VMEM((3, 2, 8) + block, bf16),
            pltpu.VMEM((3, 2, 1) + block, bf16),
            pltpu.VMEM((3, 2, 2) + block, bf16),
            pltpu.VMEM((SIDE, 16, 16, 128), bf16),
            pltpu.VMEM((SIDE, 16, 16, 128), bf16),
            pltpu.VMEM((3, 16, 16, 128), bf16),
            pltpu.VMEM((3, 4, 16, 128), bf16),
            pltpu.VMEM((3, 1, 16, 128), bf16),
            pltpu.VMEM(head_grad.shape, bf16),
            pltpu.VMEM((2, chunks // 2, chunk_rows, width), bf16),
            pltpu.VMEM((2, chunks, chunk_rows, width), bf16),
            pltpu.VMEM((2, 2, SIDE, 8, 128, width), bf16),
            pltpu.VMEM((N_DP,) + token_ids.shape, jnp.int32),
            pltpu.SemaphoreType.DMA((128,)),
            pltpu.SemaphoreType.DMA((128,)),
            pltpu.SemaphoreType.DMA((14,)),
        ],
        compiler_params=pltpu.CompilerParams(
            collective_id=3, has_side_effects=True, vmem_limit_bytes=63 << 20
        ),
    )(grads, small, head_grad, d_embed, token_ids, loss_row)


def row_mean(values):
    return jnp.mean(values, -1, keepdims=True)


def normalized(values):
    center = values - row_mean(values)
    scale = lax.rsqrt(row_mean(center * center) + LN_EPS)
    return center * scale, scale


def norm_backward(d_normed, hat, scale, gain):
    d_hat = d_normed * gain
    d_values = scale * (d_hat - row_mean(d_hat) - hat * row_mean(d_hat * hat))
    d_gain = jnp.sum(d_normed * hat, 0, keepdims=True)
    return d_values, d_gain, jnp.sum(d_normed, 0, keepdims=True)


def lane_range(first, count):
    return pl.ds(pl.multiple_of(first, 128), count)


QKV, PROJ, FC, OUT = (0, 24), (192, 8), (256, 32), (512, 8)


def load_blocks(full_ref, blocks, sems):
    share = blocks.shape[0] // 8
    copies = []
    for index in range(8):
        part = pl.ds(index * share, share)
        copies.append(pltpu.make_async_copy(full_ref.at[part], blocks.at[part], sems.at[index]))
        copies[-1].start()
    return copies


def weight_tiles(blocks, where_ref, matrix, row, rows, column, columns):
    first, in_row = matrix
    return jnp.concatenate(
        [
            jnp.concatenate(
                [
                    blocks[where_ref[first + (row + i) * in_row + column + j]]
                    for j in range(columns)
                ],
                1,
            )
            for i in range(rows)
        ],
        0,
    )


def selected_rows(ref, at_ref, count):
    return jnp.concatenate([ref[pl.ds(at_ref[i], 1), :] for i in range(count)], 0)


def pair_masks(count):
    lane = lax.broadcasted_iota(jnp.int32, (2 * count, 2 * HEAD_DIM), 1)
    row = lax.broadcasted_iota(jnp.int32, (2 * count, 2 * HEAD_DIM), 0)
    return (lane < HEAD_DIM) == (row < count)


def doubled(values, own_lanes):
    both = jnp.concatenate([values, values], 0)
    return jnp.where(own_lanes, both.astype(jnp.float32), 0.0).astype(jnp.bfloat16)


def folded(values, count):
    lane = lax.broadcasted_iota(jnp.int32, (count, 2 * HEAD_DIM), 1)
    return jnp.where(lane < HEAD_DIM, values[:count], values[count:])


def forward_kernel(
    where_ref,
    at_ref,
    length_ref,
    full_ref,
    hidden_ref,
    vec_ref,
    head_in_ref,
    query_ref,
    kv_ref,
    probs_ref,
    attended_ref,
    middle_ref,
    pre_act_ref,
    last_ref,
    blocks,
    normed_rows,
    activated,
    sems,
):
    copies = load_blocks(full_ref, blocks, sems)
    count = head_in_ref.shape[0]
    bf16 = jnp.bfloat16
    hat, _ = normalized(hidden_ref[...])
    normed_rows[...] = hat * vec_ref[0:1] + vec_ref[1:2]
    normed_one = normed_rows[...].astype(bf16)
    normed_own = selected_rows(normed_rows, at_ref, count).astype(bf16)
    for copy in copies:
        copy.wait()

    @pl.loop(0, 4)
    def _(tile):
        at = lane_range(256 * tile, 256)
        weight = weight_tiles(blocks, where_ref, QKV, 0, 8, 2 * tile, 2)
        product = jnp.dot(normed_own, weight, preferred_element_type=jnp.float32)
        query_ref[:, at] = (product + vec_ref[2:3, at]).astype(bf16)

    @pl.loop(0, 4)
    def _(tile):
        at = lane_range(256 * tile, 256)
        weight = weight_tiles(blocks, where_ref, QKV, 0, 8, 8 + 2 * tile, 2)
        product = jnp.dot(normed_one, weight, preferred_element_type=jnp.float32)
        kv_ref[:, at] = product.astype(bf16)

    @pl.loop(0, 4)
    def _(tile):
        weight = weight_tiles(blocks, where_ref, QKV, 0, 8, 16 + 2 * tile, 2)
        product = jnp.dot(normed_one, weight, preferred_element_type=jnp.float32)
        bias = vec_ref[3:4, lane_range(256 * tile, 256)]
        kv_ref[:, lane_range(D + 256 * tile, 256)] = (product + bias).astype(bf16)

    own_lanes = pair_masks(count)
    pairs = HEADS // 2
    seq_len = hidden_ref.shape[0]
    row = lax.broadcasted_iota(jnp.int32, (count, seq_len), 0)
    key = lax.broadcasted_iota(jnp.int32, (count, seq_len), 1)
    last_key = jnp.zeros((count, seq_len), jnp.int32)
    for i in range(count):
        last_key = jnp.where(row == i, jnp.minimum(at_ref[i], length_ref[0] - 1), last_key)
    allowed = jnp.concatenate([key <= last_key] * 2, 0)
    for pair in range(pairs):
        lanes = slice(128 * pair, 128 * pair + 128)
        values_at = slice(D + 128 * pair, D + 128 * pair + 128)
        scores = dot_nt(doubled(query_ref[:, lanes], own_lanes), kv_ref[:, lanes]) * HEAD_DIM ** (
            -0.5
        )
        scores = jnp.where(allowed, scores, NEG_FILL)
        exps = jnp.exp(scores - jnp.max(scores, -1, keepdims=True))
        probs = exps / jnp.sum(exps, -1, keepdims=True)
        probs_ref[2 * count * pair : 2 * count * (pair + 1)] = probs
        mixed = jnp.dot(
            probs.astype(bf16), kv_ref[:, values_at], preferred_element_type=jnp.float32
        )
        attended_ref[:, lanes] = folded(mixed, count).astype(bf16)

    attended = attended_ref[...]
    middle_ref[...] = selected_rows(hidden_ref, at_ref, count) + vec_ref[4:5]

    @pl.loop(0, 4)
    def _(tile):
        weight = weight_tiles(blocks, where_ref, PROJ, 0, 8, 2 * tile, 2)
        middle_ref[:, lane_range(256 * tile, 256)] += jnp.dot(
            attended, weight, preferred_element_type=jnp.float32
        )

    middle = middle_ref[...]
    hat, _ = normalized(middle)
    normed_two = (hat * vec_ref[5:6] + vec_ref[6:7]).astype(bf16)

    @pl.loop(0, 16)
    def _(tile):
        at = lane_range(256 * tile, 256)
        weight = weight_tiles(blocks, where_ref, FC, 0, 8, 2 * tile, 2)
        bias = vec_ref[pl.ds(7 + tile // 4, 1), lane_range(256 * (tile % 4), 256)]
        pre_act = jnp.dot(normed_two, weight, preferred_element_type=jnp.float32) + bias
        pre_act_ref[:, at] = pre_act
        activated[:, at] = gelu(pre_act).astype(bf16)

    last_ref[...] = middle + vec_ref[11:12]

    @pl.loop(0, 16)
    def _(index):
        tile, depth = index // 4, index % 4
        weight = weight_tiles(blocks, where_ref, OUT, 8 * depth, 8, 2 * tile, 2)
        last_ref[:, lane_range(256 * tile, 256)] += jnp.dot(
            activated[:, lane_range(1024 * depth, 1024)],
            weight,
            preferred_element_type=jnp.float32,
        )

    hat, _ = normalized(last_ref[...])
    head_in_ref[...] = (hat * vec_ref[12:13] + vec_ref[13:14]).astype(bf16)


def forward_call(where, positions, length, full, hidden, vectors):
    count = positions.shape[0]
    seq_len = hidden.shape[0]
    bf16 = jnp.bfloat16
    shape = jax.ShapeDtypeStruct
    return pl.pallas_call(
        forward_kernel,
        name="layer_forward",
        out_shape=(
            shape((count, D), bf16),
            shape((count, D), bf16),
            shape((seq_len, 2 * D), bf16),
            shape((HEADS * count, seq_len), jnp.float32),
            shape((count, D), bf16),
            shape((count, D), jnp.float32),
            shape((count, FF), jnp.float32),
            shape((count, D), jnp.float32),
        ),
        grid_spec=pltpu.PrefetchScalarGridSpec(
            num_scalar_prefetch=3,
            grid=(),
            in_specs=[ANY, VMEM, VMEM],
            out_specs=(VMEM,) * 8,
            scratch_shapes=[
                pltpu.VMEM(full.shape, bf16),
                pltpu.VMEM(hidden.shape, jnp.float32),
                pltpu.VMEM((count, FF), bf16),
                pltpu.SemaphoreType.DMA((8,)),
            ],
        ),
        compiler_params=pltpu.CompilerParams(vmem_limit_bytes=48 << 20),
    )(where, positions, length, full, hidden, vectors)


def gelu_slope(values):
    cube = 0.044715 * values * values
    bent = jnp.tanh(GELU_C * (values + cube * values))
    return 0.5 * (1.0 + bent) + 0.5 * values * (1.0 - bent * bent) * GELU_C * (1.0 + 3.0 * cube)


def backward_kernel(
    where_ref,
    at_ref,
    full_ref,
    hidden_ref,
    vec_ref,
    query_ref,
    kv_ref,
    probs_ref,
    attended_ref,
    middle_ref,
    pre_act_ref,
    last_ref,
    d_head_ref,
    grads_ref,
    small_ref,
    d_embed_ref,
    blocks,
    grad_blocks,
    activated,
    d_pre,
    normed,
    rows_out,
    d_qkv,
    spread,
    query_grads,
    vec_grads,
    sems,
    grad_sem,
):
    copies = load_blocks(full_ref, blocks, sems)
    count = d_head_ref.shape[0]
    bf16 = jnp.bfloat16

    def weight_grad(matrix, rows, left_ref, right):
        first, in_row = matrix

        @pl.loop(0, rows)
        def _(row):
            left = left_ref[:, lane_range(128 * row, 128)]
            for column in range(0, in_row, 2):
                product = dot_tn(left, right[:, 128 * column : 128 * column + 256]).astype(bf16)
                for side in range(2):
                    index = first + row * in_row + column + side
                    grad_blocks[index] = product[:, 128 * side : 128 * side + 128]
                    pltpu.make_async_copy(
                        grad_blocks.at[index], grads_ref.at[where_ref[index]], grad_sem
                    ).start()

    hat, scale = normalized(last_ref[...])
    d_last, vec_grads[12:13], vec_grads[13:14] = norm_backward(
        d_head_ref[...], hat, scale, vec_ref[12:13]
    )
    d_branch = d_last.astype(bf16)
    vec_grads[11:12] = jnp.sum(d_branch.astype(jnp.float32), 0, keepdims=True)
    activated[...] = gelu(pre_act_ref[...]).astype(bf16)
    weight_grad(OUT, 32, activated, d_branch)
    for copy in copies:
        copy.wait()

    @pl.loop(0, 16)
    def _(tile):
        at = lane_range(256 * tile, 256)
        weight = weight_tiles(blocks, where_ref, OUT, 2 * tile, 2, 0, 8)
        lowered = (dot_nt(d_branch, weight) * gelu_slope(pre_act_ref[:, at])).astype(bf16)
        d_pre[:, at] = lowered
        vec_grads[pl.ds(7 + tile // 4, 1), lane_range(256 * (tile % 4), 256)] = jnp.sum(
            lowered.astype(jnp.float32), 0, keepdims=True
        )

    hat, scale = normalized(middle_ref[...])
    normed[pl.ds(0, count)] = (hat * vec_ref[5:6] + vec_ref[6:7]).astype(bf16)
    weight_grad(FC, 8, normed.at[pl.ds(0, count)], d_pre[...])
    rows_out[...] = jnp.zeros(rows_out.shape, jnp.float32)

    @pl.loop(0, 16)
    def _(index):
        tile, depth = index // 4, index % 4
        weight = weight_tiles(blocks, where_ref, FC, 2 * tile, 2, 8 * depth, 8)
        rows_out[pl.ds(0, count), lane_range(256 * tile, 256)] += dot_nt(
            d_pre[:, lane_range(1024 * depth, 1024)], weight
        )

    d_middle, vec_grads[5:6], vec_grads[6:7] = norm_backward(
        rows_out[pl.ds(0, count)], hat, scale, vec_ref[5:6]
    )
    d_middle = d_middle + d_last
    d_proj = d_middle.astype(bf16)
    vec_grads[4:5] = jnp.sum(d_proj.astype(jnp.float32), 0, keepdims=True)
    weight_grad(PROJ, 8, attended_ref, d_proj)

    @pl.loop(0, 4)
    def _(tile):
        weight = weight_tiles(blocks, where_ref, PROJ, 2 * tile, 2, 0, 8)
        rows_out[pl.ds(0, count), lane_range(256 * tile, 256)] = dot_nt(d_proj, weight)

    own_lanes = pair_masks(count)
    spread[...] = jnp.zeros(spread.shape, jnp.float32)
    for pair in range(HEADS // 2):
        lanes = slice(128 * pair, 128 * pair + 128)
        values_at = slice(D + 128 * pair, D + 128 * pair + 128)
        d_mixed = doubled(rows_out[0:count, lanes].astype(bf16), own_lanes)
        probs = probs_ref[2 * count * pair : 2 * count * (pair + 1)]
        d_probs = dot_nt(d_mixed, kv_ref[:, values_at])
        inner = jnp.sum(probs * d_probs, -1, keepdims=True)
        d_scores = (probs * (d_probs - inner)).astype(bf16)
        d_values = dot_tn(probs.astype(bf16), d_mixed).astype(bf16)
        d_keys = dot_tn(d_scores, doubled(query_ref[:, lanes], own_lanes)) * HEAD_DIM ** (-0.5)
        d_query = jnp.dot(d_scores, kv_ref[:, lanes], preferred_element_type=jnp.float32)
        d_query = (folded(d_query, count) * HEAD_DIM ** (-0.5)).astype(bf16).astype(jnp.float32)
        vec_grads[2:3, lanes] = jnp.sum(d_query, 0, keepdims=True)
        vec_grads[3:4, lanes] = jnp.sum(d_values.astype(jnp.float32), 0, keepdims=True)
        query_grads[:, lanes] = d_query
        d_qkv[:, D + 128 * pair : D + 128 * pair + 128] = d_keys.astype(bf16)
        d_qkv[:, 2 * D + 128 * pair : 2 * D + 128 * pair + 128] = d_values
    for i in range(count):
        spread[pl.ds(at_ref[i], 1), :] = query_grads[i : i + 1, :]
    d_qkv[:, :D] = spread[...].astype(bf16)
    hat, scale = normalized(hidden_ref[...])
    normed[...] = (hat * vec_ref[0:1] + vec_ref[1:2]).astype(bf16)
    weight_grad(QKV, 8, normed, d_qkv)
    rows_out[...] = jnp.zeros(rows_out.shape, jnp.float32)

    @pl.loop(0, 12)
    def _(index):
        tile, depth = index // 3, index % 3
        weight = weight_tiles(blocks, where_ref, QKV, 2 * tile, 2, 8 * depth, 8)
        rows_out[:, lane_range(256 * tile, 256)] += dot_nt(
            d_qkv[:, lane_range(1024 * depth, 1024)], weight
        )

    d_hidden, vec_grads[0:1], vec_grads[1:2] = norm_backward(
        rows_out[...], hat, scale, vec_ref[0:1]
    )
    rows_out[...] = d_hidden
    for i in range(count):
        rows_out[pl.ds(at_ref[i], 1), :] += d_middle[i : i + 1]
    d_embed_ref[...] = rows_out[...].astype(bf16)
    vec_rows = vec_ref.shape[0]
    for index in range(small_ref.shape[0]):
        group, tile = index // 8, index % 8
        lanes = slice(128 * tile, 128 * tile + 128)
        vec_row = (
            vec_grads[group : group + 1, lanes]
            if group < vec_rows
            else jnp.zeros((1, 128), jnp.float32)
        )
        small_ref[index] = jnp.concatenate(
            [rows_out[8 * group : 8 * group + 8, lanes], vec_row, jnp.zeros((7, 128), jnp.float32)],
            0,
        ).astype(bf16)
    pltpu.make_async_copy(grad_blocks, grads_ref, grad_sem).wait()


def backward_call(where, positions, full, hidden, vectors, cache, d_head):
    count = positions.shape[0]
    bf16 = jnp.bfloat16
    shape = jax.ShapeDtypeStruct
    return pl.pallas_call(
        backward_kernel,
        name="layer_backward",
        out_shape=(
            shape(full.shape, bf16),
            shape((N_DP * N_VOCAB, 16, 128), bf16),
            shape(hidden.shape, bf16),
        ),
        grid_spec=pltpu.PrefetchScalarGridSpec(
            num_scalar_prefetch=2,
            grid=(),
            in_specs=[ANY] + [VMEM] * 10,
            out_specs=(ANY, VMEM, VMEM),
            scratch_shapes=[
                pltpu.VMEM(full.shape, bf16),
                pltpu.VMEM(full.shape, bf16),
                pltpu.VMEM((count, FF), bf16),
                pltpu.VMEM((count, FF), bf16),
                pltpu.VMEM(hidden.shape, bf16),
                pltpu.VMEM(hidden.shape, jnp.float32),
                pltpu.VMEM((hidden.shape[0], 3 * D), bf16),
                pltpu.VMEM(hidden.shape, jnp.float32),
                pltpu.VMEM((count, D), jnp.float32),
                pltpu.VMEM((16, D), jnp.float32),
                pltpu.SemaphoreType.DMA((8,)),
                pltpu.SemaphoreType.DMA,
            ],
        ),
        compiler_params=pltpu.CompilerParams(vmem_limit_bytes=62 << 20),
    )(where, positions, full, hidden, vectors, *cache, d_head)


def slot_places():
    slot = np.arange(N_DP * N_VOCAB * SLOTS)
    device, own = slot // SLOTS, slot % SLOTS
    inner = device % N_VOCAB
    place = (device // N_VOCAB, inner // 2 % SIDE, inner // (2 * SIDE), inner % 2)
    part = own // 2
    result = np.zeros_like(slot)
    for which, (first, second, third) in enumerate(ORDERS):
        index = which * 2 + place[CORE]
        for axis in (third, second, first):
            index = index * SIDE + place[axis]
        result = np.where(part == which, index * 2 + own % 2, result)
    return result.astype(np.int32)


def per_device(
    token_ids,
    seq_lengths,
    loss_positions,
    target_ids,
    block_of_slot,
    matrices,
    left_stats,
    right_stats,
    left_roots,
    right_roots,
    vocab_table,
    table_m,
    table_v,
    positions_table,
    pos_m,
    pos_v,
    vectors,
    vectors_m,
    vectors_v,
):
    vocab_index = lax.axis_index("vocab")
    slots = block_of_slot.shape[0]
    block_iota = jnp.arange(slots, dtype=jnp.int32)
    where = jnp.sum(
        jnp.where(block_of_slot[None, :] == block_iota[:, None], slot_places()[None, :], 0),
        1,
        dtype=jnp.int32,
    )
    own_blocks = matrices.astype(jnp.bfloat16).reshape(3, 2, BLOCK, BLOCK)
    table_low = vocab_table.astype(jnp.bfloat16)
    full, table_full, hidden = start_call(token_ids, own_blocks, table_low, positions_table)
    full_blocks = full.reshape(slots, BLOCK, BLOCK)
    own_length = lax.dynamic_index_in_dim(seq_lengths, vocab_index)
    own_positions = lax.dynamic_index_in_dim(loss_positions, vocab_index, keepdims=False)
    counted = (loss_positions < seq_lengths[:, None]).astype(jnp.float32).reshape(1, -1)
    head_in, *cache = forward_call(where, own_positions, own_length, full_blocks, hidden, vectors)
    d_head_in, head_grad, loss_row = head_call(
        head_in, table_full, target_ids.reshape(1, -1), counted
    )
    grad_blocks, small, d_embed = backward_call(
        where, own_positions, full_blocks, hidden, vectors, cache, d_head_in
    )
    owned_grads, table_grad_own, final = finish_call(
        grad_blocks.reshape(full.shape[:3] + (32, BLOCK, BLOCK)),
        small.reshape(2, SIDE, 16, 16, 128),
        head_grad,
        d_embed,
        token_ids,
        loss_row,
    )
    owned_grads = owned_grads.reshape(SLOTS, BLOCK, BLOCK)
    pos_grad = final[0].reshape(16, 8, 8, 128).transpose(0, 2, 1, 3).reshape(positions_table.shape)
    rest = final[1].transpose(0, 2, 3, 1, 4, 5).reshape(N_DP * N_VOCAB, 8, 128)
    vec_sum = rest[: 8 * vectors.shape[0], 0].reshape(vectors.shape)
    squares_all = jnp.sum(rest[:, 1])
    loss_value = jnp.sum(rest[:, 2])
    grad_norm = jnp.sqrt(squares_all + jnp.sum(pos_grad * pos_grad) + jnp.sum(vec_sum * vec_sum))
    clip_factor = CLIP_LEVEL / jnp.maximum(grad_norm, CLIP_LEVEL)
    matrices_grad = owned_grads * clip_factor
    left_new = STAT_DECAY * left_stats + (1.0 - STAT_DECAY) * jnp.einsum(
        "bij,bkj->bik", matrices_grad, matrices_grad, precision=HIGH
    )
    right_new = STAT_DECAY * right_stats + (1.0 - STAT_DECAY) * jnp.einsum(
        "bji,bjk->bik", matrices_grad, matrices_grad, precision=HIGH
    )
    left_part = jnp.einsum("bij,bjk->bik", left_roots, matrices_grad, precision=HIGH)
    precond = jnp.einsum("bij,bjk->bik", left_part, right_roots, precision=HIGH)
    matrices_new = matrices - SHAMPOO_RATE * (precond + DECAY_RATE * matrices)
    table_new, table_m_new, table_v_new = adamw(
        vocab_table, table_m, table_v, table_grad_own * clip_factor, TABLE_RATE, DECAY_RATE
    )
    positions_new, pos_m_new, pos_v_new = adamw(
        positions_table, pos_m, pos_v, pos_grad * clip_factor, POS_RATE, DECAY_RATE
    )
    vectors_new, vectors_m_new, vectors_v_new = adamw(
        vectors, vectors_m, vectors_v, vec_sum * clip_factor, VECTOR_RATE, 0.0
    )
    return (
        loss_value,
        grad_norm,
        matrices_new,
        left_new,
        right_new,
        matrices_grad,
        table_new,
        table_m_new,
        table_v_new,
        positions_new,
        pos_m_new,
        pos_v_new,
        vectors_new,
        vectors_m_new,
        vectors_v_new,
    )


def solution(mesh):
    in_specs = (
        P("dp", None),
        P("dp"),
        P("dp", None),
        P("dp", None),
        P(),
        P(("dp", "vocab"), None, None),
        P(("dp", "vocab"), None, None),
        P(("dp", "vocab"), None, None),
        P(("dp", "vocab"), None, None),
        P(("dp", "vocab"), None, None),
        P("vocab", "dp"),
        P("vocab", "dp"),
        P("vocab", "dp"),
        P(),
        P(),
        P(),
        P(),
        P(),
        P(),
    )
    out_specs = (
        P(),
        P(),
        P(("dp", "vocab"), None, None),
        P(("dp", "vocab"), None, None),
        P(("dp", "vocab"), None, None),
        P(("dp", "vocab"), None, None),
        P("vocab", "dp"),
        P("vocab", "dp"),
        P("vocab", "dp"),
        P(),
        P(),
        P(),
        P(),
        P(),
        P(),
    )
    return jax.shard_map(
        per_device, mesh=mesh, in_specs=in_specs, out_specs=out_specs, check_vma=False
    )
```

time: 1270 us -> 374 us (0.29)
  waiting for transfers between devices: 619 us -> 0 us
  Pallas kernels: 0 us -> 338 us
  blocking collectives: 193 us -> 0 us
  local copies, waits for them, and re-layouts: 184 us -> 11.8 us
  matrix products: 119 us -> 5.06 us
  other arithmetic: 128 us -> 14.9 us
  between operations: 23 us -> 4.1 us
    reduce_scatter x4 -> x0, waiting for transfers between devices: 481 us -> none  [the longest x1 303 us: per_device(): lax.psum_scatter(jnp.take(grad_blocks, block_of_slot, axis=0), ('dp', 'vo...]
    pallas_call x0 -> x5, Pallas kernels: none -> 338 us  [the longest x1 121 us: finish_call(): pl.pallas_call(finish_kernel, name='reduce_and_scatter', out_shape=(jax.S...]
    all_gather x4 -> x0, waiting for transfers between devices: 138 us -> none  [the longest x1 47.1 us: per_device(): lax.all_gather(d_embed, 'vocab', axis=0, tiled=True)]
    psum x2 -> x0, blocking collectives: 130 us -> none  [the longest x1 65.3 us: per_device(): lax.psum((d_hidden, vec_grads, squares, loss_share), ('dp', 'vocab'))]
    dot_general x23 -> x0, matrix products: 114 us -> none  [the longest x6 43.8 us: dot_tn(): lax.dot_general(left, right, (((0,), (0,)), ((), ())), preferred_element_...]
    reshape x9 -> x3, local copies, waits for them, and re-layouts: 71.2 us -> 1.4 us  [the longest x2 0.74 us: per_device(): (loss_positions < seq_lengths[:, None]).astype(jnp.float32).reshape(1, -1)]
    gather x3 -> x0, local copies, waits for them, and re-layouts: 63.4 us -> none  [the longest x1 35.4 us: per_device(): jnp.take(grad_blocks, block_of_slot, axis=0)]
    pmax x1 -> x0, blocking collectives: 62.2 us -> none  [per_device(): top_all = lax.pmax(local_top, 'vocab')]
  transfers between devices with their start and end apart: 9 -> 0, of which waited for: 6 -> 0; matrix products, arithmetic and copies ran while one was open for 15% -> 0% of each run, Pallas kernels for 0% -> 0%
where the time goes in v1:
time: 374 us
  Pallas kernels  338 us (90%)
  other arithmetic  14.9 us (4%)
  local copies, waits for them, and re-layouts  11.8 us (3%)
  matrix products  5.06 us (1%)
  between operations  4.1 us (1%)
    pallas_call x1, Pallas kernels, finish_call(): pl.pallas_call(finish_kernel, name='reduce_and_scatter', out_shape=(jax.S...  121 us
    pallas_call x1, Pallas kernels, start_call(): pl.pallas_call(start_kernel, name='gather_and_look_up', out_shape=(jax.Sh...  114 us
    pallas_call x1, Pallas kernels, head_call(): pl.pallas_call(head_kernel, name='head', out_shape=(jax.ShapeDtypeStruct(...  40.9 us
    pallas_call x1, Pallas kernels, backward_call(): pl.pallas_call(backward_kernel, name='layer_backward', out_shape=(shape(f...  39.2 us
    pallas_call x1, Pallas kernels, forward_call(): pl.pallas_call(forward_kernel, name='layer_forward', out_shape=(shape((co...  22.2 us
    unnamed x61, local copies, waits for them, and re-layouts  8.2 us

profile of v1, /device:TPU:1, one launch (start us, length us, event | category | flops | bytes accessed | tf_op | source)
XLA Modules:
  0.0 373.5 jit_solution(1649424661761703849)
XLA Ops:
  0.7 1.3 dynamic_slice.9.length_ref
  2.0 0.9 dynamic-slice_reduce_fusion.at_ref
  2.8 1.0 select_reduce_fusion.where_ref
  3.9 0.7 compare_convert_fusion
  4.7 0.7 reshape.75.counted_ref
  5.3 0.8 copy.42
  6.1 0.7 reshape.68.target_ref
  6.8 1.7 convert_element_type.7
  8.5 2.4 convert_element_type.8.table_ref
  10.9 114.3 %gather_and_look_up.1 = (bf16[3,2,4,32,128,128]{5,4,3,2,1,0:T(8,128)(2,1)}, bf16[4,1600,256]{2,1,0:T(8,128)(2,1)}, f32[128,1024]{1,0:T(8,128)}) custom-call(s32[32,128]{1,0:T(8,128)} %ids_ref.3, bf16[3,2,128,128]{3,2,1,0:T(8,128)(2,1)} %bitcast.34, bf16[1600,256]{1,0:T(8,128)(2,1)} %convert_element_type.8.table_ref, f32[128,1024]{1,0:T(8,128)} %positions_ref.1), custom_call_target="tpu_custom_call" | custom-call | tf_op jit(solution)/shard_map/gather_and_look_up/pallas_call | solution.py:467
  125.2 1.0 copy-done.1
  126.3 22.2 %layer_forward.1 = (bf16[16,1024]{1,0:T(8,128)(2,1)S(1)}, bf16[16,1024]{1,0:T(8,128)(2,1)S(1)}, bf16[128,2048]{1,0:T(8,128)(2,1)S(1)}, f32[256,128]{1,0:T(8,128)...) custom-call(s32[768]{0:T(1024)S(1)} %select_reduce_fusion.where_ref,, ...), custom_call_target="tpu_custom_call" | custom-call | tf_op jit(solution)/shard_map/layer_forward/pallas_call | solution.py:1289
  148.5 0.8 copy-done.4
  149.3 0.7 copy-done.5
  150.0 0.7 copy-done.6
  150.6 0.6 copy-done.7
  151.3 0.6 copy-done.8
  151.9 0.6 copy-done.10
  152.5 0.6 copy-done.11
  153.1 0.6 copy-done.12
  153.7 40.9 %head.1 = (f32[16,1024]{1,0:T(8,128)}, bf16[4,20,80,256]{3,2,1,0:T(8,128)(2,1)}, f32[1,512]{1,0:T(1,128)}) custom-call(bf16[16,1024]{1,0:T(8,128)(2,1)} %copy-done.12, bf16[4,1600,256]{2,1,0:T(8,128)(2,1)} %get-tuple-element.45.table_ref, s32[1,512]{1,0:T(1,128)} %reshape.68.target_ref, f32[1,512]{1,0:T(1,128)} %reshape.75.counted_ref), custom_call_target="tpu_custom_call" | custom-call | tf_op jit(solution)/shard_map/head/pallas_call | solution.py:723
  194.7 39.2 %layer_backward.1 = (bf16[768,128,128]{2,1,0:T(8,128)(2,1)}, bf16[128,16,128]{2,1,0:T(8,128)(2,1)}, bf16[128,1024]{1,0:T(8,128)(2,1)}) custom-call(s32[768]{0:T(1024)} %copy-done.9, s32[16]{0:T(128)} %copy-done.13, bf16[768,128,128]{2,1,0:T(8,128)(2,1)} %bitcast.24, f32[128,1024]{1,0:T(8,128)} %get-tuple-element.36.hidden_ref, f32[14,1024]{1,0:T(8,128)} %vec_ref.3, ...), custom_call_target="tpu_custom_call" | custom-call | tf_op jit(solution)/shard_map/layer_backward/pallas_call | solution.py:1482
  233.9 121.0 %reduce_and_scatter.1 = (f32[3,2,128,128]{3,2,1,0:T(8,128)}, f32[1600,256]{1,0:T(8,128)}, f32[2,2,4,4,4,8,128]{6,5,4,3,2,1,0:T(8,128)}) custom-call(bf16[3,2,4,32,128,128]{5,4,3,2,1,0:T(8,128)(2,1)} %bitcast.25, bf16[2,4,16,16,128]{4,3,2,1,0:T(8,128)(2,1)} %bitcast.35, bf16[4,20,80,256]{3,2,1,0:T(8,128)(2,1)} %get-tuple-element.49.head_grad_ref, ...), custom_call_target="tpu_custom_call" | custom-call | tf_op jit(solution)/shard_map/reduce_and_scatter/pallas_call | solution.py:1060
  354.9 2.1 multiply_reduce_fusion
  357.0 0.7 multiply_reduce_fusion.2
  357.8 0.8 slice_reduce_fusion
  360.9 0.7 multiply_subtract_fusion.2
  361.7 1.6 fusion.1
  363.2 1.7 fusion.2
  365.4 1.3 fusion.4
  366.8 1.4 multiply_subtract_fusion.1
  369.3 3.1 multiply_subtract_fusion
  (58 shorter events, 2.0 us)
Async XLA Ops:
  0.6 364.3 %copy-start = (f32[6,128,128]{2,1,0:T(8,128)S(1)}, f32[6,128,128]{2,1,0:T(8,128)}, u32[]{:S(2)}) copy-start(f32[6,128,128]{2,1,0:T(8,128)} %param.28) | copy-start | bytes 1179652
  2.8 122.4 %copy-start.13 = (s32[16]{0:T(128)}, s32[16]{0:T(128)S(1)}, u32[]{:S(2)}) copy-start(s32[16]{0:T(128)S(1)} %dynamic-slice_reduce_fusion.at_ref) | copy-start | bytes 196
  3.9 121.3 %copy-start.9 = (s32[768]{0:T(1024)}, s32[768]{0:T(1024)S(1)}, u32[]{:S(2)}) copy-start(s32[768]{0:T(1024)S(1)} %select_reduce_fusion.where_ref) | copy-start | bytes 9220
  8.5 116.8 %copy-start.2 = (f32[14,1024]{1,0:T(8,128)S(1)}, f32[14,1024]{1,0:T(8,128)}, u32[]{:S(2)}) copy-start(f32[14,1024]{1,0:T(8,128)} %vec_ref.3) | copy-start | bytes 172036
  125.2 1.0 copy-start.1
  148.5 0.8 copy-start.4
  149.3 0.7 copy-start.5
  150.0 0.7 copy-start.6
  150.6 0.6 copy-start.7
  151.3 0.6 copy-start.8
  151.9 0.6 copy-start.10
  152.5 0.6 copy-start.11
  153.1 0.6 copy-start.12
  354.9 5.7 %copy-start.16 = (f32[2,2,4,4,4,8,128]{6,5,4,3,2,1,0:T(8,128)S(1)}, f32[2,2,4,4,4,8,128]{6,5,4,3,2,1,0:T(8,128)}, u32[]{:S(2)}) copy-start(f32[2,2,4,4,4,8,128]{6,5,4,3,2,1,0:T(8,128)} %get-tuple-element.52) | copy-start | bytes 3145732
  354.9 5.9 %copy-start.27 = (f32[3,2,128,128]{3,2,1,0:T(8,128)S(1)}, f32[3,2,128,128]{3,2,1,0:T(8,128)}, u32[]{:S(2)}) copy-start(f32[3,2,128,128]{3,2,1,0:T(8,128)} %get-tuple-element.53) | copy-start | bytes 1179652
  357.0 3.9 %copy-start.3 = (f32[14,1024]{1,0:T(8,128)S(1)}, f32[14,1024]{1,0:T(8,128)}, u32[]{:S(2)}) copy-start(f32[14,1024]{1,0:T(8,128)} %vec_ref.3) | copy-start | bytes 172036
  357.0 3.9 %copy-start.28 = (f32[14,1024]{1,0:T(8,128)S(1)}, f32[14,1024]{1,0:T(8,128)}, u32[]{:S(2)}) copy-start(f32[14,1024]{1,0:T(8,128)} %param.37) | copy-start | bytes 172036
  357.0 3.9 %copy-start.29 = (f32[14,1024]{1,0:T(8,128)S(1)}, f32[14,1024]{1,0:T(8,128)}, u32[]{:S(2)}) copy-start(f32[14,1024]{1,0:T(8,128)} %param.38) | copy-start | bytes 172036
  357.0 4.7 %copy-start.24 = (f32[6,128,128]{2,1,0:T(8,128)S(1)}, f32[6,128,128]{2,1,0:T(8,128)}, u32[]{:S(2)}) copy-start(f32[6,128,128]{2,1,0:T(8,128)} %param.27) | copy-start | bytes 1179652
  360.6 2.6 copy-start.25
  360.8 4.1 %copy-start.14 = (f32[3,2,128,128]{3,2,1,0:T(8,128)}, f32[3,2,128,128]{3,2,1,0:T(8,128)S(1)}, u32[]{:S(2)}) copy-start(f32[3,2,128,128]{3,2,1,0:T(8,128)S(1)} %broadcast_multiply_fusion) | copy-start | bytes 1179652
  361.6 3.8 %copy-start.26 = (f32[6,128,128]{2,1,0:T(8,128)S(1)}, f32[6,128,128]{2,1,0:T(8,128)}, u32[]{:S(2)}) copy-start(f32[6,128,128]{2,1,0:T(8,128)} %param.29) | copy-start | bytes 1179652
  361.7 5.1 %copy-start.23 = (f32[128,1024]{1,0:T(8,128)S(1)}, f32[128,1024]{1,0:T(8,128)}, u32[]{:S(2)}) copy-start(f32[128,1024]{1,0:T(8,128)} %param.35) | copy-start | bytes 1572868
  363.2 2.2 copy-start.21
  363.2 5.0 %copy-start.20 = (f32[1600,256]{1,0:T(8,128)S(1)}, f32[1600,256]{1,0:T(8,128)}, u32[]{:S(2)}) copy-start(f32[1600,256]{1,0:T(8,128)} %get-tuple-element.54) | copy-start | bytes 4915204
  364.9 1.9 copy-start.17
  364.9 1.9 copy-start.22
  365.4 2.8 copy-start.19
  366.8 2.0 copy-start.15
  366.8 2.5 copy-start.18

commit v2 on v1

--- a/solution.py
+++ b/solution.py
@@ -48,16 +48,7 @@
     )
 
 
-def adamw(weight, moment_one, moment_two, grad_in, rate, decay):
-    new_one = BETA_ONE * moment_one + (1.0 - BETA_ONE) * grad_in
-    new_two = BETA_TWO * moment_two + (1.0 - BETA_TWO) * grad_in * grad_in
-    hat_one = new_one / (1.0 - BETA_ONE**STEP)
-    hat_two = new_two / (1.0 - BETA_TWO**STEP)
-    new_weight = weight - rate * (hat_one / (jnp.sqrt(hat_two) + ADAM_EPS) + decay * weight)
-    return (new_weight, new_one, new_two)
-
-
-TABLE_CHUNKS = 20
+VMEM_BYTES = 63 << 20
 MESH_IDS = pl.DeviceIdType.MESH
 ANY = pl.BlockSpec(memory_space=pl.ANY)
 VMEM = pl.BlockSpec(memory_space=pltpu.VMEM)
@@ -85,18 +76,22 @@
     return (place[X], (place[Z] * SIDE + place[Y]) * 2 + place[CORE])
 
 
-def greet(place, axes, far_axes):
+def rings_of(place, axes):
+    others = [moved(place, CORE, 1)]
+    return others + [moved(place, axis, step) for axis in axes for step in (1, 2, 3)]
+
+
+def greet(others):
     barrier = pltpu.get_barrier_semaphore()
-    others = [moved(place, CORE, 1)]
-    for axis in axes:
-        others += [moved(place, axis, 1), moved(place, axis, -1)]
-    for axis in far_axes:
-        others.append(moved(place, axis, 2))
     for other in others:
         pl.semaphore_signal(
             barrier, inc=1, device_id=device_of(other), device_id_type=MESH_IDS
         )
     pl.semaphore_wait(barrier, len(others))
+
+
+def lane_range(first, count):
+    return pl.ds(pl.multiple_of(first, 128), count)
 
 
 class Wires:
@@ -104,23 +99,39 @@
         self.send_sems, self.recv_sems, self.used = send_sems, recv_sems, 0
         self.sent = []
 
-    def send(self, source, target, place):
-        copy = pltpu.make_async_remote_copy(
+    def slot(self):
+        self.used += 1
+        return self.used - 1
+
+    def copy(self, source, target, place, send_slot, recv_slot):
+        return pltpu.make_async_remote_copy(
             src_ref=source,
             dst_ref=target,
-            send_sem=self.send_sems.at[self.used],
-            recv_sem=self.recv_sems.at[self.used],
+            send_sem=self.send_sems.at[send_slot],
+            recv_sem=self.recv_sems.at[recv_slot],
             device_id=device_of(place),
             device_id_type=MESH_IDS,
         )
-        self.used += 1
+
+    def send(self, source, target, place, bundle=None):
+        recv_slot = self.slot()
+        copy = self.copy(source, target, place, recv_slot if bundle is None else bundle, recv_slot)
         copy.start()
-        self.sent.append(copy)
+        if bundle is None:
+            self.sent.append(copy)
         return copy
 
-    def drain(self):
-        for copy in self.sent:
+    def send_all(self, source, target, place, bundle):
+        self.copy(source, target, place, bundle, bundle).start()
+
+    def whole(self, ref, place, bundle):
+        return self.copy(ref, ref, place, bundle, bundle)
+
+    def settle(self, latest=0):
+        done = len(self.sent) - latest
+        for copy in self.sent[:done]:
             copy.wait_send()
+        self.sent = self.sent[done:]
 
 
 def add_blocks(target, sources, count):
@@ -133,15 +144,16 @@
 
 
 class RingGather:
-    def __init__(self, wires, place, axis, piece, half):
+    def __init__(self, wires, place, axis, piece, half, own=None):
         self.wires, self.place, self.axis = wires, place, axis
         self.piece, self.half = piece, half
         self.mine = place[axis]
+        self.own = self.piece(self.mine) if own is None else own
 
     def start(self):
         mine = self.piece(self.mine)
-        self.up = self.wires.send(mine, mine, moved(self.place, self.axis, 1))
-        self.down = self.wires.send(mine, mine, moved(self.place, self.axis, -1))
+        self.up = self.wires.send(self.own, mine, moved(self.place, self.axis, 1))
+        self.down = self.wires.send(self.own, mine, moved(self.place, self.axis, -1))
 
     def forward(self):
         self.up.wait_recv()
@@ -157,13 +169,15 @@
 
 
 class DirectGather:
-    def __init__(self, wires, place, axis, piece):
+    def __init__(self, wires, place, axis, piece, own=None):
         self.wires, self.place, self.axis, self.piece = wires, place, axis, piece
+        self.own = self.piece(place[axis]) if own is None else own
 
     def start(self):
         mine = self.piece(self.place[self.axis])
         self.copies = [
-            self.wires.send(mine, mine, moved(self.place, self.axis, step)) for step in (1, 2, 3)
+            self.wires.send(self.own, mine, moved(self.place, self.axis, step))
+            for step in (1, 2, 3)
         ]
 
     def finish(self):
@@ -234,6 +248,75 @@
         )
 
 
+class RowGather:
+    def __init__(self, wires, place, axis, first, row):
+        self.wires, self.place, self.axis = wires, place, axis
+        self.row, self.mine, self.first = row, place[axis], first
+        self.up, self.down, self.far = [], [], {}
+        self.bundles = [wires.slot() for _ in range(3)]
+
+    def of(self, piece, index):
+        return self.row((self.mine + piece) % SIDE, (self.first + (0, 1, 3, 2)[index]) % SIDE)
+
+    def send(self, index):
+        mine = self.of(0, index)
+        up, down = moved(self.place, self.axis, 1), moved(self.place, self.axis, -1)
+        self.up.append(self.wires.send(mine, mine, up, self.bundles[0]))
+        self.down.append(self.wires.send(mine, mine, down, self.bundles[1]))
+
+    def forward(self, index):
+        upward = index < 2
+        (self.up if upward else self.down)[index].wait_recv()
+        passed = self.of(3 if upward else 1, index)
+        step = 1 if upward else -1
+        target = moved(self.place, self.axis, step)
+        self.far[index] = self.wires.send(passed, passed, target, self.bundles[2])
+        return passed
+
+    def take(self, index):
+        (self.down if index < 2 else self.up)[index].wait_recv()
+        return self.of(1 if index < 2 else 3, index)
+
+    def take_far(self, index):
+        self.far[index].wait_recv()
+        return self.of(2, index)
+
+    def settle(self, piece):
+        for bundle in self.bundles:
+            self.wires.whole(piece, self.place, bundle).wait_send()
+
+
+class QuarterReduce(RingReduce):
+    def start(self, chunk):
+        far = (self.mine + 2) % SIDE
+        up, down = moved(self.place, self.axis, 1), moved(self.place, self.axis, -1)
+        size = self.count // 4
+        landing = pl.ds(chunk * size, size)
+        if chunk == 0:
+            self.far_ups, self.far_downs = [], []
+        self.far_ups.append(
+            self.wires.send(self.half(far, chunk), self.half_in.at[0, landing], up)
+        )
+        self.far_downs.append(
+            self.wires.send(self.half(far, 2 + chunk), self.half_in.at[1, landing], down)
+        )
+
+    def forward(self):
+        after, before = (self.mine + 1) % SIDE, (self.mine + 3) % SIDE
+        up, down = moved(self.place, self.axis, 1), moved(self.place, self.axis, -1)
+        size = self.count // 4
+        for chunk, copy in enumerate(self.far_ups):
+            copy.wait_recv()
+            landed = self.half_in.at[0, pl.ds(chunk * size, size)]
+            add_blocks(self.half(after, chunk), [landed], size)
+        self.up = self.wires.send(self.piece(after), self.whole_in.at[0], up)
+        for chunk, copy in enumerate(self.far_downs):
+            copy.wait_recv()
+            landed = self.half_in.at[1, pl.ds(chunk * size, size)]
+            add_blocks(self.half(before, 2 + chunk), [landed], size)
+        self.down = self.wires.send(self.piece(before), self.whole_in.at[1], down)
+
+
 def block_ring(place, part, phase, at):
     first_axis, second_axis, third_axis = ORDERS[part]
     k1, k2, k3 = place[first_axis], place[second_axis], place[third_axis]
@@ -244,17 +327,18 @@
         )
     if phase == 1:
         return (lambda j: at(k3, 8 * j, 8), lambda j, h: at(k3, 8 * j + 4 * h, 4))
-    return (lambda j: at(j, 0, 32), lambda j, h: at(j, 16 * h, 16))
+    return (lambda j: at(j, 0, 32), lambda j, q: at(j, 8 * q, 8))
 
 
 def start_kernel(
     ids_ref,
-    own_ref,
+    matrices_ref,
     table_ref,
     positions_ref,
     full_ref,
     table_full_ref,
     hidden_ref,
+    own_low,
     table_pad,
     ids_all,
     parts,
@@ -273,60 +357,72 @@
     across = place[X]
     sibling = moved(place, CORE, 1)
     wires = Wires(send_sems, recv_sems)
+    own_low[...] = matrices_ref[...].astype(jnp.bfloat16).reshape(own_low.shape)
     own_copies = []
     for part in range(3):
         k1, k2, k3 = (place[axis] for axis in ORDERS[part])
         own_copies.append(
             pltpu.make_async_copy(
-                own_ref.at[part],
+                own_low.at[part],
                 full_ref.at[part, core, k3, pl.ds(8 * k2 + 2 * k1, 2)],
                 local_sems.at[part],
             )
         )
-    own_copies.append(
-        pltpu.make_async_copy(table_ref, table_full_ref.at[across], local_sems.at[3])
-    )
-    for copy in own_copies:
-        copy.start()
+        own_copies[-1].start()
     ids_all[across] = ids_ref[...]
-    greet(place, (X, Y, Z), (X, Y, Z))
+    greet(rings_of(place, (X, Y, Z)))
+    rings = [[], [], []]
+    for part in range(3):
+
+        def at(k3, first, count, part=part):
+            return full_ref.at[part, core, k3, pl.ds(first, count)]
+
+        first_axis, second_axis, third_axis = ORDERS[part]
+        piece, _ = block_ring(place, part, 0, at)
+        rings[0].append(DirectGather(wires, place, first_axis, piece, own_low.at[part]))
+        piece, half = block_ring(place, part, 1, at)
+        rings[1].append(RingGather(wires, place, second_axis, piece, half))
+        rings[2].append(
+            RowGather(
+                wires,
+                place,
+                third_axis,
+                place[second_axis],
+                lambda j, row, at=at: at(j, 8 * row, 8),
+            )
+        )
+    on_z, on_x, on_y = rings[2]
     ids_ring = DirectGather(wires, place, X, lambda j: ids_all.at[j])
     ids_ring.start()
-    rings = []
-    for phase in range(3):
-        row = []
-        for part in range(3):
-            piece, half = block_ring(
-                place,
-                part,
-                phase,
-                lambda k3, first, count, part=part: full_ref.at[
-                    part, core, k3, pl.ds(first, count)
-                ],
-            )
-            row.append(RingGather(wires, place, ORDERS[part][phase], piece, half))
-        rings.append(row)
-    for copy, ring in zip(own_copies, rings[0]):
-        copy.wait()
+    for ring in rings[0]:
         ring.start()
-    own_copies[3].wait()
-    table_ring = RingGather(
+    rows = table_ref.shape[0]
+    table_pad[pl.ds(0, rows)] = table_ref[...].astype(jnp.bfloat16)
+    padding = table_pad.shape[0] - rows
+    table_pad[pl.ds(rows, padding)] = jnp.zeros((padding, table_pad.shape[1]), jnp.bfloat16)
+    table_low = table_pad.at[pl.ds(0, rows)]
+    own_copies.append(
+        pltpu.make_async_copy(table_low, table_full_ref.at[across], local_sems.at[3])
+    )
+    own_copies[-1].start()
+    table_ring = RowGather(
         wires,
         place,
         X,
-        lambda j: table_full_ref.at[j],
-        lambda j, h: table_full_ref.at[j, pl.ds(800 * h, 800)],
-    )
-    rows = table_ref.shape[0]
-    table_pad[pl.ds(0, rows)] = table_ref[...]
-    padding = table_pad.shape[0] - rows
-    table_pad[pl.ds(rows, padding)] = jnp.zeros((padding, table_pad.shape[1]), jnp.bfloat16)
+        0,
+        lambda j, row: table_full_ref.at[j, pl.ds(rows // SIDE * row, rows // SIDE)],
+    )
+    own_copies[3].wait()
+    table_ring.send(0)
     base = (lax.axis_index("vocab") * rows).astype(jnp.float32)
     tiles = table_pad.shape[0] // 128
     lane = lax.broadcasted_iota(jnp.int32, (128, 128), 1).astype(jnp.float32)
 
-    def look_up(group):
-        part = group // 2
+    def group_of(part, which):
+        return 2 * ((across // 2 + part) % 2) + which
+
+    def look_up(part, side):
+        group = group_of(part, side)
 
         @pl.loop(0, 8)
         def _(quad):
@@ -350,7 +446,7 @@
             for which in range(4):
                 at_y = 2 * (quad % 2) + which // 2
                 first, second = (at_z, at_y) if part == 0 else (at_y, at_z)
-                parts[part, which % 2, first, 2 * second + group % 2] = found[
+                parts[part, which % 2, first, 2 * second + side] = found[
                     128 * which : 128 * which + 128
                 ]
 
@@ -383,28 +479,6 @@
                 landing.at[part],
             )
         )
-    ids_ring.finish()
-    for ring in rings[0]:
-        ring.forward()
-    for ring, later in zip(rings[0], rings[1]):
-        ring.finish()
-        later.start()
-    look_up(0)
-    for ring in rings[1]:
-        ring.forward()
-    look_up(1)
-    siblings = [to_sibling(0)]
-    for ring, later in zip(rings[1], rings[2]):
-        ring.finish()
-        later.start()
-    table_ring.start()
-    block_siblings = []
-    for part in range(3):
-        own = full_ref.at[part, core, place[ORDERS[part][2]]]
-        block_siblings.append(wires.send(own, own, sibling))
-    look_up(2)
-    look_up(3)
-    siblings.append(to_sibling(1))
 
     def add_sibling(part):
         siblings[part].wait_recv()
@@ -412,24 +486,8 @@
             add_blocks(parts.at[part, core, j], [sibling_in.at[part, j]], 8)
         lookup_rings[part].start()
 
-    add_sibling(0)
-    add_sibling(1)
-    table_ring.forward()
-    for ring in lookup_rings:
-        ring.forward()
-    for ring in rings[2]:
-        ring.forward()
-    for part in range(3):
-        k3 = place[ORDERS[part][2]]
-        for step in (1, 3):
-            piece = full_ref.at[part, core, (k3 + step) % SIDE]
-            block_siblings.append(wires.send(piece, piece, sibling))
-    for ring, end in zip(lookup_rings, lookup_ends):
-        ring.finish()
-        end.start()
-    for part in range(2):
-        end = lookup_ends[part]
-        end.arrive()
+    def take_result(part):
+        lookup_ends[part].arrive()
         first_axis, second_axis = lookup_axes[part]
         for which in range(2):
             total = parts[part, core, place[first_axis], 2 * place[second_axis] + which].astype(
@@ -437,12 +495,72 @@
             )
             for step in range(3):
                 total += landing[part, step, which].astype(jnp.float32)
-            ready[2 * part + which] = total.astype(jnp.bfloat16)
+            ready[group_of(part, which)] = total.astype(jnp.bfloat16)
+
+    shares = [wires.slot() for _ in range(3)]
+
+    def share(part, ref):
+        wires.send_all(ref, ref, sibling, shares[part])
+
+    look_up(0, across % 2)
+    ids_ring.finish()
+    for copy in own_copies[:3]:
+        copy.wait()
+    for ring, later in zip(rings[0], rings[1]):
+        ring.finish()
+        later.start()
+    for ring in rings[2]:
+        ring.send(0)
+    look_up(0, 1 - across % 2)
+    siblings = [to_sibling(0)]
+    for ring in rings[1]:
+        ring.forward()
+    for ring in rings[2]:
+        ring.send(1)
+    look_up(1, 0)
+    add_sibling(0)
+    for ring in rings[1]:
+        ring.finish()
+    for ring in rings[2]:
+        ring.send(2)
+    on_y.send(3)
+    on_x.send(3)
+    for index in (1, 2, 3):
+        table_ring.send(index)
+    look_up(1, 1)
+    siblings.append(to_sibling(1))
+    lookup_rings[0].forward()
+    on_z.send(3)
+    add_sibling(1)
+    for part in range(3):
+        share(part, full_ref.at[part, core, place[ORDERS[part][2]]])
+    lookup_rings[1].forward()
+    lookup_rings[0].finish()
+    lookup_ends[0].start()
+    share(0, on_z.forward(0))
+    share(0, on_z.forward(2))
+    share(1, on_x.forward(0))
+    share(1, on_x.forward(2))
+    lookup_rings[1].finish()
+    lookup_ends[1].start()
+    share(1, on_x.forward(1))
+    share(1, on_x.forward(3))
+    for index in (0, 2, 1, 3):
+        share(2, on_y.forward(index))
+    share(0, on_z.forward(1))
+    share(0, on_z.forward(3))
+    take_result(0)
+    take_result(1)
     swaps = []
     for step in (1, 2, 3):
         there = moved(place, X, step)
         swaps.append(wires.send(ready.at[there[X]], arrived.at[across], there))
     arrived[across] = ready[across]
+    for index in (0, 2, 1, 3):
+        table_ring.forward(index)
+    for part in range(3):
+        for index in range(4):
+            share(part, rings[2][part].take(index))
     for copy in swaps:
         copy.wait_recv()
     for source in range(4):
@@ -450,18 +568,22 @@
         hidden_ref[:, columns] = (
             arrived[source].astype(jnp.float32) + positions_ref[:, columns]
         )
-    table_ring.finish()
+    for index in range(4):
+        table_ring.take(index)
+    wires.settle()
+    for index in (0, 2, 1, 3):
+        for part in range(3):
+            share(part, rings[2][part].take_far(index))
+    for index in range(4):
+        table_ring.take_far(index)
+    table_ring.settle(table_full_ref.at[across])
     for part in range(3):
-        rings[2][part].finish()
-        far = full_ref.at[part, core, (place[ORDERS[part][2]] + 2) % SIDE]
-        block_siblings.append(wires.send(far, far, sibling))
-    for copy in block_siblings:
-        copy.wait_recv()
-    wires.drain()
-
-
-def start_call(token_ids, own_blocks, table_low, positions_table):
-    rows, width = table_low.shape
+        rings[2][part].settle(full_ref.at[part, core, 0])
+        wires.whole(full_ref.at[part, core], sibling, shares[part]).wait()
+
+
+def start_call(token_ids, matrices, vocab_table, positions_table):
+    rows, width = vocab_table.shape
     padded = -(-rows // 128) * 128
     bf16 = jnp.bfloat16
     return pl.pallas_call(
@@ -472,9 +594,10 @@
             jax.ShapeDtypeStruct((N_DP, rows, width), bf16),
             jax.ShapeDtypeStruct(positions_table.shape, jnp.float32),
         ),
-        in_specs=[VMEM, ANY, VMEM, VMEM],
+        in_specs=[VMEM] * 4,
         out_specs=(ANY, ANY, VMEM),
         scratch_shapes=[
+            pltpu.VMEM((3, 2, BLOCK, BLOCK), bf16),
             pltpu.VMEM((padded, width), bf16),
             pltpu.VMEM((N_DP,) + token_ids.shape, jnp.int32),
             pltpu.VMEM((2, 2, SIDE, 8, 128, width), bf16),
@@ -484,38 +607,46 @@
             pltpu.VMEM((2, 3, 2, 128, width), bf16),
             pltpu.VMEM((N_DP, 128, width), bf16),
             pltpu.VMEM((N_DP, 128, width), bf16),
-            pltpu.SemaphoreType.DMA((80,)),
-            pltpu.SemaphoreType.DMA((80,)),
+            pltpu.SemaphoreType.DMA((140,)),
+            pltpu.SemaphoreType.DMA((140,)),
             pltpu.SemaphoreType.DMA((4,)),
         ],
         compiler_params=pltpu.CompilerParams(
-            collective_id=1, has_side_effects=True, vmem_limit_bytes=60 << 20
+            collective_id=1, has_side_effects=True, vmem_limit_bytes=VMEM_BYTES
         ),
-    )(token_ids, own_blocks, table_low, positions_table)
+    )(token_ids, matrices, vocab_table, positions_table)
 
 
 def head_kernel(
     head_in_ref,
     table_ref,
     target_ref,
-    counted_ref,
+    at_ref,
+    length_ref,
     d_head_ref,
-    table_grad_ref,
+    own_grad_ref,
+    next_grad_ref,
+    far_grad_ref,
+    last_grad_ref,
     loss_ref,
+    table,
+    table_grads,
     pieces,
     rows_in,
     logits,
     d_logits,
     stats,
-    stats_in,
     d_rows,
     d_sibling,
     d_first,
     d_second,
     send_sems,
     recv_sems,
+    local_sems,
 ):
     place = coordinates()
+    table_load = pltpu.make_async_copy(table_ref, table, local_sems.at[4])
+    table_load.start()
     core = place[CORE]
     sibling = moved(place, CORE, 1)
     wires = Wires(send_sems, recv_sems)
@@ -527,7 +658,13 @@
         pieces[part, core, far, near] = head_in_ref[
             :, part * half_width : (part + 1) * half_width
         ]
-    greet(place, (Y, Z), (Y, Z))
+    vocab_group = [
+        moved(moved(moved(place, Y, near), Z, far), CORE, side)
+        for near in range(SIDE)
+        for far in range(SIDE)
+        for side in range(2)
+    ][1:]
+    greet(vocab_group)
     first_rings, second_rings = [], []
     for part in range(2):
         near_axis, far_axis = feature_axes[part]
@@ -544,6 +681,28 @@
         )
     for ring in first_rings:
         ring.start()
+    seqs = target_ref.shape[1]
+    column = lax.broadcasted_iota(jnp.int32, (seqs, seqs * own), 1)
+    row = lax.broadcasted_iota(jnp.int32, (seqs, seqs * own), 0)
+    own_seq = jnp.where(column // own == row, 1.0, 0.0)
+    slot = lax.broadcasted_iota(jnp.int32, (own, seqs * own), 0)
+    slot_column = lax.broadcasted_iota(jnp.int32, (own, seqs * own), 1)
+    own_slot = slot_column % own == slot
+
+    def laid_end_to_end(values):
+        wide = jnp.dot(
+            values.astype(jnp.float32), own_seq, precision=HIGH, preferred_element_type=jnp.float32
+        )
+        return jnp.sum(jnp.where(own_slot, wide, 0.0), 0, keepdims=True)
+
+    target = laid_end_to_end(target_ref[...]).astype(jnp.int32)
+    lengths = jnp.dot(
+        length_ref[...].astype(jnp.float32),
+        own_seq,
+        precision=HIGH,
+        preferred_element_type=jnp.float32,
+    )
+    counted = (laid_end_to_end(at_ref[...]) < lengths).astype(jnp.float32)
     for ring, later in zip(first_rings, second_rings):
         ring.finish()
         later.start()
@@ -559,20 +718,19 @@
         rows_in[own * index : own * (index + 1), :half_width] = pieces[0, at_core, at_z, at_y]
         rows_in[own * index : own * (index + 1), half_width:] = pieces[1, at_core, at_y, at_z]
 
-    groups, rows, group_width = table_ref.shape
+    table_load.wait()
+    groups, rows, group_width = table.shape
     count = rows_in.shape[0]
     chunk = rows // 4
     base = lax.axis_index("vocab") * rows
     row_iota = lax.broadcasted_iota(jnp.int32, (chunk, count), 0)
-    target = target_ref[...]
-    counted = counted_ref[...]
 
     def logit_chunk(index, top):
         at = pl.ds(pl.multiple_of(index * chunk, chunk), chunk)
         total = jnp.zeros((chunk, count), jnp.float32)
         for group in range(groups):
             total += lax.dot_general(
-                table_ref[group, at],
+                table[group, at],
                 rows_in[:, group * group_width : (group + 1) * group_width],
                 (((1,), (1,)), ((), ())),
                 preferred_element_type=jnp.float32,
@@ -600,23 +758,14 @@
     lanes = count // 4
     top = jnp.concatenate([local_top[:, lanes * i : lanes * (i + 1)] for i in range(4)], 0)
     total = jnp.concatenate([local_total[:, lanes * i : lanes * (i + 1)] for i in range(4)], 0)
-    for phase, (axis, steps) in enumerate(((CORE, (1,)), (Y, (1, 2, 3)), (Z, (1, 2, 3)))):
-        stats[phase] = jnp.concatenate([top, total], 0)
-        copies = [
-            wires.send(stats.at[phase], stats_in.at[phase, step - 1], moved(place, axis, step))
-            for step in steps
-        ]
-        for copy in copies:
-            copy.wait_recv()
-        tops, totals = [top], [total]
-        for step in steps:
-            received = stats_in[phase, step - 1]
-            tops.append(received[:4])
-            totals.append(received[4:])
-        top = tops[0]
-        for other in tops[1:]:
-            top = jnp.maximum(top, other)
-        total = sum(part * jnp.exp(part_top - top) for part, part_top in zip(totals, tops))
+    mine = stats.at[lax.axis_index("vocab")]
+    mine[...] = jnp.concatenate([top, total], 0)
+    bundle = wires.slot()
+    for other in vocab_group:
+        wires.send_all(mine, mine, other, bundle)
+    wires.whole(stats.at[pl.ds(0, len(vocab_group))], sibling, bundle).wait()
+    top = jnp.max(stats[:, :4], 0)
+    total = jnp.sum(stats[:, 4:] * jnp.exp(stats[:, :4] - top[None]), 0)
     log_total = top + jnp.log(total)
     log_total = jnp.concatenate([log_total[i : i + 1] for i in range(4)], 1)
     first_device = (lax.axis_index("vocab") == 0).astype(jnp.float32)
@@ -635,7 +784,7 @@
         for group in range(groups):
             rows_grad = lax.dot_general(
                 lowered,
-                table_ref[group],
+                table[group],
                 (((0,), (0,)), ((), ())),
                 preferred_element_type=jnp.float32,
             ).astype(jnp.bfloat16)
@@ -679,31 +828,33 @@
         )
         first_rings[part].start()
 
-    def table_grad_chunk(index):
-        at = pl.ds(pl.multiple_of(index * chunk, chunk), chunk)
-        blocks_in_chunk = chunk // table_grad_ref.shape[2]
-        for group in range(groups):
+    grad_refs = (own_grad_ref, next_grad_ref, far_grad_ref, last_grad_ref)
+    stores = []
+
+    def table_grad(step):
+        group = (place[X] + step) % N_DP
+        columns = lane_range(group * group_width, group_width)
+
+        @pl.loop(0, 4)
+        def _(index):
+            at = pl.ds(pl.multiple_of(index * chunk, chunk), chunk)
             product = jnp.dot(
-                d_logits[at],
-                rows_in[:, group * group_width : (group + 1) * group_width],
-                preferred_element_type=jnp.float32,
+                d_logits[at], rows_in[:, columns], preferred_element_type=jnp.float32
             ).astype(jnp.bfloat16)
-            table_grad_ref[group, pl.ds(index * blocks_in_chunk, blocks_in_chunk)] = (
-                product.reshape((blocks_in_chunk,) + table_grad_ref.shape[2:])
-            )
-
-    @pl.loop(0, 2)
-    def _(index):
-        table_grad_chunk(index)
-
+            table_grads[step, at] = product
+
+        stores.append(
+            pltpu.make_async_copy(table_grads.at[step], grad_refs[step], local_sems.at[step])
+        )
+        stores[-1].start()
+
+    table_grad(1)
+    table_grad(2)
     for ring, later in zip(first_rings, second_rings):
         ring.finish()
         later.start()
-
-    @pl.loop(2, 4)
-    def _(index):
-        table_grad_chunk(index)
-
+    table_grad(3)
+    table_grad(0)
     for part in range(2):
         second_rings[part].arrive()
         first_axis, second_axis = reduce_axes[part]
@@ -711,13 +862,15 @@
         for step in range(3):
             total += d_second[part, step].astype(jnp.float32)
         d_head_ref[:, part * half_width : (part + 1) * half_width] = total
-    wires.drain()
-
-
-def head_call(head_in, table_full, target_row, counted_row):
+    wires.settle()
+    for copy in stores:
+        copy.wait()
+
+
+def head_call(head_in, table_full, targets, positions, lengths):
     groups, rows, group_width = table_full.shape
     own, width = head_in.shape
-    count = target_row.shape[1]
+    count = targets.size
     half = width // 2
     bf16 = jnp.bfloat16
     return pl.pallas_call(
@@ -725,59 +878,63 @@
         name="head",
         out_shape=(
             jax.ShapeDtypeStruct((own, width), jnp.float32),
-            jax.ShapeDtypeStruct((groups, TABLE_CHUNKS, rows // TABLE_CHUNKS, group_width), bf16),
+            *[jax.ShapeDtypeStruct((rows, group_width), bf16)] * groups,
             jax.ShapeDtypeStruct((1, count), jnp.float32),
         ),
-        in_specs=[VMEM] * 4,
-        out_specs=(VMEM,) * 3,
+        in_specs=[VMEM, ANY, VMEM, VMEM, VMEM],
+        out_specs=(VMEM,) + (ANY,) * groups + (VMEM,),
         scratch_shapes=[
+            pltpu.VMEM(table_full.shape, bf16),
+            pltpu.VMEM(table_full.shape, bf16),
             pltpu.VMEM((2, 2, SIDE, SIDE, own, half), bf16),
             pltpu.VMEM((count, width), bf16),
             pltpu.VMEM((rows, count), jnp.float32),
             pltpu.VMEM((rows, count), bf16),
-            pltpu.VMEM((3, 8, count // 4), jnp.float32),
-            pltpu.VMEM((3, 3, 8, count // 4), jnp.float32),
+            pltpu.VMEM((N_VOCAB, 8, count // 4), jnp.float32),
             pltpu.VMEM((2, 2, SIDE, SIDE, own, half), bf16),
             pltpu.VMEM((2, SIDE, SIDE, own, half), bf16),
             pltpu.VMEM((2, 3, SIDE, own, half), bf16),
             pltpu.VMEM((2, 3, own, half), bf16),
             pltpu.SemaphoreType.DMA((40,)),
             pltpu.SemaphoreType.DMA((40,)),
+            pltpu.SemaphoreType.DMA((5,)),
         ],
         compiler_params=pltpu.CompilerParams(
-            collective_id=2, has_side_effects=True, vmem_limit_bytes=60 << 20
+            collective_id=2, has_side_effects=True, vmem_limit_bytes=VMEM_BYTES
         ),
-    )(head_in, table_full, target_row, counted_row)
+    )(head_in, table_full, targets, positions, lengths)
 
 
 def finish_kernel(
     grads_ref,
     small_ref,
-    head_grad_ref,
+    own_grad_ref,
+    next_grad_ref,
+    far_grad_ref,
+    last_grad_ref,
     d_embed_ref,
     ids_ref,
     loss_ref,
     grads_out_ref,
     table_grad_ref,
     final_ref,
+    totals_ref,
     sums,
     sibling_in,
     half_a,
     whole_a,
     half_b,
     whole_b,
-    half_c,
     whole_c,
     small_sums,
     small_sibling,
     small_a,
     small_b,
     small_c,
-    table_sums,
-    table_half,
-    table_whole,
+    table_parts,
     embeds,
     ids_all,
+    totals_all,
     send_sems,
     recv_sems,
     local_sems,
@@ -796,13 +953,16 @@
         return copy
 
     third = [place[ORDERS[part][2]] for part in range(3)]
-    table_load = load(head_grad_ref, table_sums)
+    small_load = load(small_ref.at[core], small_sums)
     block_loads = {}
     for step in (2, 1, 3, 0):
         for part in range(3):
             j = (third[part] + step) % SIDE
             block_loads[part, step] = load(grads_ref.at[part, core, j], sums.at[part, j])
-    small_load = load(small_ref.at[core], small_sums)
+    table_loads = [
+        load(ref, table_parts.at[index])
+        for index, ref in enumerate((own_grad_ref, next_grad_ref, far_grad_ref, last_grad_ref))
+    ]
 
     width = table_grad_ref.shape[1]
     embed_axes = ((Y, Z), (Z, Y))
@@ -813,7 +973,13 @@
     own_columns = pl.ds(pl.multiple_of(across * width, width), width)
     landing[...] = d_embed_ref[:, own_columns]
     ids_all[across] = ids_ref[...]
-    greet(place, (X, Y, Z), (X, Y, Z))
+    line = [
+        moved(moved(place, X, step), CORE, side) for step in range(SIDE) for side in range(2)
+    ][1:]
+    plane = [
+        moved(moved(place, Y, step), Z, other) for step in range(SIDE) for other in range(SIDE)
+    ][1:]
+    greet(line + plane)
     swaps = []
     for step in (1, 2, 3):
         there = moved(place, X, step)
@@ -834,11 +1000,14 @@
     for part in range(2):
         near_axis, far_axis = embed_axes[part]
         embed_first.append(
-            DirectGather(
+            RingGather(
                 wires,
                 place,
                 near_axis,
                 lambda j, part=part, k=place[far_axis]: embeds.at[part, core, k, pl.ds(2 * j, 2)],
+                lambda j, h, part=part, k=place[far_axis]: embeds.at[
+                    part, core, k, pl.ds(2 * j + h, 1)
+                ],
             )
         )
         embed_second.append(
@@ -850,41 +1019,27 @@
                 lambda j, h, part=part: embeds.at[part, core, j, pl.ds(4 * h, 4)],
             )
         )
-    table_ring = RingReduce(
-        wires,
-        place,
-        X,
-        lambda j: table_sums.at[j],
-        lambda j, h: table_sums.at[j, pl.ds(TABLE_CHUNKS // 2 * h, TABLE_CHUNKS // 2)],
-        TABLE_CHUNKS,
-        table_half,
-        table_whole,
-    )
-    rings = []
-    for phase, (half_in, whole_in) in enumerate(
-        ((half_c, whole_c), (half_b, whole_b), (half_a, whole_a))
-    ):
-        row = []
-        for part in range(3):
-            piece, half = block_ring(
-                place,
-                part,
-                phase,
-                lambda k3, first, count, part=part: sums.at[part, k3, pl.ds(first, count)],
+    first_rings, middle_rings, last_rings = [], [], []
+    for part in range(3):
+
+        def at(k3, first, count, part=part):
+            return sums.at[part, k3, pl.ds(first, count)]
+
+        last_axis, middle_axis, first_axis = ORDERS[part]
+        piece, half = block_ring(place, part, 2, at)
+        first_rings.append(
+            QuarterReduce(
+                wires, place, first_axis, piece, half, 32, half_a.at[part], whole_a.at[part]
             )
-            row.append(
-                RingReduce(
-                    wires,
-                    place,
-                    ORDERS[part][phase],
-                    piece,
-                    half,
-                    (2, 8, 32)[phase],
-                    half_in.at[part],
-                    whole_in.at[part],
-                )
+        )
+        piece, half = block_ring(place, part, 1, at)
+        middle_rings.append(
+            RingReduce(
+                wires, place, middle_axis, piece, half, 8, half_b.at[part], whole_b.at[part]
             )
-        rings.append(row)
+        )
+        piece, _ = block_ring(place, part, 0, at)
+        last_rings.append(DirectReduce(wires, place, last_axis, piece, 2, whole_c.at[part]))
     small_rings = [
         DirectReduce(wires, place, Z, lambda j: small_sums.at[j], 16, small_a),
         DirectReduce(
@@ -895,69 +1050,28 @@
         ),
     ]
 
-    for copy in swaps:
-        copy.wait_recv()
-    for ring in embed_first:
-        ring.start()
-    table_load.wait()
-    table_ring.start()
-
     def add_crossing(part, step):
         j = (third[part] + step) % SIDE
         block_loads[part, step].wait()
         crossings[part, step].wait_recv()
         add_blocks(sums.at[part, j], [sibling_in.at[part, j]], 32)
 
-    small_load.wait()
-    small_crossing.wait_recv()
-    for j in range(4):
-        add_blocks(small_sums.at[j], [small_sibling.at[j]], 16)
-    for ring, later in zip(embed_first, embed_second):
-        ring.finish()
-        later.start()
-    small_rings[0].start()
-    for part in range(3):
-        add_crossing(part, 2)
-        rings[2][part].start()
-    for ring in embed_second:
-        ring.forward()
-    for part in range(3):
-        add_crossing(part, 1)
-        add_crossing(part, 3)
     embed_siblings = []
-    for part in range(2):
-        k = place[embed_axes[part][1]]
-        for step in (0, 1, 3):
-            piece = embeds.at[part, core, (k + step) % SIDE]
-            embed_siblings.append(wires.send(piece, piece, sibling))
-    table_ring.forward()
-    for ring in rings[2]:
-        ring.forward()
-    for part in range(3):
-        add_crossing(part, 0)
-    for part in range(2):
-        embed_second[part].finish()
-        k = place[embed_axes[part][1]]
-        piece = embeds.at[part, core, (k + 2) % SIDE]
+
+    def share(part, step):
+        piece = embeds.at[part, core, (place[embed_axes[part][1]] + step) % SIDE]
         embed_siblings.append(wires.send(piece, piece, sibling))
-    ids_ring.finish()
-    small_rings[0].finish()
-    small_rings[1].start()
 
     rows = table_grad_ref.shape[0]
     chunk = rows // 4
     base = lax.axis_index("vocab") * rows
     row_iota = lax.broadcasted_iota(jnp.int32, (chunk, 512), 0)
 
-    @pl.loop(0, 4)
-    def _(index):
-        at = pl.ds(pl.multiple_of(index * chunk, chunk), chunk)
-        table_grad_ref[at] = jnp.zeros((chunk, width), jnp.float32)
-
-    def scatter_rows(part, at_core):
-        @pl.loop(0, 8)
-        def _(index):
-            at_far, pair = index // 2, index % 2
+    def scatter_rows(part, at_core, step):
+        at_far = (place[embed_axes[part][1]] + step) % SIDE
+
+        @pl.loop(0, 2)
+        def _(pair):
             values = embeds[part, at_core, at_far, pl.ds(4 * pair, 4)].reshape(512, width)
             ids = []
             for which in range(4):
@@ -973,65 +1087,15 @@
                 hot = jnp.where(row_iota + row * chunk == ids, 1.0, 0.0).astype(jnp.bfloat16)
                 table_grad_ref[at] += jnp.dot(hot, values, preferred_element_type=jnp.float32)
 
-    scatter_rows(0, core)
-    table_ring.arrive()
-    table_block = rows // TABLE_CHUNKS
-
-    @pl.loop(0, TABLE_CHUNKS)
-    def _(index):
-        at = pl.ds(pl.multiple_of(index * table_block, table_block), table_block)
-        table_grad_ref[at] += (
-            table_sums[across, index].astype(jnp.float32)
-            + table_whole[0, index].astype(jnp.float32)
-            + table_whole[1, index].astype(jnp.float32)
-        )
-
-    scatter_rows(1, core)
-    small_rings[1].finish()
-    small_rings[2].start()
-    for ring, later in zip(rings[2], rings[1]):
-        ring.finish()
-        later.start()
-    for copy in embed_siblings:
-        copy.wait_recv()
-    scatter_rows(0, 1 - core)
-    for ring in rings[1]:
-        ring.forward()
-    scatter_rows(1, 1 - core)
-    for ring, later in zip(rings[1], rings[0]):
-        ring.finish()
-        later.start()
-    small_rings[2].finish()
-    table_squares = jnp.zeros((1, width), jnp.float32)
-    for index in range(4):
-        values = table_grad_ref[index * chunk : (index + 1) * chunk]
-        table_squares += jnp.sum(values * values, 0, keepdims=True)
-    squares = table_squares[:, :128] + table_squares[:, 128:]
-    for ring in rings[0]:
-        ring.forward()
-    for part in range(3):
-        rings[0][part].arrive()
-        k1, k2, k3 = (place[axis] for axis in ORDERS[part])
-        for which in range(2):
-            total = sums[part, k3, 8 * k2 + 2 * k1 + which].astype(jnp.float32)
-            for side in range(2):
-                total += whole_c[part, side, which].astype(jnp.float32)
-            grads_out_ref[part, which] = total
-            squares += jnp.sum(total * total, 0, keepdims=True)
-    loss = sum(loss_ref[:, 128 * index : 128 * (index + 1)] for index in range(4))
-    own_small = small_sums[place[Z], 4 * place[Y] + across].astype(jnp.float32)
-    final_ref[0, core, place[Z], place[Y], across] = own_small[:8]
-    final_ref[1, core, across, place[Z], place[Y]] = jnp.concatenate(
-        [own_small[8:9], squares, loss, jnp.zeros((5, 128), jnp.float32)], 0
-    )
-    lead = [(0, core), (1, core)]
-    orders = (((X, Y, Z)), (Y, Z, X))
+    lead = ((0, core), (1, core))
+    orders = ((X, Y, Z), (Y, Z, X))
+    gathers = []
     for phase in range(3):
-        gathers = []
+        row = []
         for part in range(2):
-            first_axis, second_axis, third_axis = orders[part]
+            _, second_axis, third_axis = orders[part]
             keys = (place[third_axis], place[second_axis])[: 2 - phase]
-            gathers.append(
+            row.append(
                 DirectGather(
                     wires,
                     place,
@@ -1039,23 +1103,147 @@
                     lambda j, key=lead[part] + keys: final_ref.at[key + (j,)],
                 )
             )
-        for gather in gathers:
-            gather.start()
-        for gather in gathers:
-            gather.finish()
-    copies = []
+        gathers.append(row)
+
+    small_load.wait()
+    small_crossing.wait_recv()
+    for j in range(4):
+        add_blocks(small_sums.at[j], [small_sibling.at[j]], 16)
+    for part in range(3):
+        add_crossing(part, 2)
+        first_rings[part].start(0)
+    for copy in swaps:
+        copy.wait_recv()
+    for ring in embed_first:
+        ring.start()
+    small_rings[0].start()
+    for part in range(3):
+        add_crossing(part, 1)
+    for ring in embed_first:
+        ring.forward()
+    for part in range(3):
+        first_rings[part].start(1)
+    for ring, later in zip(embed_first, embed_second):
+        ring.finish()
+        later.start()
+    small_rings[0].finish()
+    small_rings[1].start()
+    share(0, 0)
+    share(1, 0)
+    for part in range(3):
+        add_crossing(part, 3)
+    ids_ring.finish()
+    for copy in table_loads:
+        copy.wait()
+
+    @pl.loop(0, rows // 80)
+    def _(index):
+        at = pl.ds(pl.multiple_of(index * 80, 80), 80)
+        total = table_parts[0, at].astype(jnp.float32)
+        for step in range(1, N_DP):
+            total += table_parts[step, at].astype(jnp.float32)
+        table_grad_ref[at] = total
+
+    scatter_rows(0, core, 0)
+    scatter_rows(1, core, 0)
+    for part in range(3):
+        add_crossing(part, 0)
+    for ring in first_rings:
+        ring.forward()
+    for copy in embed_siblings:
+        copy.wait_recv()
+    embed_siblings.clear()
+    scatter_rows(0, 1 - core, 0)
+    scatter_rows(1, 1 - core, 0)
     for part in range(2):
+        embed_second[part].forward()
+        share(part, 1)
+        share(part, 3)
+    small_rings[1].finish()
+    small_rings[2].start()
+    for part in range(2):
+        scatter_rows(part, core, 1)
+        scatter_rows(part, core, 3)
+    for copy in embed_siblings:
+        copy.wait_recv()
+    embed_siblings.clear()
+    for part in range(2):
+        scatter_rows(part, 1 - core, 1)
+        scatter_rows(part, 1 - core, 3)
+    small_rings[2].finish()
+    own_small = small_sums[place[Z], 4 * place[Y] + across].astype(jnp.float32)
+    final_ref[0, core, place[Z], place[Y], across] = own_small[:8]
+    final_ref[1, core, across, place[Z], place[Y]] = jnp.concatenate(
+        [own_small[8:9], jnp.zeros((7, 128), jnp.float32)], 0
+    )
+    wires.settle(17)
+    for ring, later in zip(first_rings, middle_rings):
+        ring.finish()
+        later.start()
+    for gather in gathers[0]:
+        gather.start()
+    for part in range(2):
+        embed_second[part].finish()
+        share(part, 2)
+    scatter_rows(0, core, 2)
+    for ring in middle_rings:
+        ring.forward()
+    for gather, later in zip(gathers[0], gathers[1]):
+        gather.finish()
+        later.start()
+    scatter_rows(1, core, 2)
+    for copy in embed_siblings:
+        copy.wait_recv()
+    scatter_rows(0, 1 - core, 2)
+    for ring, later in zip(middle_rings, last_rings):
+        ring.finish()
+        later.start()
+    for gather, later in zip(gathers[1], gathers[2]):
+        gather.finish()
+        later.start()
+    scatter_rows(1, 1 - core, 2)
+    table_squares = jnp.zeros((1, width), jnp.float32)
+    for index in range(4):
+        values = table_grad_ref[index * chunk : (index + 1) * chunk]
+        table_squares += jnp.sum(values * values, 0, keepdims=True)
+    squares = table_squares[:, :128] + table_squares[:, 128:]
+    for part in range(3):
+        last_rings[part].arrive()
+        k1, k2, k3 = (place[axis] for axis in ORDERS[part])
+        for which in range(2):
+            total = sums[part, k3, 8 * k2 + 2 * k1 + which].astype(jnp.float32)
+            for step in range(3):
+                total += whole_c[part, step, which].astype(jnp.float32)
+            grads_out_ref[part, which] = total
+            squares += jnp.sum(total * total, 0, keepdims=True)
+    final_siblings = []
+    for part in range(2):
+        gathers[2][part].finish()
         mine = final_ref.at[part, core]
-        copies.append(wires.send(mine, mine, sibling))
-    for copy in copies:
+        final_siblings.append(wires.send(mine, mine, sibling))
+    loss = sum(loss_ref[:, 128 * index : 128 * (index + 1)] for index in range(4))
+    totals = jnp.concatenate([squares, loss, jnp.zeros((6, 128), jnp.float32)], 0)
+    for phase, (own, others) in enumerate(
+        ((2 * across + core, line), (SIDE * place[Z] + place[Y], plane))
+    ):
+        mine = totals_all.at[phase, own]
+        mine[...] = totals
+        bundle = wires.slot()
+        for other in others:
+            wires.send_all(mine, mine, other, bundle)
+        wires.whole(totals_all.at[phase, pl.ds(0, len(others))], sibling, bundle).wait()
+        totals = totals_all[phase, 0]
+        for index in range(1, len(others) + 1):
+            totals += totals_all[phase, index]
+    totals_ref[...] = totals
+    for copy in final_siblings:
         copy.wait_recv()
-    wires.drain()
-
-
-def finish_call(grads, small, head_grad, d_embed, token_ids, loss_row):
+    wires.settle()
+
+
+def finish_call(grads, small, head_grads, d_embed, token_ids, loss_row):
     bf16 = jnp.bfloat16
-    groups, chunks, chunk_rows, width = head_grad.shape
-    rows = chunks * chunk_rows
+    rows, width = head_grads[0].shape
     block = (BLOCK, BLOCK)
     return pl.pallas_call(
         finish_kernel,
@@ -1064,9 +1252,10 @@
             jax.ShapeDtypeStruct((3, 2) + block, jnp.float32),
             jax.ShapeDtypeStruct((rows, width), jnp.float32),
             jax.ShapeDtypeStruct((2, 2, SIDE, SIDE, SIDE, 8, 128), jnp.float32),
+            jax.ShapeDtypeStruct((8, 128), jnp.float32),
         ),
-        in_specs=[ANY, ANY, ANY, VMEM, VMEM, VMEM],
-        out_specs=(VMEM,) * 3,
+        in_specs=[ANY] * 6 + [VMEM] * 3,
+        out_specs=(VMEM,) * 4,
         scratch_shapes=[
             pltpu.VMEM((3, SIDE, 32) + block, bf16),
             pltpu.VMEM((3, SIDE, 32) + block, bf16),
@@ -1074,26 +1263,24 @@
             pltpu.VMEM((3, 2, 32) + block, bf16),
             pltpu.VMEM((3, 2, 4) + block, bf16),
             pltpu.VMEM((3, 2, 8) + block, bf16),
-            pltpu.VMEM((3, 2, 1) + block, bf16),
-            pltpu.VMEM((3, 2, 2) + block, bf16),
+            pltpu.VMEM((3, 3, 2) + block, bf16),
             pltpu.VMEM((SIDE, 16, 16, 128), bf16),
             pltpu.VMEM((SIDE, 16, 16, 128), bf16),
             pltpu.VMEM((3, 16, 16, 128), bf16),
             pltpu.VMEM((3, 4, 16, 128), bf16),
             pltpu.VMEM((3, 1, 16, 128), bf16),
-            pltpu.VMEM(head_grad.shape, bf16),
-            pltpu.VMEM((2, chunks // 2, chunk_rows, width), bf16),
-            pltpu.VMEM((2, chunks, chunk_rows, width), bf16),
+            pltpu.VMEM((N_DP, rows, width), bf16),
             pltpu.VMEM((2, 2, SIDE, 8, 128, width), bf16),
             pltpu.VMEM((N_DP,) + token_ids.shape, jnp.int32),
-            pltpu.SemaphoreType.DMA((128,)),
-            pltpu.SemaphoreType.DMA((128,)),
-            pltpu.SemaphoreType.DMA((14,)),
+            pltpu.VMEM((2, SIDE * SIDE, 8, 128), jnp.float32),
+            pltpu.SemaphoreType.DMA((160,)),
+            pltpu.SemaphoreType.DMA((160,)),
+            pltpu.SemaphoreType.DMA((17,)),
         ],
         compiler_params=pltpu.CompilerParams(
-            collective_id=3, has_side_effects=True, vmem_limit_bytes=63 << 20
+            collective_id=3, has_side_effects=True, vmem_limit_bytes=VMEM_BYTES
         ),
-    )(grads, small, head_grad, d_embed, token_ids, loss_row)
+    )(grads, small, *head_grads, d_embed, token_ids, loss_row)
 
 
 def row_mean(values):
@@ -1111,10 +1298,6 @@
     d_values = scale * (d_hat - row_mean(d_hat) - hat * row_mean(d_hat * hat))
     d_gain = jnp.sum(d_normed * hat, 0, keepdims=True)
     return d_values, d_gain, jnp.sum(d_normed, 0, keepdims=True)
-
-
-def lane_range(first, count):
-    return pl.ds(pl.multiple_of(first, 128), count)
 
 
 QKV, PROJ, FC, OUT = (0, 24), (192, 8), (256, 32), (512, 8)
@@ -1147,8 +1330,8 @@
     )
 
 
-def selected_rows(ref, at_ref, count):
-    return jnp.concatenate([ref[pl.ds(at_ref[i], 1), :] for i in range(count)], 0)
+def selected_rows(ref, positions):
+    return jnp.concatenate([ref[pl.ds(position, 1), :] for position in positions], 0)
 
 
 def pair_masks(count):
@@ -1190,10 +1373,13 @@
     copies = load_blocks(full_ref, blocks, sems)
     count = head_in_ref.shape[0]
     bf16 = jnp.bfloat16
+    own = lax.axis_index("vocab")
+    positions = [at_ref[i, own] for i in range(count)]
+    length = length_ref[own]
     hat, _ = normalized(hidden_ref[...])
     normed_rows[...] = hat * vec_ref[0:1] + vec_ref[1:2]
     normed_one = normed_rows[...].astype(bf16)
-    normed_own = selected_rows(normed_rows, at_ref, count).astype(bf16)
+    normed_own = selected_rows(normed_rows, positions).astype(bf16)
     for copy in copies:
         copy.wait()
 
@@ -1225,7 +1411,7 @@
     key = lax.broadcasted_iota(jnp.int32, (count, seq_len), 1)
     last_key = jnp.zeros((count, seq_len), jnp.int32)
     for i in range(count):
-        last_key = jnp.where(row == i, jnp.minimum(at_ref[i], length_ref[0] - 1), last_key)
+        last_key = jnp.where(row == i, jnp.minimum(positions[i], length - 1), last_key)
     allowed = jnp.concatenate([key <= last_key] * 2, 0)
     for pair in range(pairs):
         lanes = slice(128 * pair, 128 * pair + 128)
@@ -1243,7 +1429,7 @@
         attended_ref[:, lanes] = folded(mixed, count).astype(bf16)
 
     attended = attended_ref[...]
-    middle_ref[...] = selected_rows(hidden_ref, at_ref, count) + vec_ref[4:5]
+    middle_ref[...] = selected_rows(hidden_ref, positions) + vec_ref[4:5]
 
     @pl.loop(0, 4)
     def _(tile):
@@ -1281,7 +1467,7 @@
     head_in_ref[...] = (hat * vec_ref[12:13] + vec_ref[13:14]).astype(bf16)
 
 
-def forward_call(where, positions, length, full, hidden, vectors):
+def forward_call(where, positions, lengths, full, hidden, vectors):
     count = positions.shape[0]
     seq_len = hidden.shape[0]
     bf16 = jnp.bfloat16
@@ -1311,8 +1497,8 @@
                 pltpu.SemaphoreType.DMA((8,)),
             ],
         ),
-        compiler_params=pltpu.CompilerParams(vmem_limit_bytes=48 << 20),
-    )(where, positions, length, full, hidden, vectors)
+        compiler_params=pltpu.CompilerParams(vmem_limit_bytes=VMEM_BYTES),
+    )(where, positions, lengths, full, hidden, vectors)
 
 
 def gelu_slope(values):
@@ -1354,18 +1540,23 @@
     copies = load_blocks(full_ref, blocks, sems)
     count = d_head_ref.shape[0]
     bf16 = jnp.bfloat16
-
-    def weight_grad(matrix, rows, left_ref, right):
+    own = lax.axis_index("vocab")
+    positions = [at_ref[i, own] for i in range(count)]
+
+    def weight_grad(matrix, rows, left_ref, right, together=4):
         first, in_row = matrix
 
-        @pl.loop(0, rows)
-        def _(row):
-            left = left_ref[:, lane_range(128 * row, 128)]
+        @pl.loop(0, rows // together)
+        def _(group):
+            left = left_ref[:, lane_range(128 * together * group, 128 * together)]
             for column in range(0, in_row, 2):
                 product = dot_tn(left, right[:, 128 * column : 128 * column + 256]).astype(bf16)
-                for side in range(2):
-                    index = first + row * in_row + column + side
-                    grad_blocks[index] = product[:, 128 * side : 128 * side + 128]
+                for inner in range(2 * together):
+                    row, side = inner // 2, inner % 2
+                    index = first + (group * together + row) * in_row + column + side
+                    grad_blocks[index] = product[
+                        128 * row : 128 * row + 128, 128 * side : 128 * side + 128
+                    ]
                     pltpu.make_async_copy(
                         grad_blocks.at[index], grads_ref.at[where_ref[index]], grad_sem
                     ).start()
@@ -1437,7 +1628,7 @@
         d_qkv[:, D + 128 * pair : D + 128 * pair + 128] = d_keys.astype(bf16)
         d_qkv[:, 2 * D + 128 * pair : 2 * D + 128 * pair + 128] = d_values
     for i in range(count):
-        spread[pl.ds(at_ref[i], 1), :] = query_grads[i : i + 1, :]
+        spread[pl.ds(positions[i], 1), :] = query_grads[i : i + 1, :]
     d_qkv[:, :D] = spread[...].astype(bf16)
     hat, scale = normalized(hidden_ref[...])
     normed[...] = (hat * vec_ref[0:1] + vec_ref[1:2]).astype(bf16)
@@ -1457,7 +1648,7 @@
     )
     rows_out[...] = d_hidden
     for i in range(count):
-        rows_out[pl.ds(at_ref[i], 1), :] += d_middle[i : i + 1]
+        rows_out[pl.ds(positions[i], 1), :] += d_middle[i : i + 1]
     d_embed_ref[...] = rows_out[...].astype(bf16)
     vec_rows = vec_ref.shape[0]
     for index in range(small_ref.shape[0]):
@@ -1507,8 +1698,160 @@
                 pltpu.SemaphoreType.DMA,
             ],
         ),
-        compiler_params=pltpu.CompilerParams(vmem_limit_bytes=62 << 20),
+        compiler_params=pltpu.CompilerParams(vmem_limit_bytes=VMEM_BYTES),
     )(where, positions, full, hidden, vectors, *cache, d_head)
+
+
+def adam_step(weight, moment_one, moment_two, grad_in, rate, decay):
+    new_one = BETA_ONE * moment_one + (1.0 - BETA_ONE) * grad_in
+    new_two = BETA_TWO * moment_two + (1.0 - BETA_TWO) * grad_in * grad_in
+    hat_one = new_one * (1.0 / (1.0 - BETA_ONE**STEP))
+    hat_two = new_two * (1.0 / (1.0 - BETA_TWO**STEP))
+    change = hat_one / (jnp.sqrt(hat_two) + ADAM_EPS)
+    if decay:
+        change = change + decay * weight
+    return weight - rate * change, new_one, new_two
+
+
+def high_dot(left, right, contract=((1,), (0,))):
+    return lax.dot_general(
+        left, right, (contract, ((), ())), precision=HIGH, preferred_element_type=jnp.float32
+    )
+
+
+def update_kernel(*refs):
+    names = 18
+    sources, targets = refs[:names], refs[names : names + 14]
+    buffers = refs[names + 14 : names + 14 + names]
+    results = refs[names + 14 + names : names + 28 + names]
+    vec_grad, load_sems, store_sems = refs[names + 28 + names :]
+    loads = [
+        pltpu.make_async_copy(source, buffer, load_sems.at[index])
+        for index, (source, buffer) in enumerate(zip(sources, buffers))
+    ]
+    for copy in loads:
+        copy.start()
+    stores = []
+
+    def store(index, at=None):
+        source, target = results[index], targets[index]
+        if at is not None:
+            source, target = source.at[at], target.at[at]
+        copy = pltpu.make_async_copy(source, target, store_sems.at[len(stores)])
+        copy.start()
+        stores.append(copy)
+
+    totals, final, grads, matrices, left_stats, right_stats, left_roots, right_roots = buffers[:8]
+    table_grad, table, table_m, table_v = buffers[8:12]
+    positions, pos_m, pos_v, vectors, vectors_m, vectors_v = buffers[12:]
+    scalars, matrices_new, left_new, right_new, matrices_grad = results[:5]
+    for copy in loads[:2]:
+        copy.wait()
+    row_squares = jnp.zeros((8, 128), jnp.float32)
+    for part in range(2):
+        for core in range(2):
+            values = final[part, core].reshape(SIDE**3, 8, 128)
+            row_squares += jnp.sum(values * values, 0)
+    squares = jnp.sum(totals[0:1]) + jnp.sum(row_squares)
+    loss = jnp.sum(totals[1:2])
+    norm = jnp.sqrt(jnp.full((1, 128), squares, jnp.float32))
+    clip = CLIP_LEVEL / jnp.maximum(norm, CLIP_LEVEL)
+    scalars[...] = jnp.concatenate(
+        [jnp.full((1, 128), loss, jnp.float32), norm, jnp.zeros((6, 128), jnp.float32)], 0
+    )
+    store(0)
+    for copy in loads[2:8]:
+        copy.wait()
+
+    @pl.loop(0, SLOTS, unroll=3)
+    def _(slot):
+        grad = grads[slot // 2, slot % 2] * clip
+        matrices_grad[slot] = grad
+        left_new[slot] = STAT_DECAY * left_stats[slot] + (1.0 - STAT_DECAY) * high_dot(
+            grad, grad, ((1,), (1,))
+        )
+        right_new[slot] = STAT_DECAY * right_stats[slot] + (1.0 - STAT_DECAY) * high_dot(
+            grad, grad, ((0,), (0,))
+        )
+        stepped = high_dot(high_dot(left_roots[slot], grad), right_roots[slot])
+        weight = matrices[slot]
+        matrices_new[slot] = weight - SHAMPOO_RATE * (stepped + DECAY_RATE * weight)
+
+    for index in range(1, 5):
+        store(index)
+    for copy in loads[8:12]:
+        copy.wait()
+    rows, width = table.shape
+    wide_clip = jnp.concatenate([clip] * (width // 128), 1)
+    chunk = rows // 4
+    for index in range(4):
+
+        @pl.loop(0, chunk // 80)
+        def _(inner):
+            at = pl.ds(pl.multiple_of(index * chunk + inner * 80, 80), 80)
+            grad = table_grad[at] * wide_clip
+            stepped = adam_step(
+                table[at], table_m[at], table_v[at], grad, TABLE_RATE, DECAY_RATE
+            )
+            for order, value in enumerate(stepped):
+                results[5 + order][at] = value
+
+        for order in range(3):
+            store(5 + order, pl.ds(index * chunk, chunk))
+    for copy in loads[12:]:
+        copy.wait()
+    tiles = D // 128
+    for index in range(N_DP * N_VOCAB):
+        at_core, rest = index // 64, index % 64
+        at_z, at_y, at_x = rest // 16, rest // 4 % 4, rest % 4
+        group, lanes = index // tiles, slice(128 * (index % tiles), 128 * (index % tiles) + 128)
+        at = slice(8 * group, 8 * group + 8)
+        stepped = adam_step(
+            positions[at, lanes],
+            pos_m[at, lanes],
+            pos_v[at, lanes],
+            final[0, at_core, at_z, at_y, at_x] * clip,
+            POS_RATE,
+            DECAY_RATE,
+        )
+        for order, value in enumerate(stepped):
+            results[8 + order][at, lanes] = value
+        if group < vectors.shape[0]:
+            vec_grad[group : group + 1, lanes] = (
+                final[1, at_core, at_x, at_z, at_y, 0:1] * clip
+            )
+    for index in range(8, 11):
+        store(index)
+    stepped = adam_step(
+        vectors[...], vectors_m[...], vectors_v[...], vec_grad[...], VECTOR_RATE, 0.0
+    )
+    for order, value in enumerate(stepped):
+        results[11 + order][...] = value
+        store(11 + order)
+    for copy in stores:
+        copy.wait()
+
+
+def update_call(totals, final, grads, blocks, table_grad, table, positions, vectors):
+    sources = [totals, final, grads, *blocks, table_grad, *table, *positions, *vectors]
+    shape = lambda array: jax.ShapeDtypeStruct(array.shape, jnp.float32)
+    targets = [shape(totals)] + [shape(blocks[0])] * 4
+    targets += [shape(array) for array in (*table, *positions, *vectors)]
+    return pl.pallas_call(
+        update_kernel,
+        name="optimizer_update",
+        out_shape=tuple(targets),
+        in_specs=[ANY] * len(sources),
+        out_specs=(ANY,) * len(targets),
+        scratch_shapes=[pltpu.VMEM(array.shape, jnp.float32) for array in sources]
+        + [pltpu.VMEM(target.shape, jnp.float32) for target in targets]
+        + [
+            pltpu.VMEM(vectors[0].shape, jnp.float32),
+            pltpu.SemaphoreType.DMA((len(sources),)),
+            pltpu.SemaphoreType.DMA((len(targets) + 9,)),
+        ],
+        compiler_params=pltpu.CompilerParams(vmem_limit_bytes=VMEM_BYTES),
+    )(*sources)
 
 
 def slot_places():
@@ -1547,7 +1890,6 @@
     vectors_m,
     vectors_v,
 ):
-    vocab_index = lax.axis_index("vocab")
     slots = block_of_slot.shape[0]
     block_iota = jnp.arange(slots, dtype=jnp.int32)
     where = jnp.sum(
@@ -1555,72 +1897,41 @@
         1,
         dtype=jnp.int32,
     )
-    own_blocks = matrices.astype(jnp.bfloat16).reshape(3, 2, BLOCK, BLOCK)
-    table_low = vocab_table.astype(jnp.bfloat16)
-    full, table_full, hidden = start_call(token_ids, own_blocks, table_low, positions_table)
+    full, table_full, hidden = start_call(token_ids, matrices, vocab_table, positions_table)
     full_blocks = full.reshape(slots, BLOCK, BLOCK)
-    own_length = lax.dynamic_index_in_dim(seq_lengths, vocab_index)
-    own_positions = lax.dynamic_index_in_dim(loss_positions, vocab_index, keepdims=False)
-    counted = (loss_positions < seq_lengths[:, None]).astype(jnp.float32).reshape(1, -1)
-    head_in, *cache = forward_call(where, own_positions, own_length, full_blocks, hidden, vectors)
-    d_head_in, head_grad, loss_row = head_call(
-        head_in, table_full, target_ids.reshape(1, -1), counted
-    )
+    positions = loss_positions.T
+    head_in, *cache = forward_call(
+        where, positions, seq_lengths, full_blocks, hidden, vectors
+    )
+    d_head_in, *head_grads, loss_row = head_call(
+        head_in, table_full, target_ids.T, positions, seq_lengths.reshape(1, -1)
+    )
+    for step in range(1, N_DP):
+        head_grads[step] = lax.ppermute(
+            head_grads[step], "dp", [(i, (i + step) % N_DP) for i in range(N_DP)]
+        )
     grad_blocks, small, d_embed = backward_call(
-        where, own_positions, full_blocks, hidden, vectors, cache, d_head_in
-    )
-    owned_grads, table_grad_own, final = finish_call(
+        where, positions, full_blocks, hidden, vectors, cache, d_head_in
+    )
+    owned_grads, table_grad_own, final, totals = finish_call(
         grad_blocks.reshape(full.shape[:3] + (32, BLOCK, BLOCK)),
         small.reshape(2, SIDE, 16, 16, 128),
-        head_grad,
+        head_grads,
         d_embed,
         token_ids,
         loss_row,
     )
-    owned_grads = owned_grads.reshape(SLOTS, BLOCK, BLOCK)
-    pos_grad = final[0].reshape(16, 8, 8, 128).transpose(0, 2, 1, 3).reshape(positions_table.shape)
-    rest = final[1].transpose(0, 2, 3, 1, 4, 5).reshape(N_DP * N_VOCAB, 8, 128)
-    vec_sum = rest[: 8 * vectors.shape[0], 0].reshape(vectors.shape)
-    squares_all = jnp.sum(rest[:, 1])
-    loss_value = jnp.sum(rest[:, 2])
-    grad_norm = jnp.sqrt(squares_all + jnp.sum(pos_grad * pos_grad) + jnp.sum(vec_sum * vec_sum))
-    clip_factor = CLIP_LEVEL / jnp.maximum(grad_norm, CLIP_LEVEL)
-    matrices_grad = owned_grads * clip_factor
-    left_new = STAT_DECAY * left_stats + (1.0 - STAT_DECAY) * jnp.einsum(
-        "bij,bkj->bik", matrices_grad, matrices_grad, precision=HIGH
-    )
-    right_new = STAT_DECAY * right_stats + (1.0 - STAT_DECAY) * jnp.einsum(
-        "bji,bjk->bik", matrices_grad, matrices_grad, precision=HIGH
-    )
-    left_part = jnp.einsum("bij,bjk->bik", left_roots, matrices_grad, precision=HIGH)
-    precond = jnp.einsum("bij,bjk->bik", left_part, right_roots, precision=HIGH)
-    matrices_new = matrices - SHAMPOO_RATE * (precond + DECAY_RATE * matrices)
-    table_new, table_m_new, table_v_new = adamw(
-        vocab_table, table_m, table_v, table_grad_own * clip_factor, TABLE_RATE, DECAY_RATE
-    )
-    positions_new, pos_m_new, pos_v_new = adamw(
-        positions_table, pos_m, pos_v, pos_grad * clip_factor, POS_RATE, DECAY_RATE
-    )
-    vectors_new, vectors_m_new, vectors_v_new = adamw(
-        vectors, vectors_m, vectors_v, vec_sum * clip_factor, VECTOR_RATE, 0.0
-    )
-    return (
-        loss_value,
-        grad_norm,
-        matrices_new,
-        left_new,
-        right_new,
-        matrices_grad,
-        table_new,
-        table_m_new,
-        table_v_new,
-        positions_new,
-        pos_m_new,
-        pos_v_new,
-        vectors_new,
-        vectors_m_new,
-        vectors_v_new,
-    )
+    scalars, *updated = update_call(
+        totals,
+        final,
+        owned_grads,
+        (matrices, left_stats, right_stats, left_roots, right_roots),
+        table_grad_own,
+        (vocab_table, table_m, table_v),
+        (positions_table, pos_m, pos_v),
+        (vectors, vectors_m, vectors_v),
+    )
+    return (scalars[0, 0], scalars[1, 0], *updated)
 
 
 def solution(mesh):

time: 374 us -> 312 us (0.83)
  Pallas kernels: 338 us -> 303 us
  other arithmetic: 14.9 us -> 1.61 us
  local copies, waits for them, and re-layouts: 11.8 us -> 2.14 us
  matrix products: 5.06 us -> 0 us
    pallas_call x1, Pallas kernels: 114 us -> 94.3 us  [start_call(): pl.pallas_call(start_kernel, name='gather_and_look_up', out_shape=(jax.Sh...]
    pallas_call x1, Pallas kernels: 121 us -> 103 us  [finish_call(): pl.pallas_call(finish_kernel, name='reduce_and_scatter', out_shape=(jax.S...]
    pallas_call x0 -> x1, Pallas kernels: none -> 8.59 us  [update_call(): pl.pallas_call(update_kernel, name='optimizer_update', out_shape=tuple(ta...]
    unnamed x61 -> x2, local copies, waits for them, and re-layouts: 8.2 us -> 0.86 us
    sub x3 -> x0, other arithmetic: 5.25 us -> none  [adamw(): weight - rate * (hat_one / (jnp.sqrt(hat_two) + ADAM_EPS) + decay * weight)]
    dot_general x4 -> x0, matrix products: 5.06 us -> none  [the longest x1 1.68 us: per_device(): jnp.einsum('bij,bkj->bik', matrices_grad, matrices_grad, precision=HIGH)]
    convert_element_type x2 -> x0, other arithmetic: 4.13 us -> none  [the longest x1 2.43 us: per_device(): table_low = vocab_table.astype(jnp.bfloat16)]
  transfers between devices with their start and end apart: 0 -> 3, of which waited for: 0 -> 0; matrix products, arithmetic and copies ran while one was open for 0% -> 0% of each run, Pallas kernels for 0% -> 12%
where the time goes in v2:
time: 312 us; the launch traced here: 311 us
  Pallas kernels  303 us (97%)
  starting transfers between devices  3.36 us (1%)
    pallas_call x1, Pallas kernels, finish_call(): pl.pallas_call(finish_kernel, name='reduce_and_scatter', out_shape=(jax.S...  103 us
    pallas_call x1, Pallas kernels, start_call(): pl.pallas_call(start_kernel, name='gather_and_look_up', out_shape=(jax.Sh...  94.3 us
    pallas_call x1, Pallas kernels, head_call(): pl.pallas_call(head_kernel, name='head', out_shape=(jax.ShapeDtypeStruct(...  37.6 us
    pallas_call x1, Pallas kernels, backward_call(): pl.pallas_call(backward_kernel, name='layer_backward', out_shape=(shape(f...  36.5 us
    pallas_call x1, Pallas kernels, forward_call(): pl.pallas_call(forward_kernel, name='layer_forward', out_shape=(shape((co...  23.5 us
    pallas_call x1, Pallas kernels, update_call(): pl.pallas_call(update_kernel, name='optimizer_update', out_shape=tuple(ta...  8.59 us
  transfers between devices with their start and end apart: 3, of which 0 were waited for; matrix products, arithmetic and copies ran while one was open for 0% of the time, Pallas kernels for 12%

profile of v2, /device:TPU:1, one launch (start us, length us, event | category | flops | bytes accessed | tf_op | source)
XLA Modules:
  0.0 311.3 jit_solution(7020169128726260507)
XLA Ops:
  0.6 1.6 select_reduce_fusion.where_ref
  2.3 94.3 %gather_and_look_up.1 = (bf16[3,2,4,32,128,128]{5,4,3,2,1,0:T(8,128)(2,1)}, bf16[4,1600,256]{2,1,0:T(8,128)(2,1)}, f32[128,1024]{1,0:T(8,128)}) custom-call(s32[32,128]{1,0:T(8,128)} %ids_ref.3, f32[6,128,128]{2,1,0:T(8,128)} %refs_3_.1, f32[1600,256]{1,0:T(8,128)} %refs_9_.1, f32[128,1024]{1,0:T(8,128)} %refs_12_.1), custom_call_target="tpu_custom_call" | custom-call | tf_op jit(solution)/shard_map/gather_and_look_up/pallas_call | solution.py:589
  96.6 23.5 %layer_forward.1 = (bf16[16,1024]{1,0:T(8,128)(2,1)}, bf16[16,1024]{1,0:T(8,128)(2,1)}, bf16[128,2048]{1,0:T(8,128)(2,1)}, f32[256,128]{1,0:T(8,128)}, bf16[16,1...) custom-call(s32[768]{0:T(1024)} %select_reduce_fusion.where_ref, ...), custom_call_target="tpu_custom_call" | custom-call | tf_op jit(solution)/shard_map/layer_forward/pallas_call | solution.py:1475
  120.1 37.6 %head.1 = (f32[16,1024]{1,0:T(8,128)}, bf16[1600,256]{1,0:T(8,128)(2,1)}, bf16[1600,256]{1,0:T(8,128)(2,1)}, bf16[1600,256]{1,0:T(8,128)(2,1)}, bf16[1600,256]{1,0:T(8,128)(2,1)}, /*index=5*/f32[1,512]{1,0:T(1,128)}) custom-call(bf16[16,1024]{1,0:T(8,128)(2,1)} %get-tuple-element.62.head_in_ref, bf16[4,1600,256]{2,1,0:T(8,128)(2,1)} %get-tuple-element.63.table_ref, ...), custom_call_target="tpu_custom_call" | custom-call | tf_op jit(solution)/shard_map/head/pallas_call | solution.py:876
  157.7 0.1 collective-permute-start
  157.8 1.7 collective-permute-start.1
  159.5 1.6 collective-permute-start.2
  161.1 36.5 %layer_backward.1 = (bf16[768,128,128]{2,1,0:T(8,128)(2,1)}, bf16[128,16,128]{2,1,0:T(8,128)(2,1)}, bf16[128,1024]{1,0:T(8,128)(2,1)}) custom-call(s32[768]{0:T(1024)} %select_reduce_fusion.where_ref, s32[16,32]{1,0:T(8,128)} %bitcast.14, bf16[768,128,128]{2,1,0:T(8,128)(2,1)} %bitcast.9, f32[128,1024]{1,0:T(8,128)} %get-tuple-element.54.hidden_ref, ...), custom_call_target="tpu_custom_call" | custom-call | tf_op jit(solution)/shard_map/layer_backward/pallas_call | solution.py:1673
  197.5 0.0 collective-permute-done.next_grad_ref
  197.5 0.0 copy-start
  197.6 0.0 collective-permute-done.1.far_grad_ref
  197.6 0.0 collective-permute-done.2.last_grad_ref
  197.6 0.9 copy-done
  198.4 103.0 %reduce_and_scatter.1 = (f32[3,2,128,128]{3,2,1,0:T(8,128)}, f32[1600,256]{1,0:T(8,128)}, f32[2,2,4,4,4,8,128]{6,5,4,3,2,1,0:T(8,128)}, f32[8,128]{1,0:T(8,128)}) custom-call(bf16[3,2,4,32,128,128]{5,4,3,2,1,0:T(8,128)(2,1)} %bitcast.10, bf16[2,4,16,16,128]{4,3,2,1,0:T(8,128)(2,1)} %bitcast.11, bf16[1600,256]{1,0:T(8,128)(2,1)} %get-tuple-element.67.own_grad_ref, ...), custom_call_target="tpu_custom_call" | custom-call | tf_op jit(solution)/shard_map/reduce_and_scatter/pallas_call | solution.py:1248
  301.4 8.6 %optimizer_update.1 = (f32[8,128]{1,0:T(8,128)}, f32[6,128,128]{2,1,0:T(8,128)}, f32[6,128,128]{2,1,0:T(8,128)}, f32[6,128,128]{2,1,0:T(8,128)}, f32[6,128,128]{...) custom-call(f32[8,128]{1,0:T(8,128)} %get-tuple-element.73.refs_0_, ...), custom_call_target="tpu_custom_call" | custom-call | tf_op jit(solution)/shard_map/optimizer_update/pallas_call | solution.py:1840
  310.0 1.3 fusion
Async XLA Ops:
  157.7 39.8 %collective-permute-start = (bf16[1600,256]{1,0:T(8,128)(2,1)}, bf16[1600,256]{1,0:T(8,128)(2,1)S(1)}, u32[]{:S(2)}, u32[]{:S(2)}) collective-permute-start(bf16[1600,256]{1,0:T(8,128)(2,1)} %get-tuple-element.68), channel_id=1, source_target_pairs={{0,32},{32,64},{64,96},{96,0},{1,33},{33,65},{65,97},{97,1},{2,34}... | collective-permute-start | bytes 2457608 | tf_op jit(solution)/shard_map/ppermute | solution.py:1910
  157.8 39.8 %collective-permute-start.1 = (bf16[1600,256]{1,0:T(8,128)(2,1)}, bf16[1600,256]{1,0:T(8,128)(2,1)}, u32[]{:S(2)}, u32[]{:S(2)}) collective-permute-start(bf16[1600,256]{1,0:T(8,128)(2,1)} %get-tuple-element.69), channel_id=1, source_target_pairs={{0,64},{32,96},{64,0},{96,32},{1,65},{33,97},{65,1},{97,33},{2,66}... | collective-permute-start | bytes 2457608 | tf_op jit(solution)/shard_map/ppermute | solution.py:1910
  159.5 38.1 %collective-permute-start.2 = (bf16[1600,256]{1,0:T(8,128)(2,1)}, bf16[1600,256]{1,0:T(8,128)(2,1)}, u32[]{:S(2)}, u32[]{:S(2)}) collective-permute-start(bf16[1600,256]{1,0:T(8,128)(2,1)} %get-tuple-element.70), channel_id=1, source_target_pairs={{0,96},{32,0},{64,32},{96,64},{1,97},{33,1},{65,33},{97,65},{2,98}... | collective-permute-start | bytes 2457608 | tf_op jit(solution)/shard_map/ppermute | solution.py:1910
  197.5 0.9 copy-start

commit v3 on v2

--- a/solution.py
+++ b/solution.py
@@ -49,6 +49,7 @@
 
 
 VMEM_BYTES = 63 << 20
+TABLE_CHUNKS = 20
 MESH_IDS = pl.DeviceIdType.MESH
 ANY = pl.BlockSpec(memory_space=pl.ANY)
 VMEM = pl.BlockSpec(memory_space=pltpu.VMEM)
@@ -82,16 +83,17 @@
 
 
 def greet(others):
-    barrier = pltpu.get_barrier_semaphore()
     for other in others:
         pl.semaphore_signal(
-            barrier, inc=1, device_id=device_of(other), device_id_type=MESH_IDS
-        )
-    pl.semaphore_wait(barrier, len(others))
-
-
-def lane_range(first, count):
-    return pl.ds(pl.multiple_of(first, 128), count)
+            pltpu.get_barrier_semaphore(),
+            inc=1,
+            device_id=device_of(other),
+            device_id_type=MESH_IDS,
+        )
+
+
+def await_greetings(others):
+    pl.semaphore_wait(pltpu.get_barrier_semaphore(), len(others))
 
 
 class Wires:
@@ -134,13 +136,18 @@
         self.sent = self.sent[done:]
 
 
+def lane_range(first, count):
+    return pl.ds(pl.multiple_of(first, 128), count)
+
+
 def add_blocks(target, sources, count):
     @pl.loop(0, count)
     def _(i):
-        total = target[i].astype(jnp.float32)
+        at = i if len(target.shape) == 3 else lane_range(128 * i, 128)
+        total = target[at].astype(jnp.float32)
         for source in sources:
-            total += source[i].astype(jnp.float32)
-        target[i] = total.astype(target.dtype)
+            total += source[at].astype(jnp.float32)
+        target[at] = total.astype(target.dtype)
 
 
 class RingGather:
@@ -293,28 +300,41 @@
         size = self.count // 4
         landing = pl.ds(chunk * size, size)
         if chunk == 0:
-            self.far_ups, self.far_downs = [], []
+            self.far_ups, self.far_downs, self.wholes = [], [], []
         self.far_ups.append(
-            self.wires.send(self.half(far, chunk), self.half_in.at[0, landing], up)
+            self.wires.send(self.half(far, 2 * chunk), self.half_in.at[0, landing], up)
         )
         self.far_downs.append(
-            self.wires.send(self.half(far, 2 + chunk), self.half_in.at[1, landing], down)
-        )
+            self.wires.send(self.half(far, 2 * chunk + 1), self.half_in.at[1, landing], down)
+        )
+
+    def send_quarter(self, piece, quarter, side):
+        size = self.count // 4
+        landing = self.whole_in.at[side, pl.ds(quarter * size, size)]
+        there = moved(self.place, self.axis, 1 if side == 0 else -1)
+        self.wholes.append(self.wires.send(self.half(piece, quarter), landing, there))
+
+    def start_near(self):
+        after, before = (self.mine + 1) % SIDE, (self.mine + 3) % SIDE
+        for quarter in (0, 2):
+            self.send_quarter(after, quarter + 1, 0)
+            self.send_quarter(before, quarter, 1)
 
     def forward(self):
         after, before = (self.mine + 1) % SIDE, (self.mine + 3) % SIDE
-        up, down = moved(self.place, self.axis, 1), moved(self.place, self.axis, -1)
         size = self.count // 4
-        for chunk, copy in enumerate(self.far_ups):
+        for chunk in range(2):
+            landed = pl.ds(chunk * size, size)
+            self.far_ups[chunk].wait_recv()
+            add_blocks(self.half(after, 2 * chunk), [self.half_in.at[0, landed]], size)
+            self.send_quarter(after, 2 * chunk, 0)
+            self.far_downs[chunk].wait_recv()
+            add_blocks(self.half(before, 2 * chunk + 1), [self.half_in.at[1, landed]], size)
+            self.send_quarter(before, 2 * chunk + 1, 1)
+
+    def arrive(self):
+        for copy in self.wholes:
             copy.wait_recv()
-            landed = self.half_in.at[0, pl.ds(chunk * size, size)]
-            add_blocks(self.half(after, chunk), [landed], size)
-        self.up = self.wires.send(self.piece(after), self.whole_in.at[0], up)
-        for chunk, copy in enumerate(self.far_downs):
-            copy.wait_recv()
-            landed = self.half_in.at[1, pl.ds(chunk * size, size)]
-            add_blocks(self.half(before, 2 + chunk), [landed], size)
-        self.down = self.wires.send(self.piece(before), self.whole_in.at[1], down)
 
 
 def block_ring(place, part, phase, at):
@@ -330,13 +350,16 @@
     return (lambda j: at(j, 0, 32), lambda j, q: at(j, 8 * q, 8))
 
 
-def start_kernel(
+def gather_phase(
+    place,
+    wires,
+    others,
     ids_ref,
     matrices_ref,
     table_ref,
     positions_ref,
-    full_ref,
-    table_full_ref,
+    blocks,
+    table,
     hidden_ref,
     own_low,
     table_pad,
@@ -348,34 +371,29 @@
     landing,
     ready,
     arrived,
-    send_sems,
-    recv_sems,
     local_sems,
 ):
-    place = coordinates()
     core = place[CORE]
     across = place[X]
     sibling = moved(place, CORE, 1)
-    wires = Wires(send_sems, recv_sems)
+
+    def blocks_at(part, side, k3, first, count):
+        start = ((2 * part + side) * SIDE + k3) * 32 + first
+        return blocks.at[pl.ds(start, count)]
+
     own_low[...] = matrices_ref[...].astype(jnp.bfloat16).reshape(own_low.shape)
-    own_copies = []
     for part in range(3):
         k1, k2, k3 = (place[axis] for axis in ORDERS[part])
-        own_copies.append(
-            pltpu.make_async_copy(
-                own_low.at[part],
-                full_ref.at[part, core, k3, pl.ds(8 * k2 + 2 * k1, 2)],
-                local_sems.at[part],
-            )
-        )
-        own_copies[-1].start()
+        first = ((2 * part + core) * SIDE + k3) * 32 + 8 * k2 + 2 * k1
+        for which in range(2):
+            blocks[first + which] = own_low[part, which]
     ids_all[across] = ids_ref[...]
-    greet(rings_of(place, (X, Y, Z)))
+    table[across] = table_ref[...].astype(jnp.bfloat16)
     rings = [[], [], []]
     for part in range(3):
 
         def at(k3, first, count, part=part):
-            return full_ref.at[part, core, k3, pl.ds(first, count)]
+            return blocks_at(part, core, k3, first, count)
 
         first_axis, second_axis, third_axis = ORDERS[part]
         piece, _ = block_ring(place, part, 0, at)
@@ -393,27 +411,17 @@
         )
     on_z, on_x, on_y = rings[2]
     ids_ring = DirectGather(wires, place, X, lambda j: ids_all.at[j])
-    ids_ring.start()
-    for ring in rings[0]:
-        ring.start()
     rows = table_ref.shape[0]
     table_pad[pl.ds(0, rows)] = table_ref[...].astype(jnp.bfloat16)
     padding = table_pad.shape[0] - rows
     table_pad[pl.ds(rows, padding)] = jnp.zeros((padding, table_pad.shape[1]), jnp.bfloat16)
-    table_low = table_pad.at[pl.ds(0, rows)]
-    own_copies.append(
-        pltpu.make_async_copy(table_low, table_full_ref.at[across], local_sems.at[3])
-    )
-    own_copies[-1].start()
     table_ring = RowGather(
         wires,
         place,
         X,
         0,
-        lambda j, row: table_full_ref.at[j, pl.ds(rows // SIDE * row, rows // SIDE)],
-    )
-    own_copies[3].wait()
-    table_ring.send(0)
+        lambda j, row: table.at[j, pl.ds(rows // SIDE * row, rows // SIDE)],
+    )
     base = (lax.axis_index("vocab") * rows).astype(jnp.float32)
     tiles = table_pad.shape[0] // 128
     lane = lax.broadcasted_iota(jnp.int32, (128, 128), 1).astype(jnp.float32)
@@ -421,10 +429,10 @@
     def group_of(part, which):
         return 2 * ((across // 2 + part) % 2) + which
 
-    def look_up(part, side):
+    def look_up(part, side, half):
         group = group_of(part, side)
 
-        @pl.loop(0, 8)
+        @pl.loop(4 * half, 4 * half + 4)
         def _(quad):
             hot_rows = []
             for which in range(4):
@@ -446,12 +454,16 @@
             for which in range(4):
                 at_y = 2 * (quad % 2) + which // 2
                 first, second = (at_z, at_y) if part == 0 else (at_y, at_z)
-                parts[part, which % 2, first, 2 * second + side] = found[
-                    128 * which : 128 * which + 128
-                ]
+                at = lookup_rows(part, which % 2, first, 2 * second + side, 1)
+                parts[at] = found[128 * which : 128 * which + 128]
+
+    def lookup_rows(part, side, first, index, count):
+        start = ((2 * part + side) * SIDE + first) * 8 + index
+        return lane_range(128 * start, 128 * count)
 
     def to_sibling(part):
-        return wires.send(parts.at[part, 1 - core], sibling_in.at[part], sibling)
+        crossing = parts.at[lookup_rows(part, 1 - core, 0, 0, 32)]
+        return wires.send(crossing, sibling_in.at[part], sibling)
 
     lookup_axes = ((Z, Y), (Y, Z))
     lookup_rings, lookup_ends = [], []
@@ -462,8 +474,8 @@
                 wires,
                 place,
                 first_axis,
-                lambda j, part=part: parts.at[part, core, j],
-                lambda j, h, part=part: parts.at[part, core, j, pl.ds(4 * h, 4)],
+                lambda j, part=part: parts.at[lookup_rows(part, core, j, 0, 8)],
+                lambda j, h, part=part: parts.at[lookup_rows(part, core, j, 4 * h, 4)],
                 8,
                 half_in.at[part],
                 whole_in.at[part],
@@ -474,7 +486,9 @@
                 wires,
                 place,
                 second_axis,
-                lambda j, part=part, k=place[first_axis]: parts.at[part, core, k, pl.ds(2 * j, 2)],
+                lambda j, part=part, k=place[first_axis]: parts.at[
+                    lookup_rows(part, core, k, 2 * j, 2)
+                ],
                 2,
                 landing.at[part],
             )
@@ -482,19 +496,17 @@
 
     def add_sibling(part):
         siblings[part].wait_recv()
-        for j in range(4):
-            add_blocks(parts.at[part, core, j], [sibling_in.at[part, j]], 8)
+        add_blocks(parts.at[lookup_rows(part, core, 0, 0, 32)], [sibling_in.at[part]], 32)
         lookup_rings[part].start()
 
     def take_result(part):
         lookup_ends[part].arrive()
         first_axis, second_axis = lookup_axes[part]
         for which in range(2):
-            total = parts[part, core, place[first_axis], 2 * place[second_axis] + which].astype(
-                jnp.float32
-            )
+            at = lookup_rows(part, core, place[first_axis], 2 * place[second_axis] + which, 1)
+            total = parts[at].astype(jnp.float32)
             for step in range(3):
-                total += landing[part, step, which].astype(jnp.float32)
+                total += landing[part, step, 128 * which : 128 * which + 128].astype(jnp.float32)
             ready[group_of(part, which)] = total.astype(jnp.bfloat16)
 
     shares = [wires.slot() for _ in range(3)]
@@ -502,62 +514,70 @@
     def share(part, ref):
         wires.send_all(ref, ref, sibling, shares[part])
 
-    look_up(0, across % 2)
-    ids_ring.finish()
-    for copy in own_copies[:3]:
-        copy.wait()
+    own_side = across % 2
+    await_greetings(others)
+    ids_ring.start()
+    for ring in rings[0]:
+        ring.start()
+    table_ring.send(0)
+    look_up(0, own_side, 0)
+    look_up(0, own_side, 1)
     for ring, later in zip(rings[0], rings[1]):
         ring.finish()
         later.start()
     for ring in rings[2]:
         ring.send(0)
-    look_up(0, 1 - across % 2)
+    ids_ring.finish()
+    look_up(0, 1 - own_side, 0)
+    look_up(0, 1 - own_side, 1)
     siblings = [to_sibling(0)]
+    look_up(1, 0, 0)
     for ring in rings[1]:
         ring.forward()
-    for ring in rings[2]:
+    look_up(1, 0, 1)
+    add_sibling(0)
+    for ring in (on_y, on_x, on_z):
         ring.send(1)
-    look_up(1, 0)
-    add_sibling(0)
+    look_up(1, 1, 0)
+    look_up(1, 1, 1)
+    siblings.append(to_sibling(1))
     for ring in rings[1]:
         ring.finish()
-    for ring in rings[2]:
-        ring.send(2)
-    on_y.send(3)
+    on_y.send(2)
+    on_x.send(2)
+    lookup_rings[0].forward()
+    add_sibling(1)
+    on_z.send(2)
     on_x.send(3)
-    for index in (1, 2, 3):
-        table_ring.send(index)
-    look_up(1, 1)
-    siblings.append(to_sibling(1))
-    lookup_rings[0].forward()
-    on_z.send(3)
-    add_sibling(1)
+    table_ring.send(1)
     for part in range(3):
-        share(part, full_ref.at[part, core, place[ORDERS[part][2]]])
+        share(part, blocks_at(part, core, place[ORDERS[part][2]], 0, 32))
     lookup_rings[1].forward()
+    share(1, on_x.forward(0))
+    share(1, on_x.forward(2))
     lookup_rings[0].finish()
     lookup_ends[0].start()
-    share(0, on_z.forward(0))
-    share(0, on_z.forward(2))
-    share(1, on_x.forward(0))
-    share(1, on_x.forward(2))
+    on_z.send(3)
+    on_y.send(3)
+    share(1, on_x.forward(1))
+    share(1, on_x.forward(3))
+    table_ring.send(2)
+    table_ring.send(3)
     lookup_rings[1].finish()
     lookup_ends[1].start()
-    share(1, on_x.forward(1))
-    share(1, on_x.forward(3))
-    for index in (0, 2, 1, 3):
-        share(2, on_y.forward(index))
-    share(0, on_z.forward(1))
-    share(0, on_z.forward(3))
+    for ring_part, ring in ((0, on_z), (2, on_y)):
+        for index in (0, 2):
+            share(ring_part, ring.forward(index))
     take_result(0)
+    for ring_part, ring in ((0, on_z), (2, on_y)):
+        for index in (1, 3):
+            share(ring_part, ring.forward(index))
     take_result(1)
     swaps = []
     for step in (1, 2, 3):
         there = moved(place, X, step)
         swaps.append(wires.send(ready.at[there[X]], arrived.at[across], there))
     arrived[across] = ready[across]
-    for index in (0, 2, 1, 3):
-        table_ring.forward(index)
     for part in range(3):
         for index in range(4):
             share(part, rings[2][part].take(index))
@@ -568,68 +588,32 @@
         hidden_ref[:, columns] = (
             arrived[source].astype(jnp.float32) + positions_ref[:, columns]
         )
-    for index in range(4):
-        table_ring.take(index)
-    wires.settle()
+    table_ring.forward(0)
+    table_ring.forward(2)
     for index in (0, 2, 1, 3):
         for part in range(3):
             share(part, rings[2][part].take_far(index))
-    for index in range(4):
-        table_ring.take_far(index)
-    table_ring.settle(table_full_ref.at[across])
+    for index in (1, 3):
+        table_ring.forward(index)
     for part in range(3):
-        rings[2][part].settle(full_ref.at[part, core, 0])
-        wires.whole(full_ref.at[part, core], sibling, shares[part]).wait()
-
-
-def start_call(token_ids, matrices, vocab_table, positions_table):
-    rows, width = vocab_table.shape
-    padded = -(-rows // 128) * 128
-    bf16 = jnp.bfloat16
-    return pl.pallas_call(
-        start_kernel,
-        name="gather_and_look_up",
-        out_shape=(
-            jax.ShapeDtypeStruct((3, 2, SIDE, 32, BLOCK, BLOCK), bf16),
-            jax.ShapeDtypeStruct((N_DP, rows, width), bf16),
-            jax.ShapeDtypeStruct(positions_table.shape, jnp.float32),
-        ),
-        in_specs=[VMEM] * 4,
-        out_specs=(ANY, ANY, VMEM),
-        scratch_shapes=[
-            pltpu.VMEM((3, 2, BLOCK, BLOCK), bf16),
-            pltpu.VMEM((padded, width), bf16),
-            pltpu.VMEM((N_DP,) + token_ids.shape, jnp.int32),
-            pltpu.VMEM((2, 2, SIDE, 8, 128, width), bf16),
-            pltpu.VMEM((2, SIDE, 8, 128, width), bf16),
-            pltpu.VMEM((2, 2, 4, 128, width), bf16),
-            pltpu.VMEM((2, 2, 8, 128, width), bf16),
-            pltpu.VMEM((2, 3, 2, 128, width), bf16),
-            pltpu.VMEM((N_DP, 128, width), bf16),
-            pltpu.VMEM((N_DP, 128, width), bf16),
-            pltpu.SemaphoreType.DMA((140,)),
-            pltpu.SemaphoreType.DMA((140,)),
-            pltpu.SemaphoreType.DMA((4,)),
-        ],
-        compiler_params=pltpu.CompilerParams(
-            collective_id=1, has_side_effects=True, vmem_limit_bytes=VMEM_BYTES
-        ),
-    )(token_ids, matrices, vocab_table, positions_table)
-
-
-def head_kernel(
+        rings[2][part].settle(blocks.at[pl.ds(0, 32)])
+        wires.whole(blocks.at[pl.ds(0, 128)], sibling, shares[part]).wait()
+    return table_ring
+
+
+def head_phase(
+    place,
+    wires,
+    vocab_group,
+    table_ring,
     head_in_ref,
-    table_ref,
+    table,
     target_ref,
     at_ref,
     length_ref,
     d_head_ref,
-    own_grad_ref,
-    next_grad_ref,
-    far_grad_ref,
-    last_grad_ref,
+    table_grad_ref,
     loss_ref,
-    table,
     table_grads,
     pieces,
     rows_in,
@@ -640,16 +624,10 @@
     d_sibling,
     d_first,
     d_second,
-    send_sems,
-    recv_sems,
     local_sems,
 ):
-    place = coordinates()
-    table_load = pltpu.make_async_copy(table_ref, table, local_sems.at[4])
-    table_load.start()
     core = place[CORE]
     sibling = moved(place, CORE, 1)
-    wires = Wires(send_sems, recv_sems)
     own, width = head_in_ref.shape
     half_width = width // 2
     feature_axes = ((Y, Z), (Z, Y))
@@ -658,13 +636,6 @@
         pieces[part, core, far, near] = head_in_ref[
             :, part * half_width : (part + 1) * half_width
         ]
-    vocab_group = [
-        moved(moved(moved(place, Y, near), Z, far), CORE, side)
-        for near in range(SIDE)
-        for far in range(SIDE)
-        for side in range(2)
-    ][1:]
-    greet(vocab_group)
     first_rings, second_rings = [], []
     for part in range(2):
         near_axis, far_axis = feature_axes[part]
@@ -703,6 +674,7 @@
         preferred_element_type=jnp.float32,
     )
     counted = (laid_end_to_end(at_ref[...]) < lengths).astype(jnp.float32)
+    wires.settle(12)
     for ring, later in zip(first_rings, second_rings):
         ring.finish()
         later.start()
@@ -718,7 +690,10 @@
         rows_in[own * index : own * (index + 1), :half_width] = pieces[0, at_core, at_z, at_y]
         rows_in[own * index : own * (index + 1), half_width:] = pieces[1, at_core, at_y, at_z]
 
-    table_load.wait()
+    for index in range(4):
+        table_ring.take(index)
+        table_ring.take_far(index)
+    table_ring.settle(table.at[0])
     groups, rows, group_width = table.shape
     count = rows_in.shape[0]
     chunk = rows // 4
@@ -828,33 +803,33 @@
         )
         first_rings[part].start()
 
-    grad_refs = (own_grad_ref, next_grad_ref, far_grad_ref, last_grad_ref)
     stores = []
 
-    def table_grad(step):
-        group = (place[X] + step) % N_DP
-        columns = lane_range(group * group_width, group_width)
-
+    def table_grad(group):
         @pl.loop(0, 4)
         def _(index):
             at = pl.ds(pl.multiple_of(index * chunk, chunk), chunk)
             product = jnp.dot(
-                d_logits[at], rows_in[:, columns], preferred_element_type=jnp.float32
+                d_logits[at],
+                rows_in[:, group * group_width : (group + 1) * group_width],
+                preferred_element_type=jnp.float32,
             ).astype(jnp.bfloat16)
-            table_grads[step, at] = product
-
+            table_grads[pl.ds(pl.multiple_of(group * rows + index * chunk, chunk), chunk)] = product
+
+        at = pl.ds(group * rows, rows)
         stores.append(
-            pltpu.make_async_copy(table_grads.at[step], grad_refs[step], local_sems.at[step])
+            pltpu.make_async_copy(table_grads.at[at], table_grad_ref.at[at], local_sems.at[group])
         )
         stores[-1].start()
 
+    table_grad(0)
     table_grad(1)
-    table_grad(2)
     for ring, later in zip(first_rings, second_rings):
         ring.finish()
         later.start()
+    table_grad(2)
     table_grad(3)
-    table_grad(0)
+    wires.settle(6)
     for part in range(2):
         second_rings[part].arrive()
         first_axis, second_axis = reduce_axes[part]
@@ -862,56 +837,13 @@
         for step in range(3):
             total += d_second[part, step].astype(jnp.float32)
         d_head_ref[:, part * half_width : (part + 1) * half_width] = total
-    wires.settle()
-    for copy in stores:
-        copy.wait()
-
-
-def head_call(head_in, table_full, targets, positions, lengths):
-    groups, rows, group_width = table_full.shape
-    own, width = head_in.shape
-    count = targets.size
-    half = width // 2
-    bf16 = jnp.bfloat16
-    return pl.pallas_call(
-        head_kernel,
-        name="head",
-        out_shape=(
-            jax.ShapeDtypeStruct((own, width), jnp.float32),
-            *[jax.ShapeDtypeStruct((rows, group_width), bf16)] * groups,
-            jax.ShapeDtypeStruct((1, count), jnp.float32),
-        ),
-        in_specs=[VMEM, ANY, VMEM, VMEM, VMEM],
-        out_specs=(VMEM,) + (ANY,) * groups + (VMEM,),
-        scratch_shapes=[
-            pltpu.VMEM(table_full.shape, bf16),
-            pltpu.VMEM(table_full.shape, bf16),
-            pltpu.VMEM((2, 2, SIDE, SIDE, own, half), bf16),
-            pltpu.VMEM((count, width), bf16),
-            pltpu.VMEM((rows, count), jnp.float32),
-            pltpu.VMEM((rows, count), bf16),
-            pltpu.VMEM((N_VOCAB, 8, count // 4), jnp.float32),
-            pltpu.VMEM((2, 2, SIDE, SIDE, own, half), bf16),
-            pltpu.VMEM((2, SIDE, SIDE, own, half), bf16),
-            pltpu.VMEM((2, 3, SIDE, own, half), bf16),
-            pltpu.VMEM((2, 3, own, half), bf16),
-            pltpu.SemaphoreType.DMA((40,)),
-            pltpu.SemaphoreType.DMA((40,)),
-            pltpu.SemaphoreType.DMA((5,)),
-        ],
-        compiler_params=pltpu.CompilerParams(
-            collective_id=2, has_side_effects=True, vmem_limit_bytes=VMEM_BYTES
-        ),
-    )(head_in, table_full, targets, positions, lengths)
+    return stores
 
 
 def finish_kernel(
     grads_ref,
     small_ref,
-    own_grad_ref,
-    next_grad_ref,
-    far_grad_ref,
-    last_grad_ref,
+    head_grad_ref,
     d_embed_ref,
     ids_ref,
     loss_ref,
@@ -931,7 +863,9 @@
     small_a,
     small_b,
     small_c,
-    table_parts,
+    table_sums,
+    table_half,
+    table_whole,
     embeds,
     ids_all,
     totals_all,
@@ -959,10 +893,7 @@
         for part in range(3):
             j = (third[part] + step) % SIDE
             block_loads[part, step] = load(grads_ref.at[part, core, j], sums.at[part, j])
-    table_loads = [
-        load(ref, table_parts.at[index])
-        for index, ref in enumerate((own_grad_ref, next_grad_ref, far_grad_ref, last_grad_ref))
-    ]
+    table_load = load(head_grad_ref, table_sums)
 
     width = table_grad_ref.shape[1]
     embed_axes = ((Y, Z), (Z, Y))
@@ -980,6 +911,7 @@
         moved(moved(place, Y, step), Z, other) for step in range(SIDE) for other in range(SIDE)
     ][1:]
     greet(line + plane)
+    await_greetings(line + plane)
     swaps = []
     for step in (1, 2, 3):
         there = moved(place, X, step)
@@ -989,12 +921,13 @@
     ids_ring.start()
     small_crossing = wires.send(small_ref.at[1 - core], small_sibling, sibling)
     crossings = {}
-    for step in (2, 1, 3, 0):
+    for step, half in ((2, 0), (2, 1), (1, None), (3, None), (0, None)):
         for part in range(3):
             j = (third[part] + step) % SIDE
-            crossings[part, step] = wires.send(
-                grads_ref.at[part, 1 - core, j], sibling_in.at[part, j], sibling
-            )
+            source, target = grads_ref.at[part, 1 - core, j], sibling_in.at[part, j]
+            if half is not None:
+                source, target = source.at[pl.ds(16 * half, 16)], target.at[pl.ds(16 * half, 16)]
+            crossings[part, step, half] = wires.send(source, target, sibling)
 
     embed_first, embed_second = [], []
     for part in range(2):
@@ -1040,6 +973,16 @@
         )
         piece, _ = block_ring(place, part, 0, at)
         last_rings.append(DirectReduce(wires, place, last_axis, piece, 2, whole_c.at[part]))
+    table_ring = QuarterReduce(
+        wires,
+        place,
+        X,
+        lambda j: table_sums.at[j],
+        lambda j, q: table_sums.at[j, pl.ds(TABLE_CHUNKS // 4 * q, TABLE_CHUNKS // 4)],
+        TABLE_CHUNKS,
+        table_half,
+        table_whole,
+    )
     small_rings = [
         DirectReduce(wires, place, Z, lambda j: small_sums.at[j], 16, small_a),
         DirectReduce(
@@ -1050,11 +993,15 @@
         ),
     ]
 
-    def add_crossing(part, step):
+    def add_crossing(part, step, half=None):
         j = (third[part] + step) % SIDE
-        block_loads[part, step].wait()
-        crossings[part, step].wait_recv()
-        add_blocks(sums.at[part, j], [sibling_in.at[part, j]], 32)
+        if not half:
+            block_loads[part, step].wait()
+        crossings[part, step, half].wait_recv()
+        at = pl.ds(0, 32) if half is None else pl.ds(16 * half, 16)
+        add_blocks(
+            sums.at[part, j, at], [sibling_in.at[part, j, at]], 32 if half is None else 16
+        )
 
     embed_siblings = []
 
@@ -1105,24 +1052,29 @@
             )
         gathers.append(row)
 
-    small_load.wait()
-    small_crossing.wait_recv()
-    for j in range(4):
-        add_blocks(small_sums.at[j], [small_sibling.at[j]], 16)
     for part in range(3):
-        add_crossing(part, 2)
+        add_crossing(part, 2, 0)
         first_rings[part].start(0)
     for copy in swaps:
         copy.wait_recv()
     for ring in embed_first:
         ring.start()
+    table_load.wait()
+    table_ring.start(0)
+    table_ring.start(1)
+    small_load.wait()
+    small_crossing.wait_recv()
+    for j in range(4):
+        add_blocks(small_sums.at[j], [small_sibling.at[j]], 16)
     small_rings[0].start()
     for part in range(3):
-        add_crossing(part, 1)
+        add_crossing(part, 2, 1)
     for ring in embed_first:
         ring.forward()
     for part in range(3):
         first_rings[part].start(1)
+    for part in range(3):
+        add_crossing(part, 1)
     for ring, later in zip(embed_first, embed_second):
         ring.finish()
         later.start()
@@ -1132,24 +1084,22 @@
     share(1, 0)
     for part in range(3):
         add_crossing(part, 3)
+    for part in range(3):
+        first_rings[part].start_near()
+    table_ring.start_near()
     ids_ring.finish()
-    for copy in table_loads:
-        copy.wait()
-
-    @pl.loop(0, rows // 80)
+
+    @pl.loop(0, 4)
     def _(index):
-        at = pl.ds(pl.multiple_of(index * 80, 80), 80)
-        total = table_parts[0, at].astype(jnp.float32)
-        for step in range(1, N_DP):
-            total += table_parts[step, at].astype(jnp.float32)
-        table_grad_ref[at] = total
+        at = pl.ds(pl.multiple_of(index * chunk, chunk), chunk)
+        table_grad_ref[at] = jnp.zeros((chunk, width), jnp.float32)
 
     scatter_rows(0, core, 0)
     scatter_rows(1, core, 0)
+    for ring in first_rings:
+        ring.forward()
     for part in range(3):
         add_crossing(part, 0)
-    for ring in first_rings:
-        ring.forward()
     for copy in embed_siblings:
         copy.wait_recv()
     embed_siblings.clear()
@@ -1161,6 +1111,7 @@
         share(part, 3)
     small_rings[1].finish()
     small_rings[2].start()
+    table_ring.forward()
     for part in range(2):
         scatter_rows(part, core, 1)
         scatter_rows(part, core, 3)
@@ -1170,16 +1121,16 @@
     for part in range(2):
         scatter_rows(part, 1 - core, 1)
         scatter_rows(part, 1 - core, 3)
+    wires.settle(32)
+    for ring, later in zip(first_rings, middle_rings):
+        ring.finish()
+        later.start()
     small_rings[2].finish()
     own_small = small_sums[place[Z], 4 * place[Y] + across].astype(jnp.float32)
     final_ref[0, core, place[Z], place[Y], across] = own_small[:8]
     final_ref[1, core, across, place[Z], place[Y]] = jnp.concatenate(
         [own_small[8:9], jnp.zeros((7, 128), jnp.float32)], 0
     )
-    wires.settle(17)
-    for ring, later in zip(first_rings, middle_rings):
-        ring.finish()
-        later.start()
     for gather in gathers[0]:
         gather.start()
     for part in range(2):
@@ -1202,6 +1153,18 @@
         gather.finish()
         later.start()
     scatter_rows(1, 1 - core, 2)
+    table_ring.arrive()
+    table_block = rows // TABLE_CHUNKS
+
+    @pl.loop(0, TABLE_CHUNKS)
+    def _(index):
+        at = pl.ds(pl.multiple_of(index * table_block, table_block), table_block)
+        table_grad_ref[at] += (
+            table_sums[across, index].astype(jnp.float32)
+            + table_whole[0, index].astype(jnp.float32)
+            + table_whole[1, index].astype(jnp.float32)
+        )
+
     table_squares = jnp.zeros((1, width), jnp.float32)
     for index in range(4):
         values = table_grad_ref[index * chunk : (index + 1) * chunk]
@@ -1241,9 +1204,10 @@
     wires.settle()
 
 
-def finish_call(grads, small, head_grads, d_embed, token_ids, loss_row):
+def finish_call(grads, small, head_grad, d_embed, token_ids, loss_row):
     bf16 = jnp.bfloat16
-    rows, width = head_grads[0].shape
+    _, chunks, chunk_rows, width = head_grad.shape
+    rows = chunks * chunk_rows
     block = (BLOCK, BLOCK)
     return pl.pallas_call(
         finish_kernel,
@@ -1254,7 +1218,7 @@
             jax.ShapeDtypeStruct((2, 2, SIDE, SIDE, SIDE, 8, 128), jnp.float32),
             jax.ShapeDtypeStruct((8, 128), jnp.float32),
         ),
-        in_specs=[ANY] * 6 + [VMEM] * 3,
+        in_specs=[ANY] * 3 + [VMEM] * 3,
         out_specs=(VMEM,) * 4,
         scratch_shapes=[
             pltpu.VMEM((3, SIDE, 32) + block, bf16),
@@ -1269,7 +1233,9 @@
             pltpu.VMEM((3, 16, 16, 128), bf16),
             pltpu.VMEM((3, 4, 16, 128), bf16),
             pltpu.VMEM((3, 1, 16, 128), bf16),
-            pltpu.VMEM((N_DP, rows, width), bf16),
+            pltpu.VMEM(head_grad.shape, bf16),
+            pltpu.VMEM((2, chunks // 2, chunk_rows, width), bf16),
+            pltpu.VMEM((2, chunks, chunk_rows, width), bf16),
             pltpu.VMEM((2, 2, SIDE, 8, 128, width), bf16),
             pltpu.VMEM((N_DP,) + token_ids.shape, jnp.int32),
             pltpu.VMEM((2, SIDE * SIDE, 8, 128), jnp.float32),
@@ -1280,7 +1246,7 @@
         compiler_params=pltpu.CompilerParams(
             collective_id=3, has_side_effects=True, vmem_limit_bytes=VMEM_BYTES
         ),
-    )(grads, small, *head_grads, d_embed, token_ids, loss_row)
+    )(grads, small, head_grad, d_embed, token_ids, loss_row)
 
 
 def row_mean(values):
@@ -1350,11 +1316,10 @@
     return jnp.where(lane < HEAD_DIM, values[:count], values[count:])
 
 
-def forward_kernel(
+def forward_phase(
     where_ref,
     at_ref,
     length_ref,
-    full_ref,
     hidden_ref,
     vec_ref,
     head_in_ref,
@@ -1368,9 +1333,7 @@
     blocks,
     normed_rows,
     activated,
-    sems,
 ):
-    copies = load_blocks(full_ref, blocks, sems)
     count = head_in_ref.shape[0]
     bf16 = jnp.bfloat16
     own = lax.axis_index("vocab")
@@ -1380,8 +1343,6 @@
     normed_rows[...] = hat * vec_ref[0:1] + vec_ref[1:2]
     normed_one = normed_rows[...].astype(bf16)
     normed_own = selected_rows(normed_rows, positions).astype(bf16)
-    for copy in copies:
-        copy.wait()
 
     @pl.loop(0, 4)
     def _(tile):
@@ -1467,38 +1428,216 @@
     head_in_ref[...] = (hat * vec_ref[12:13] + vec_ref[13:14]).astype(bf16)
 
 
-def forward_call(where, positions, lengths, full, hidden, vectors):
-    count = positions.shape[0]
-    seq_len = hidden.shape[0]
-    bf16 = jnp.bfloat16
+def forward_kernel(
+    where_ref,
+    at_smem_ref,
+    length_smem_ref,
+    ids_ref,
+    target_ref,
+    at_ref,
+    length_ref,
+    matrices_ref,
+    table_ref,
+    positions_ref,
+    vec_ref,
+    full_ref,
+    hidden_ref,
+    query_ref,
+    kv_ref,
+    probs_ref,
+    attended_ref,
+    middle_ref,
+    pre_act_ref,
+    last_ref,
+    d_head_ref,
+    table_grad_ref,
+    loss_ref,
+    blocks,
+    table,
+    own_low,
+    table_pad,
+    ids_all,
+    parts,
+    sibling_in,
+    half_in,
+    whole_in,
+    landing,
+    ready,
+    arrived,
+    normed_rows,
+    activated,
+    head_in,
+    pieces,
+    rows_in,
+    logits,
+    d_logits,
+    stats,
+    d_rows,
+    d_sibling,
+    d_first,
+    d_second,
+    send_sems,
+    recv_sems,
+    local_sems,
+):
+    place = coordinates()
+    wires = Wires(send_sems, recv_sems)
+    vocab_group = [
+        moved(moved(moved(place, Y, near), Z, far), CORE, side)
+        for near in range(SIDE)
+        for far in range(SIDE)
+        for side in range(2)
+    ][1:]
+    others = vocab_group + [moved(place, X, step) for step in (1, 2, 3)]
+    greet(others)
+    table_ring = gather_phase(
+        place,
+        wires,
+        others,
+        ids_ref,
+        matrices_ref,
+        table_ref,
+        positions_ref,
+        blocks,
+        table,
+        hidden_ref,
+        own_low,
+        table_pad,
+        ids_all,
+        parts,
+        sibling_in,
+        half_in,
+        whole_in,
+        landing,
+        ready,
+        arrived,
+        local_sems,
+    )
+    keep = pltpu.make_async_copy(blocks, full_ref, local_sems.at[4])
+    keep.start()
+    forward_phase(
+        where_ref,
+        at_smem_ref,
+        length_smem_ref,
+        hidden_ref,
+        vec_ref,
+        head_in,
+        query_ref,
+        kv_ref,
+        probs_ref,
+        attended_ref,
+        middle_ref,
+        pre_act_ref,
+        last_ref,
+        blocks,
+        normed_rows,
+        activated,
+    )
+    stores = head_phase(
+        place,
+        wires,
+        vocab_group,
+        table_ring,
+        head_in,
+        table,
+        target_ref,
+        at_ref,
+        length_ref,
+        d_head_ref,
+        table_grad_ref,
+        loss_ref,
+        parts,
+        pieces,
+        rows_in,
+        logits,
+        d_logits,
+        stats,
+        d_rows,
+        d_sibling,
+        d_first,
+        d_second,
+        local_sems,
+    )
+    wires.settle()
+    keep.wait()
+    for copy in stores:
+        copy.wait()
+
+
+def forward_call(where, positions, lengths, token_ids, target_ids, matrices, vocab_table, positions_table, vectors):
+    rows, width = vocab_table.shape
+    padded = -(-rows // 128) * 128
+    own, seqs = positions.shape
+    seq_len = positions_table.shape[0]
+    count, half = own * seqs, D // 2
+    bf16, f32 = jnp.bfloat16, jnp.float32
     shape = jax.ShapeDtypeStruct
+    slots = where.shape[0]
+    smem = pl.BlockSpec(memory_space=pltpu.SMEM)
     return pl.pallas_call(
         forward_kernel,
-        name="layer_forward",
+        name="forward_and_head",
         out_shape=(
-            shape((count, D), bf16),
-            shape((count, D), bf16),
+            shape((slots, BLOCK, BLOCK), bf16),
+            shape((seq_len, D), f32),
+            shape((own, D), bf16),
             shape((seq_len, 2 * D), bf16),
-            shape((HEADS * count, seq_len), jnp.float32),
-            shape((count, D), bf16),
-            shape((count, D), jnp.float32),
-            shape((count, FF), jnp.float32),
-            shape((count, D), jnp.float32),
+            shape((HEADS * own, seq_len), f32),
+            shape((own, D), bf16),
+            shape((own, D), f32),
+            shape((own, FF), f32),
+            shape((own, D), f32),
+            shape((own, D), f32),
+            shape((N_DP * rows, width), bf16),
+            shape((1, count), f32),
         ),
-        grid_spec=pltpu.PrefetchScalarGridSpec(
-            num_scalar_prefetch=3,
-            grid=(),
-            in_specs=[ANY, VMEM, VMEM],
-            out_specs=(VMEM,) * 8,
-            scratch_shapes=[
-                pltpu.VMEM(full.shape, bf16),
-                pltpu.VMEM(hidden.shape, jnp.float32),
-                pltpu.VMEM((count, FF), bf16),
-                pltpu.SemaphoreType.DMA((8,)),
-            ],
+        in_specs=[smem] * 3 + [VMEM] * 8,
+        out_specs=(ANY,) + (VMEM,) * 9 + (ANY, VMEM),
+        scratch_shapes=[
+            pltpu.VMEM((slots, BLOCK, BLOCK), bf16),
+            pltpu.VMEM((N_DP, rows, width), bf16),
+            pltpu.VMEM((3, 2, BLOCK, BLOCK), bf16),
+            pltpu.VMEM((padded, width), bf16),
+            pltpu.VMEM((N_DP,) + token_ids.shape, jnp.int32),
+            pltpu.VMEM((128 * 128, width), bf16),
+            pltpu.VMEM((2, 32 * 128, width), bf16),
+            pltpu.VMEM((2, 2, 4 * 128, width), bf16),
+            pltpu.VMEM((2, 2, 8 * 128, width), bf16),
+            pltpu.VMEM((2, 3, 2 * 128, width), bf16),
+            pltpu.VMEM((N_DP, 128, width), bf16),
+            pltpu.VMEM((N_DP, 128, width), bf16),
+            pltpu.VMEM((seq_len, D), f32),
+            pltpu.VMEM((own, FF), bf16),
+            pltpu.VMEM((own, D), bf16),
+            pltpu.VMEM((2, 2, SIDE, SIDE, own, half), bf16),
+            pltpu.VMEM((count, D), bf16),
+            pltpu.VMEM((rows, count), f32),
+            pltpu.VMEM((rows, count), bf16),
+            pltpu.VMEM((N_VOCAB, 8, count // 4), f32),
+            pltpu.VMEM((2, 2, SIDE, SIDE, own, half), bf16),
+            pltpu.VMEM((2, SIDE, SIDE, own, half), bf16),
+            pltpu.VMEM((2, 3, SIDE, own, half), bf16),
+            pltpu.VMEM((2, 3, own, half), bf16),
+            pltpu.SemaphoreType.DMA((200,)),
+            pltpu.SemaphoreType.DMA((200,)),
+            pltpu.SemaphoreType.DMA((5,)),
+        ],
+        compiler_params=pltpu.CompilerParams(
+            collective_id=1, has_side_effects=True, vmem_limit_bytes=VMEM_BYTES
         ),
-        compiler_params=pltpu.CompilerParams(vmem_limit_bytes=VMEM_BYTES),
-    )(where, positions, lengths, full, hidden, vectors)
+    )(
+        where,
+        positions,
+        lengths,
+        token_ids,
+        target_ids,
+        positions,
+        lengths.reshape(1, -1),
+        matrices,
+        vocab_table,
+        positions_table,
+        vectors,
+    )
 
 
 def gelu_slope(values):
@@ -1721,10 +1860,10 @@
 
 def update_kernel(*refs):
     names = 18
-    sources, targets = refs[:names], refs[names : names + 14]
-    buffers = refs[names + 14 : names + 14 + names]
-    results = refs[names + 14 + names : names + 28 + names]
-    vec_grad, load_sems, store_sems = refs[names + 28 + names :]
+    sources, (loss_ref, norm_ref, *targets) = refs[:names], refs[names : names + 15]
+    buffers = refs[names + 15 : 2 * names + 15]
+    results = refs[2 * names + 15 : 2 * names + 28]
+    vec_grad, load_sems, store_sems = refs[2 * names + 28 :]
     loads = [
         pltpu.make_async_copy(source, buffer, load_sems.at[index])
         for index, (source, buffer) in enumerate(zip(sources, buffers))
@@ -1744,7 +1883,7 @@
     totals, final, grads, matrices, left_stats, right_stats, left_roots, right_roots = buffers[:8]
     table_grad, table, table_m, table_v = buffers[8:12]
     positions, pos_m, pos_v, vectors, vectors_m, vectors_v = buffers[12:]
-    scalars, matrices_new, left_new, right_new, matrices_grad = results[:5]
+    matrices_new, left_new, right_new, matrices_grad = results[:4]
     for copy in loads[:2]:
         copy.wait()
     row_squares = jnp.zeros((8, 128), jnp.float32)
@@ -1756,10 +1895,8 @@
     loss = jnp.sum(totals[1:2])
     norm = jnp.sqrt(jnp.full((1, 128), squares, jnp.float32))
     clip = CLIP_LEVEL / jnp.maximum(norm, CLIP_LEVEL)
-    scalars[...] = jnp.concatenate(
-        [jnp.full((1, 128), loss, jnp.float32), norm, jnp.zeros((6, 128), jnp.float32)], 0
-    )
-    store(0)
+    loss_ref[0, 0] = loss
+    norm_ref[0, 0] = jnp.max(norm)
     for copy in loads[2:8]:
         copy.wait()
 
@@ -1777,7 +1914,7 @@
         weight = matrices[slot]
         matrices_new[slot] = weight - SHAMPOO_RATE * (stepped + DECAY_RATE * weight)
 
-    for index in range(1, 5):
+    for index in range(4):
         store(index)
     for copy in loads[8:12]:
         copy.wait()
@@ -1794,10 +1931,10 @@
                 table[at], table_m[at], table_v[at], grad, TABLE_RATE, DECAY_RATE
             )
             for order, value in enumerate(stepped):
-                results[5 + order][at] = value
+                results[4 + order][at] = value
 
         for order in range(3):
-            store(5 + order, pl.ds(index * chunk, chunk))
+            store(4 + order, pl.ds(index * chunk, chunk))
     for copy in loads[12:]:
         copy.wait()
     tiles = D // 128
@@ -1815,19 +1952,19 @@
             DECAY_RATE,
         )
         for order, value in enumerate(stepped):
-            results[8 + order][at, lanes] = value
+            results[7 + order][at, lanes] = value
         if group < vectors.shape[0]:
             vec_grad[group : group + 1, lanes] = (
                 final[1, at_core, at_x, at_z, at_y, 0:1] * clip
             )
-    for index in range(8, 11):
+    for index in range(7, 10):
         store(index)
     stepped = adam_step(
         vectors[...], vectors_m[...], vectors_v[...], vec_grad[...], VECTOR_RATE, 0.0
     )
     for order, value in enumerate(stepped):
-        results[11 + order][...] = value
-        store(11 + order)
+        results[10 + order][...] = value
+        store(10 + order)
     for copy in stores:
         copy.wait()
 
@@ -1835,14 +1972,16 @@
 def update_call(totals, final, grads, blocks, table_grad, table, positions, vectors):
     sources = [totals, final, grads, *blocks, table_grad, *table, *positions, *vectors]
     shape = lambda array: jax.ShapeDtypeStruct(array.shape, jnp.float32)
-    targets = [shape(totals)] + [shape(blocks[0])] * 4
+    targets = [shape(blocks[0])] * 4
     targets += [shape(array) for array in (*table, *positions, *vectors)]
+    scalar = jax.ShapeDtypeStruct((1, 1), jnp.float32)
+    smem = pl.BlockSpec(memory_space=pltpu.SMEM)
     return pl.pallas_call(
         update_kernel,
         name="optimizer_update",
-        out_shape=tuple(targets),
+        out_shape=(scalar, scalar, *targets),
         in_specs=[ANY] * len(sources),
-        out_specs=(ANY,) * len(targets),
+        out_specs=(smem, smem) + (ANY,) * len(targets),
         scratch_shapes=[pltpu.VMEM(array.shape, jnp.float32) for array in sources]
         + [pltpu.VMEM(target.shape, jnp.float32) for target in targets]
         + [
@@ -1890,38 +2029,36 @@
     vectors_m,
     vectors_v,
 ):
-    slots = block_of_slot.shape[0]
-    block_iota = jnp.arange(slots, dtype=jnp.int32)
+    block_iota = jnp.arange(block_of_slot.shape[0], dtype=jnp.int32)
     where = jnp.sum(
         jnp.where(block_of_slot[None, :] == block_iota[:, None], slot_places()[None, :], 0),
         1,
         dtype=jnp.int32,
     )
-    full, table_full, hidden = start_call(token_ids, matrices, vocab_table, positions_table)
-    full_blocks = full.reshape(slots, BLOCK, BLOCK)
     positions = loss_positions.T
-    head_in, *cache = forward_call(
-        where, positions, seq_lengths, full_blocks, hidden, vectors
-    )
-    d_head_in, *head_grads, loss_row = head_call(
-        head_in, table_full, target_ids.T, positions, seq_lengths.reshape(1, -1)
-    )
-    for step in range(1, N_DP):
-        head_grads[step] = lax.ppermute(
-            head_grads[step], "dp", [(i, (i + step) % N_DP) for i in range(N_DP)]
-        )
+    full, hidden, *cache, d_head_in, head_grad, loss_row = forward_call(
+        where,
+        positions,
+        seq_lengths,
+        token_ids,
+        target_ids.T,
+        matrices,
+        vocab_table,
+        positions_table,
+        vectors,
+    )
     grad_blocks, small, d_embed = backward_call(
-        where, positions, full_blocks, hidden, vectors, cache, d_head_in
+        where, positions, full, hidden, vectors, cache, d_head_in
     )
     owned_grads, table_grad_own, final, totals = finish_call(
-        grad_blocks.reshape(full.shape[:3] + (32, BLOCK, BLOCK)),
+        grad_blocks.reshape(3, 2, SIDE, 32, BLOCK, BLOCK),
         small.reshape(2, SIDE, 16, 16, 128),
-        head_grads,
+        head_grad.reshape(N_DP, TABLE_CHUNKS, -1, head_grad.shape[1]),
         d_embed,
         token_ids,
         loss_row,
     )
-    scalars, *updated = update_call(
+    loss, norm, *updated = update_call(
         totals,
         final,
         owned_grads,
@@ -1931,7 +2068,7 @@
         (positions_table, pos_m, pos_v),
         (vectors, vectors_m, vectors_v),
     )
-    return (scalars[0, 0], scalars[1, 0], *updated)
+    return (loss.reshape(()), norm.reshape(()), *updated)
 
 
 def solution(mesh):

time: 312 us -> 287 us (0.920)
  Pallas kernels: 303 us -> 284 us
  starting transfers between devices: 3.36 us -> 0 us
    pallas_call x4 -> x2, Pallas kernels: 164 us -> 146 us  [the longest x1 137 us: forward_call(): pl.pallas_call(forward_kernel, name='forward_and_head', out_shape=(shape(...]
    ppermute x3 -> x0, starting transfers between devices: 3.36 us -> none  [per_device(): lax.ppermute(head_grads[step], 'dp', [(i, (i + step) % N_DP) for i in ran...]
  transfers between devices with their start and end apart: 3 -> 0, of which waited for: 0 -> 0; matrix products, arithmetic and copies ran while one was open for 0% -> 0% of each run, Pallas kernels for 12% -> 0%
where the time goes in v3:
time: 287 us
  Pallas kernels  284 us (99%)
    pallas_call x1, Pallas kernels, forward_call(): pl.pallas_call(forward_kernel, name='forward_and_head', out_shape=(shape(...  137 us
    pallas_call x1, Pallas kernels, finish_call(): pl.pallas_call(finish_kernel, name='reduce_and_scatter', out_shape=(jax.S...  101 us
    pallas_call x1, Pallas kernels, backward_call(): pl.pallas_call(backward_kernel, name='layer_backward', out_shape=(shape(f...  36.5 us
    pallas_call x1, Pallas kernels, update_call(): pl.pallas_call(update_kernel, name='optimizer_update', out_shape=(scalar,...  9.13 us

profile of v3, /device:TPU:1, one launch (start us, length us, event | category | flops | bytes accessed | tf_op | source)
XLA Modules:
  0.0 286.5 jit_solution(11767534167836736090)
XLA Ops:
  0.6 1.6 select_reduce_fusion.where_ref
  2.3 137.0 %forward_and_head.1 = (bf16[768,128,128]{2,1,0:T(8,128)(2,1)}, f32[128,1024]{1,0:T(8,128)}, bf16[16,1024]{1,0:T(8,128)(2,1)}, bf16[128,2048]{1,0:T(8,128)(2,1)},...) custom-call(s32[768]{0:T(1024)} %select_reduce_fusion.where_ref, ...), custom_call_target="tpu_custom_call" | custom-call | tf_op jit(solution)/shard_map/forward_and_head/pallas_call | solution.py:1577
  139.2 36.5 %layer_backward.1 = (bf16[768,128,128]{2,1,0:T(8,128)(2,1)}, bf16[128,16,128]{2,1,0:T(8,128)(2,1)}, bf16[128,1024]{1,0:T(8,128)(2,1)}) custom-call(s32[768]{0:T(1024)} %select_reduce_fusion.where_ref, s32[16,32]{1,0:T(8,128)} %bitcast.13, bf16[768,128,128]{2,1,0:T(8,128)(2,1)} %get-tuple-element.49.full_ref, f32[128,1024]{1,0:T(8,128)} %get-tuple-element.50.hidden_ref, ...), custom_call_target="tpu_custom_call" | custom-call | tf_op jit(solution)/shard_map/layer_backward/pallas_call | solution.py:1812
  175.7 101.5 %reduce_and_scatter.1 = (f32[3,2,128,128]{3,2,1,0:T(8,128)}, f32[1600,256]{1,0:T(8,128)}, f32[2,2,4,4,4,8,128]{6,5,4,3,2,1,0:T(8,128)}, f32[8,128]{1,0:T(8,128)}) custom-call(bf16[3,2,4,32,128,128]{5,4,3,2,1,0:T(8,128)(2,1)} %bitcast.8, bf16[2,4,16,16,128]{4,3,2,1,0:T(8,128)(2,1)} %bitcast.10, bf16[4,20,80,256]{3,2,1,0:T(8,128)(2,1)} %bitcast.9, ...), custom_call_target="tpu_custom_call" | custom-call | tf_op jit(solution)/shard_map/reduce_and_scatter/pallas_call | solution.py:1212
  277.2 9.1 %optimizer_update.1 = (f32[1,1]{1,0:T(1,128)}, f32[1,1]{1,0:T(1,128)}, f32[6,128,128]{2,1,0:T(8,128)}, f32[6,128,128]{2,1,0:T(8,128)}, f32[6,128,128]{2,1,0:T(8,...) custom-call(f32[8,128]{1,0:T(8,128)} %get-tuple-element.64.refs_0_, ...), custom_call_target="tpu_custom_call" | custom-call | tf_op jit(solution)/shard_map/optimizer_update/pallas_call | solution.py:1979

commit v4 on v3

--- a/solution.py
+++ b/solution.py
@@ -1,3 +1,5 @@
+import math
+
 import jax
 import jax.numpy as jnp
 import numpy as np
@@ -98,12 +100,16 @@
 
 class Wires:
     def __init__(self, send_sems, recv_sems):
-        self.send_sems, self.recv_sems, self.used = send_sems, recv_sems, 0
-        self.sent = []
-
-    def slot(self):
-        self.used += 1
-        return self.used - 1
+        self.send_sems, self.recv_sems = send_sems, recv_sems
+        self.send_slots, self.recv_slots, self.sent = 0, 0, []
+
+    def send_slot(self):
+        self.send_slots += 1
+        return self.send_slots - 1
+
+    def recv_slot(self):
+        self.recv_slots += 1
+        return self.recv_slots - 1
 
     def copy(self, source, target, place, send_slot, recv_slot):
         return pltpu.make_async_remote_copy(
@@ -115,19 +121,25 @@
             device_id_type=MESH_IDS,
         )
 
-    def send(self, source, target, place, bundle=None):
-        recv_slot = self.slot()
-        copy = self.copy(source, target, place, recv_slot if bundle is None else bundle, recv_slot)
+    def send(self, source, target, place, send_slot=None):
+        slot = self.send_slot() if send_slot is None else send_slot
+        copy = self.copy(source, target, place, slot, self.recv_slot())
         copy.start()
-        if bundle is None:
+        if send_slot is None:
             self.sent.append(copy)
         return copy
 
+    def bundle(self):
+        return self.send_slot(), self.recv_slot()
+
     def send_all(self, source, target, place, bundle):
-        self.copy(source, target, place, bundle, bundle).start()
+        self.copy(source, target, place, *bundle).start()
 
     def whole(self, ref, place, bundle):
-        return self.copy(ref, ref, place, bundle, bundle)
+        return self.copy(ref, ref, place, *bundle)
+
+    def await_sent(self, ref, place, send_slot):
+        self.copy(ref, ref, place, send_slot, 0).wait_send()
 
     def settle(self, latest=0):
         done = len(self.sent) - latest
@@ -138,6 +150,20 @@
 
 def lane_range(first, count):
     return pl.ds(pl.multiple_of(first, 128), count)
+
+
+class Group:
+    def __init__(self, wires, place):
+        self.wires, self.place, self.slot, self.size = wires, place, wires.send_slot(), 0
+
+    def send(self, source, target, place):
+        self.size += math.prod(source.shape) * jnp.dtype(source.dtype).itemsize
+        return self.wires.send(source, target, place, self.slot)
+
+    def settle(self, blocks):
+        count, rest = divmod(self.size, math.prod(blocks.shape[1:]) * 2)
+        assert rest == 0 and count <= blocks.shape[0]
+        self.wires.await_sent(blocks.at[pl.ds(0, count)], self.place, self.slot)
 
 
 def add_blocks(target, sources, count):
@@ -260,7 +286,7 @@
         self.wires, self.place, self.axis = wires, place, axis
         self.row, self.mine, self.first = row, place[axis], first
         self.up, self.down, self.far = [], [], {}
-        self.bundles = [wires.slot() for _ in range(3)]
+        self.bundles = [wires.send_slot() for _ in range(3)]
 
     def of(self, piece, index):
         return self.row((self.mine + piece) % SIDE, (self.first + (0, 1, 3, 2)[index]) % SIDE)
@@ -290,7 +316,7 @@
 
     def settle(self, piece):
         for bundle in self.bundles:
-            self.wires.whole(piece, self.place, bundle).wait_send()
+            self.wires.await_sent(piece, self.place, bundle)
 
 
 class QuarterReduce(RingReduce):
@@ -376,6 +402,7 @@
     core = place[CORE]
     across = place[X]
     sibling = moved(place, CORE, 1)
+    group = Group(wires, place)
 
     def blocks_at(part, side, k3, first, count):
         start = ((2 * part + side) * SIDE + k3) * 32 + first
@@ -397,9 +424,9 @@
 
         first_axis, second_axis, third_axis = ORDERS[part]
         piece, _ = block_ring(place, part, 0, at)
-        rings[0].append(DirectGather(wires, place, first_axis, piece, own_low.at[part]))
+        rings[0].append(DirectGather(group, place, first_axis, piece, own_low.at[part]))
         piece, half = block_ring(place, part, 1, at)
-        rings[1].append(RingGather(wires, place, second_axis, piece, half))
+        rings[1].append(RingGather(group, place, second_axis, piece, half))
         rings[2].append(
             RowGather(
                 wires,
@@ -430,13 +457,13 @@
         return 2 * ((across // 2 + part) % 2) + which
 
     def look_up(part, side, half):
-        group = group_of(part, side)
+        dp_group = group_of(part, side)
 
         @pl.loop(4 * half, 4 * half + 4)
         def _(quad):
             hot_rows = []
             for which in range(4):
-                ids = ids_all[group, pl.ds(4 * quad + which, 1), :].astype(jnp.float32) - base
+                ids = ids_all[dp_group, pl.ds(4 * quad + which, 1), :].astype(jnp.float32) - base
                 column = jnp.transpose(jnp.broadcast_to(ids, (128, 128)))
                 hot_rows.append(
                     jnp.concatenate(
@@ -463,7 +490,7 @@
 
     def to_sibling(part):
         crossing = parts.at[lookup_rows(part, 1 - core, 0, 0, 32)]
-        return wires.send(crossing, sibling_in.at[part], sibling)
+        return group.send(crossing, sibling_in.at[part], sibling)
 
     lookup_axes = ((Z, Y), (Y, Z))
     lookup_rings, lookup_ends = [], []
@@ -471,7 +498,7 @@
         first_axis, second_axis = lookup_axes[part]
         lookup_rings.append(
             RingReduce(
-                wires,
+                group,
                 place,
                 first_axis,
                 lambda j, part=part: parts.at[lookup_rows(part, core, j, 0, 8)],
@@ -483,7 +510,7 @@
         )
         lookup_ends.append(
             DirectReduce(
-                wires,
+                group,
                 place,
                 second_axis,
                 lambda j, part=part, k=place[first_axis]: parts.at[
@@ -509,7 +536,7 @@
                 total += landing[part, step, 128 * which : 128 * which + 128].astype(jnp.float32)
             ready[group_of(part, which)] = total.astype(jnp.bfloat16)
 
-    shares = [wires.slot() for _ in range(3)]
+    shares = [wires.bundle() for _ in range(3)]
 
     def share(part, ref):
         wires.send_all(ref, ref, sibling, shares[part])
@@ -576,7 +603,7 @@
     swaps = []
     for step in (1, 2, 3):
         there = moved(place, X, step)
-        swaps.append(wires.send(ready.at[there[X]], arrived.at[across], there))
+        swaps.append(group.send(ready.at[there[X]], arrived.at[across], there))
     arrived[across] = ready[across]
     for part in range(3):
         for index in range(4):
@@ -595,6 +622,8 @@
             share(part, rings[2][part].take_far(index))
     for index in (1, 3):
         table_ring.forward(index)
+    group.settle(blocks)
+    wires.settle()
     for part in range(3):
         rings[2][part].settle(blocks.at[pl.ds(0, 32)])
         wires.whole(blocks.at[pl.ds(0, 128)], sibling, shares[part]).wait()
@@ -616,20 +645,20 @@
     loss_ref,
     table_grads,
     pieces,
-    rows_in,
     logits,
-    d_logits,
     stats,
     d_rows,
     d_sibling,
     d_first,
     d_second,
     local_sems,
+    arrange_out,
 ):
     core = place[CORE]
     sibling = moved(place, CORE, 1)
     own, width = head_in_ref.shape
     half_width = width // 2
+    sends = Group(wires, place)
     feature_axes = ((Y, Z), (Z, Y))
     for part in range(2):
         near, far = (place[axis] for axis in feature_axes[part])
@@ -641,14 +670,14 @@
         near_axis, far_axis = feature_axes[part]
         first_rings.append(
             DirectGather(
-                wires,
+                sends,
                 place,
                 near_axis,
                 lambda j, part=part, k=place[far_axis]: pieces.at[part, core, k, j],
             )
         )
         second_rings.append(
-            DirectGather(wires, place, far_axis, lambda j, part=part: pieces.at[part, core, j])
+            DirectGather(sends, place, far_axis, lambda j, part=part: pieces.at[part, core, j])
         )
     for ring in first_rings:
         ring.start()
@@ -674,28 +703,51 @@
         preferred_element_type=jnp.float32,
     )
     counted = (laid_end_to_end(at_ref[...]) < lengths).astype(jnp.float32)
-    wires.settle(12)
+    for index in range(8):
+        arrange_out(index)
     for ring, later in zip(first_rings, second_rings):
         ring.finish()
         later.start()
+    for index in range(8, 16):
+        arrange_out(index)
     crossing = []
     for part in range(2):
         second_rings[part].finish()
         mine = pieces.at[part, core]
-        crossing.append(wires.send(mine, mine, sibling))
+        crossing.append(sends.send(mine, mine, sibling))
     for copy in crossing:
         copy.wait_recv()
-    for index in range(32):
-        at_z, at_y, at_core = index // 8, index // 2 % SIDE, index % 2
-        rows_in[own * index : own * (index + 1), :half_width] = pieces[0, at_core, at_z, at_y]
-        rows_in[own * index : own * (index + 1), half_width:] = pieces[1, at_core, at_y, at_z]
-
     for index in range(4):
         table_ring.take(index)
         table_ring.take_far(index)
     table_ring.settle(table.at[0])
     groups, rows, group_width = table.shape
-    count = rows_in.shape[0]
+    count = own * N_VOCAB
+    exp_sums, hit_sums = groups * rows, groups * (rows + count)
+    rows_first = groups * (rows + 2 * count)
+    for index in range(N_VOCAB):
+        at_z, at_y, at_core = index // 8, index // 2 % SIDE, index % 2
+        halves = (pieces[0, at_core, at_z, at_y], pieces[1, at_core, at_y, at_z])
+        for group in range(groups):
+            column = group % 2 * group_width
+            table_grads[pl.ds(rows_first + group * count + own * index, own)] = halves[group // 2][
+                :, column : column + group_width
+            ]
+
+    def rows_in(group):
+        return table_grads[pl.ds(rows_first + group * count, count)]
+
+    half_count = count // 2
+    lowered_first = groups * (rows + 3 * count)
+
+    def lower(index, values):
+        values = values.astype(jnp.bfloat16)
+        for side in range(2):
+            first = pl.multiple_of(lowered_first + side * rows + index * chunk, 16)
+            table_grads[pl.ds(first, chunk)] = values[
+                :, side * half_count : (side + 1) * half_count
+            ]
+
     chunk = rows // 4
     base = lax.axis_index("vocab") * rows
     row_iota = lax.broadcasted_iota(jnp.int32, (chunk, count), 0)
@@ -706,7 +758,7 @@
         for group in range(groups):
             total += lax.dot_general(
                 table[group, at],
-                rows_in[:, group * group_width : (group + 1) * group_width],
+                rows_in(group),
                 (((1,), (1,)), ((), ())),
                 preferred_element_type=jnp.float32,
             )
@@ -726,6 +778,7 @@
         pick += jnp.sum(jnp.where(hits, values, 0.0), 0, keepdims=True)
         values = jnp.exp(values - local_top)
         logits[at] = values
+        lower(index, values)
         return total + jnp.sum(values, 0, keepdims=True), pick
 
     zero_row = jnp.zeros((1, count), jnp.float32)
@@ -735,9 +788,25 @@
     total = jnp.concatenate([local_total[:, lanes * i : lanes * (i + 1)] for i in range(4)], 0)
     mine = stats.at[lax.axis_index("vocab")]
     mine[...] = jnp.concatenate([top, total], 0)
-    bundle = wires.slot()
+    bundle = wires.bundle()
     for other in vocab_group:
         wires.send_all(mine, mine, other, bundle)
+    def table_products(first):
+        for side in range(2):
+            lowered = table_grads[pl.ds(lowered_first + side * rows, rows)]
+            for group in range(groups):
+                product = dot_tn(lowered, table[group]).astype(jnp.bfloat16)
+                at = pl.ds(first + group * count + half_count * side, half_count)
+                table_grads[at] = product
+
+    table_products(exp_sums)
+
+    @pl.loop(0, 4)
+    def _(index):
+        hits = row_iota + (base + index * chunk) == target
+        lower(index, jnp.where(hits, 1.0, 0.0))
+
+    table_products(hit_sums)
     wires.whole(stats.at[pl.ds(0, len(vocab_group))], sibling, bundle).wait()
     top = jnp.max(stats[:, :4], 0)
     total = jnp.sum(stats[:, 4:] * jnp.exp(stats[:, :4] - top[None]), 0)
@@ -748,31 +817,29 @@
     weight = counted / (N_DP * N_VOCAB * own)
     scale = jnp.exp(local_top - log_total) * weight
 
-    @pl.loop(0, 4)
-    def _(index):
-        at = pl.ds(pl.multiple_of(index * chunk, chunk), chunk)
-        hits = row_iota + (base + index * chunk) == target
-        d_logits[at] = (logits[at] * scale - jnp.where(hits, weight, 0.0)).astype(jnp.bfloat16)
-
-    for side in range(2):
-        lowered = d_logits[:, 256 * side : 256 * (side + 1)]
+    def down_rows(values, index):
+        return jnp.transpose(
+            jnp.broadcast_to(values[:, 128 * index : 128 * index + 128], (128, 128))
+        )
+
+    for tile in range(count // 128):
+        tile_scale = jnp.concatenate([down_rows(scale, tile)] * 2, 1)
+        tile_weight = jnp.concatenate([down_rows(weight, tile)] * 2, 1)
         for group in range(groups):
-            rows_grad = lax.dot_general(
-                lowered,
-                table[group],
-                (((0,), (0,)), ((), ())),
-                preferred_element_type=jnp.float32,
-            ).astype(jnp.bfloat16)
+            at = group * count + 128 * tile
+            exp_part = table_grads[pl.ds(exp_sums + at, 128)].astype(jnp.float32)
+            hit_part = table_grads[pl.ds(hit_sums + at, 128)].astype(jnp.float32)
+            rows_grad = (exp_part * tile_scale - hit_part * tile_weight).astype(jnp.bfloat16)
             part, column = group // 2, group % 2 * group_width
-            for index in range(16):
-                inner = 16 * side + index
+            for index in range(128 // own):
+                inner = 128 // own * tile + index
                 at_z, at_y, at_core = inner // 8, inner // 2 % SIDE, inner % 2
                 first, second = (at_z, at_y) if part == 0 else (at_y, at_z)
                 d_rows[part, at_core, first, second, :, column : column + group_width] = (
                     rows_grad[own * index : own * (index + 1)]
                 )
     crossing = [
-        wires.send(d_rows.at[part, 1 - core], d_sibling.at[part], sibling) for part in range(2)
+        sends.send(d_rows.at[part, 1 - core], d_sibling.at[part], sibling) for part in range(2)
     ]
     reduce_axes = ((Z, Y), (Y, Z))
     first_rings, second_rings = [], []
@@ -783,7 +850,7 @@
             add_blocks(d_rows.at[part, core, j], [d_sibling.at[part, j]], 4)
         first_rings.append(
             DirectReduce(
-                wires,
+                sends,
                 place,
                 first_axis,
                 lambda j, part=part: d_rows.at[part, core, j],
@@ -793,7 +860,7 @@
         )
         second_rings.append(
             DirectReduce(
-                wires,
+                sends,
                 place,
                 second_axis,
                 lambda j, part=part, k=place[first_axis]: d_rows.at[part, core, k, j],
@@ -805,15 +872,24 @@
 
     stores = []
 
+    @pl.loop(0, 4)
+    def _(index):
+        at = pl.ds(pl.multiple_of(index * chunk, chunk), chunk)
+        hits = row_iota + (base + index * chunk) == target
+        lower(index, logits[at] * scale - jnp.where(hits, weight, 0.0))
+
     def table_grad(group):
         @pl.loop(0, 4)
         def _(index):
-            at = pl.ds(pl.multiple_of(index * chunk, chunk), chunk)
-            product = jnp.dot(
-                d_logits[at],
-                rows_in[:, group * group_width : (group + 1) * group_width],
-                preferred_element_type=jnp.float32,
-            ).astype(jnp.bfloat16)
+            product = jnp.zeros((chunk, group_width), jnp.float32)
+            for side in range(2):
+                first = pl.multiple_of(lowered_first + side * rows + index * chunk, 16)
+                product += jnp.dot(
+                    table_grads[pl.ds(first, chunk)],
+                    rows_in(group)[side * half_count : (side + 1) * half_count],
+                    preferred_element_type=jnp.float32,
+                )
+            product = product.astype(jnp.bfloat16)
             table_grads[pl.ds(pl.multiple_of(group * rows + index * chunk, chunk), chunk)] = product
 
         at = pl.ds(group * rows, rows)
@@ -829,7 +905,6 @@
         later.start()
     table_grad(2)
     table_grad(3)
-    wires.settle(6)
     for part in range(2):
         second_rings[part].arrive()
         first_axis, second_axis = reduce_axes[part]
@@ -837,7 +912,30 @@
         for step in range(3):
             total += d_second[part, step].astype(jnp.float32)
         d_head_ref[:, part * half_width : (part + 1) * half_width] = total
-    return stores
+    return stores, sends
+
+
+def split(values):
+    high = values.astype(jnp.bfloat16)
+    return high, (values - high.astype(jnp.float32)).astype(jnp.bfloat16)
+
+
+def fine_dot(left, right, contract=((1,), (0,))):
+    (left_high, left_low), (right_high, right_low) = split(left), split(right)
+
+    def product(one, other):
+        return lax.dot_general(
+            one, other, (contract, ((), ())), preferred_element_type=jnp.float32
+        )
+
+    return product(left_high, right_high) + (
+        product(left_high, right_low) + product(left_low, right_high)
+    )
+
+
+def clip_for(squares):
+    norm = jnp.sqrt(jnp.full((1, 128), squares, jnp.float32))
+    return norm, CLIP_LEVEL / jnp.maximum(norm, CLIP_LEVEL)
 
 
 def finish_kernel(
@@ -845,12 +943,23 @@
     small_ref,
     head_grad_ref,
     d_embed_ref,
+    left_roots_ref,
     ids_ref,
     loss_ref,
+    grads_out_target,
+    table_grad_target,
+    final_target,
+    left_gram_target,
+    right_gram_target,
+    left_part_target,
+    totals_ref,
     grads_out_ref,
     table_grad_ref,
     final_ref,
-    totals_ref,
+    left_gram,
+    right_gram,
+    left_part,
+    left_roots,
     sums,
     sibling_in,
     half_a,
@@ -878,6 +987,11 @@
     across = place[X]
     sibling = moved(place, CORE, 1)
     wires = Wires(send_sems, recv_sems)
+    to_sibling, to_owners, to_table, later_sends = (Group(wires, place) for _ in range(4))
+
+    def sums_at(part, k3, first, count):
+        return sums.at[pl.ds((SIDE * part + k3) * 32 + first, count)]
+
     loads = []
 
     def load(source, target):
@@ -885,15 +999,6 @@
         copy.start()
         loads.append(copy)
         return copy
-
-    third = [place[ORDERS[part][2]] for part in range(3)]
-    small_load = load(small_ref.at[core], small_sums)
-    block_loads = {}
-    for step in (2, 1, 3, 0):
-        for part in range(3):
-            j = (third[part] + step) % SIDE
-            block_loads[part, step] = load(grads_ref.at[part, core, j], sums.at[part, j])
-    table_load = load(head_grad_ref, table_sums)
 
     width = table_grad_ref.shape[1]
     embed_axes = ((Y, Z), (Z, Y))
@@ -902,7 +1007,17 @@
     far = place[Z] * (1 - source_part) + place[Y] * source_part
     landing = embeds.at[source_part, core, far, 2 * near + across % 2]
     own_columns = pl.ds(pl.multiple_of(across * width, width), width)
-    landing[...] = d_embed_ref[:, own_columns]
+    embed_load = load(d_embed_ref.at[:, own_columns], landing)
+    third = [place[ORDERS[part][2]] for part in range(3)]
+    small_load = load(small_ref.at[core], small_sums)
+    block_loads = {}
+    for step in (2, 1, 3, 0):
+        for part in range(3):
+            j = (third[part] + step) % SIDE
+            block_loads[part, step] = load(grads_ref.at[part, core, j], sums_at(part, j, 0, 32))
+    table_load = load(head_grad_ref, table_sums)
+    roots_load = load(left_roots_ref, left_roots)
+
     ids_all[across] = ids_ref[...]
     line = [
         moved(moved(place, X, step), CORE, side) for step in range(SIDE) for side in range(2)
@@ -927,14 +1042,14 @@
             source, target = grads_ref.at[part, 1 - core, j], sibling_in.at[part, j]
             if half is not None:
                 source, target = source.at[pl.ds(16 * half, 16)], target.at[pl.ds(16 * half, 16)]
-            crossings[part, step, half] = wires.send(source, target, sibling)
+            crossings[part, step, half] = to_sibling.send(source, target, sibling)
 
     embed_first, embed_second = [], []
     for part in range(2):
         near_axis, far_axis = embed_axes[part]
         embed_first.append(
             RingGather(
-                wires,
+                to_owners,
                 place,
                 near_axis,
                 lambda j, part=part, k=place[far_axis]: embeds.at[part, core, k, pl.ds(2 * j, 2)],
@@ -945,7 +1060,7 @@
         )
         embed_second.append(
             RingGather(
-                wires,
+                later_sends,
                 place,
                 far_axis,
                 lambda j, part=part: embeds.at[part, core, j],
@@ -956,25 +1071,25 @@
     for part in range(3):
 
         def at(k3, first, count, part=part):
-            return sums.at[part, k3, pl.ds(first, count)]
+            return sums_at(part, k3, first, count)
 
         last_axis, middle_axis, first_axis = ORDERS[part]
         piece, half = block_ring(place, part, 2, at)
         first_rings.append(
             QuarterReduce(
-                wires, place, first_axis, piece, half, 32, half_a.at[part], whole_a.at[part]
+                to_owners, place, first_axis, piece, half, 32, half_a.at[part], whole_a.at[part]
             )
         )
         piece, half = block_ring(place, part, 1, at)
         middle_rings.append(
             RingReduce(
-                wires, place, middle_axis, piece, half, 8, half_b.at[part], whole_b.at[part]
+                later_sends, place, middle_axis, piece, half, 8, half_b.at[part], whole_b.at[part]
             )
         )
         piece, _ = block_ring(place, part, 0, at)
-        last_rings.append(DirectReduce(wires, place, last_axis, piece, 2, whole_c.at[part]))
+        last_rings.append(DirectReduce(later_sends, place, last_axis, piece, 2, whole_c.at[part]))
     table_ring = QuarterReduce(
-        wires,
+        to_table,
         place,
         X,
         lambda j: table_sums.at[j],
@@ -998,16 +1113,15 @@
         if not half:
             block_loads[part, step].wait()
         crossings[part, step, half].wait_recv()
-        at = pl.ds(0, 32) if half is None else pl.ds(16 * half, 16)
-        add_blocks(
-            sums.at[part, j, at], [sibling_in.at[part, j, at]], 32 if half is None else 16
-        )
+        first, count = (0, 32) if half is None else (16 * half, 16)
+        landed = sibling_in.at[part, j, pl.ds(first, count)]
+        add_blocks(sums_at(part, j, first, count), [landed], count)
 
     embed_siblings = []
 
     def share(part, step):
         piece = embeds.at[part, core, (place[embed_axes[part][1]] + step) % SIDE]
-        embed_siblings.append(wires.send(piece, piece, sibling))
+        embed_siblings.append(later_sends.send(piece, piece, sibling))
 
     rows = table_grad_ref.shape[0]
     chunk = rows // 4
@@ -1057,6 +1171,7 @@
         first_rings[part].start(0)
     for copy in swaps:
         copy.wait_recv()
+    embed_load.wait()
     for ring in embed_first:
         ring.start()
     table_load.wait()
@@ -1121,7 +1236,7 @@
     for part in range(2):
         scatter_rows(part, 1 - core, 1)
         scatter_rows(part, 1 - core, 3)
-    wires.settle(32)
+    to_sibling.settle(sums)
     for ring, later in zip(first_rings, middle_rings):
         ring.finish()
         later.start()
@@ -1146,6 +1261,8 @@
     for copy in embed_siblings:
         copy.wait_recv()
     scatter_rows(0, 1 - core, 2)
+    to_owners.settle(sums)
+    wires.settle(6)
     for ring, later in zip(middle_rings, last_rings):
         ring.finish()
         later.start()
@@ -1169,12 +1286,13 @@
     for index in range(4):
         values = table_grad_ref[index * chunk : (index + 1) * chunk]
         table_squares += jnp.sum(values * values, 0, keepdims=True)
-    squares = table_squares[:, :128] + table_squares[:, 128:]
+    squares = jnp.zeros((1, 128), jnp.float32)
+    to_table.settle(sums)
     for part in range(3):
         last_rings[part].arrive()
         k1, k2, k3 = (place[axis] for axis in ORDERS[part])
         for which in range(2):
-            total = sums[part, k3, 8 * k2 + 2 * k1 + which].astype(jnp.float32)
+            total = sums_at(part, k3, 8 * k2 + 2 * k1 + which, 1)[0].astype(jnp.float32)
             for step in range(3):
                 total += whole_c[part, step, which].astype(jnp.float32)
             grads_out_ref[part, which] = total
@@ -1184,27 +1302,54 @@
         gathers[2][part].finish()
         mine = final_ref.at[part, core]
         final_siblings.append(wires.send(mine, mine, sibling))
+    stores = []
+
+    def store(source, target):
+        stores.append(pltpu.make_async_copy(source, target, local_sems.at[17 + len(stores)]))
+        stores[-1].start()
+
+    own_clip = clip_for(jnp.sum(squares))[1]
+    squares += table_squares[:, :128] + table_squares[:, 128:]
+    roots_load.wait()
+
+    def products(slots):
+        for slot in slots:
+            grad = grads_out_ref[slot // 2, slot % 2] * own_clip
+            left_gram[slot] = fine_dot(grad, grad, ((1,), (1,)))
+            right_gram[slot] = fine_dot(grad, grad, ((0,), (0,)))
+            left_part[slot] = fine_dot(left_roots[slot], grad)
+
+    store(table_grad_ref, table_grad_target)
+    store(grads_out_ref, grads_out_target)
     loss = sum(loss_ref[:, 128 * index : 128 * (index + 1)] for index in range(4))
     totals = jnp.concatenate([squares, loss, jnp.zeros((6, 128), jnp.float32)], 0)
+    for copy in final_siblings:
+        copy.wait_recv()
+    store(final_ref, final_target)
     for phase, (own, others) in enumerate(
         ((2 * across + core, line), (SIDE * place[Z] + place[Y], plane))
     ):
         mine = totals_all.at[phase, own]
         mine[...] = totals
-        bundle = wires.slot()
+        bundle = wires.bundle()
         for other in others:
             wires.send_all(mine, mine, other, bundle)
+        products(range(3 * phase, 3 * phase + 3))
         wires.whole(totals_all.at[phase, pl.ds(0, len(others))], sibling, bundle).wait()
         totals = totals_all[phase, 0]
         for index in range(1, len(others) + 1):
             totals += totals_all[phase, index]
     totals_ref[...] = totals
-    for copy in final_siblings:
-        copy.wait_recv()
+    store(left_gram, left_gram_target)
+    store(right_gram, right_gram_target)
+    store(left_part, left_part_target)
+    later_sends.settle(sums)
     wires.settle()
-
-
-def finish_call(grads, small, head_grad, d_embed, token_ids, loss_row):
+    for copy in stores:
+        copy.wait()
+
+
+def finish_call(grads, small, head_grad, d_embed, left_roots, token_ids, loss_row):
     bf16 = jnp.bfloat16
     _, chunks, chunk_rows, width = head_grad.shape
     rows = chunks * chunk_rows
@@ -1216,12 +1361,17 @@
             jax.ShapeDtypeStruct((3, 2) + block, jnp.float32),
             jax.ShapeDtypeStruct((rows, width), jnp.float32),
             jax.ShapeDtypeStruct((2, 2, SIDE, SIDE, SIDE, 8, 128), jnp.float32),
+            *[jax.ShapeDtypeStruct(left_roots.shape, jnp.float32)] * 3,
             jax.ShapeDtypeStruct((8, 128), jnp.float32),
         ),
-        in_specs=[ANY] * 3 + [VMEM] * 3,
-        out_specs=(VMEM,) * 4,
+        in_specs=[ANY] * 5 + [VMEM] * 2,
+        out_specs=(ANY,) * 6 + (VMEM,),
         scratch_shapes=[
-            pltpu.VMEM((3, SIDE, 32) + block, bf16),
+            pltpu.VMEM((3, 2) + block, jnp.float32),
+            pltpu.VMEM((rows, width), jnp.float32),
+            pltpu.VMEM((2, 2, SIDE, SIDE, SIDE, 8, 128), jnp.float32),
+            *[pltpu.VMEM(left_roots.shape, jnp.float32)] * 4,
+            pltpu.VMEM((3 * SIDE * 32,) + block, bf16),
             pltpu.VMEM((3, SIDE, 32) + block, bf16),
             pltpu.VMEM((3, 2, 16) + block, bf16),
             pltpu.VMEM((3, 2, 32) + block, bf16),
@@ -1239,14 +1389,14 @@
             pltpu.VMEM((2, 2, SIDE, 8, 128, width), bf16),
             pltpu.VMEM((N_DP,) + token_ids.shape, jnp.int32),
             pltpu.VMEM((2, SIDE * SIDE, 8, 128), jnp.float32),
-            pltpu.SemaphoreType.DMA((160,)),
-            pltpu.SemaphoreType.DMA((160,)),
-            pltpu.SemaphoreType.DMA((17,)),
+            pltpu.SemaphoreType.DMA((42,)),
+            pltpu.SemaphoreType.DMA((146,)),
+            pltpu.SemaphoreType.DMA((23,)),
         ],
         compiler_params=pltpu.CompilerParams(
             collective_id=3, has_side_effects=True, vmem_limit_bytes=VMEM_BYTES
         ),
-    )(grads, small, head_grad, d_embed, token_ids, loss_row)
+    )(grads, small, head_grad, d_embed, left_roots, token_ids, loss_row)
 
 
 def row_mean(values):
@@ -1436,22 +1586,24 @@
     target_ref,
     at_ref,
     length_ref,
-    matrices_ref,
-    table_ref,
-    positions_ref,
-    vec_ref,
-    full_ref,
-    hidden_ref,
-    query_ref,
-    kv_ref,
-    probs_ref,
-    attended_ref,
-    middle_ref,
-    pre_act_ref,
-    last_ref,
-    d_head_ref,
-    table_grad_ref,
-    loss_ref,
+    *refs,
+):
+    sources, refs = refs[:4], refs[4:]
+    (full_ref, out_blocks_ref), targets, refs = refs[:2], refs[2:10], refs[10:]
+    (d_head_ref, table_grad_ref, loss_ref), refs = refs[:3], refs[3:]
+    held, kept, refs = refs[:4], refs[4:12], refs[12:]
+    matrices_ref, table_ref, positions_ref, vec_ref = held
+    (
+        hidden_ref,
+        query_ref,
+        kv_ref,
+        probs_ref,
+        attended_ref,
+        middle_ref,
+        pre_act_ref,
+        last_ref,
+    ) = kept
+    (
     blocks,
     table,
     own_low,
@@ -1468,20 +1620,25 @@
     activated,
     head_in,
     pieces,
-    rows_in,
     logits,
-    d_logits,
     stats,
     d_rows,
     d_sibling,
     d_first,
     d_second,
+    out_staging,
     send_sems,
     recv_sems,
     local_sems,
-):
+    ) = refs
     place = coordinates()
     wires = Wires(send_sems, recv_sems)
+    loads = [
+        pltpu.make_async_copy(source, target, local_sems.at[5 + index])
+        for index, (source, target) in enumerate(zip(sources, held))
+    ]
+    for copy in loads:
+        copy.start()
     vocab_group = [
         moved(moved(moved(place, Y, near), Z, far), CORE, side)
         for near in range(SIDE)
@@ -1490,6 +1647,8 @@
     ][1:]
     others = vocab_group + [moved(place, X, step) for step in (1, 2, 3)]
     greet(others)
+    for copy in loads:
+        copy.wait()
     table_ring = gather_phase(
         place,
         wires,
@@ -1533,7 +1692,26 @@
         normed_rows,
         activated,
     )
-    stores = head_phase(
+    keeps = [keep]
+    for index, (source, target) in enumerate(zip(kept, targets)):
+        keeps.append(pltpu.make_async_copy(source, target, local_sems.at[9 + index]))
+        keeps[-1].start()
+
+    def arrange_out(chunk):
+        if chunk >= 2:
+            keeps[len(keeps) - 2].wait()
+            del keeps[len(keeps) - 2]
+        slot = out_staging.at[chunk % 2]
+
+        @pl.loop(0, 16, unroll=4)
+        def _(index):
+            slot[index] = blocks[where_ref[OUT[0] + 16 * chunk + index]]
+
+        target = out_blocks_ref.at[pl.ds(16 * chunk, 16)]
+        keeps.append(pltpu.make_async_copy(slot, target, local_sems.at[17 + chunk % 2]))
+        keeps[-1].start()
+
+    stores, sends = head_phase(
         place,
         wires,
         vocab_group,
@@ -1548,19 +1726,17 @@
         loss_ref,
         parts,
         pieces,
-        rows_in,
         logits,
-        d_logits,
         stats,
         d_rows,
         d_sibling,
         d_first,
         d_second,
         local_sems,
-    )
-    wires.settle()
-    keep.wait()
-    for copy in stores:
+        arrange_out,
+    )
+    sends.settle(blocks)
+    for copy in keeps + stores:
         copy.wait()
 
 
@@ -1573,27 +1749,33 @@
     bf16, f32 = jnp.bfloat16, jnp.float32
     shape = jax.ShapeDtypeStruct
     slots = where.shape[0]
+    cache = (
+        shape((seq_len, D), f32),
+        shape((own, D), bf16),
+        shape((seq_len, 2 * D), bf16),
+        shape((HEADS * own, seq_len), f32),
+        shape((own, D), bf16),
+        shape((own, D), f32),
+        shape((own, FF), f32),
+        shape((own, D), f32),
+    )
+    states = (matrices, vocab_table, positions_table, vectors)
     smem = pl.BlockSpec(memory_space=pltpu.SMEM)
     return pl.pallas_call(
         forward_kernel,
         name="forward_and_head",
         out_shape=(
             shape((slots, BLOCK, BLOCK), bf16),
-            shape((seq_len, D), f32),
-            shape((own, D), bf16),
-            shape((seq_len, 2 * D), bf16),
-            shape((HEADS * own, seq_len), f32),
-            shape((own, D), bf16),
-            shape((own, D), f32),
-            shape((own, FF), f32),
-            shape((own, D), f32),
+            shape((slots // 3, BLOCK, BLOCK), bf16),
+            *cache,
             shape((own, D), f32),
             shape((N_DP * rows, width), bf16),
             shape((1, count), f32),
         ),
-        in_specs=[smem] * 3 + [VMEM] * 8,
-        out_specs=(ANY,) + (VMEM,) * 9 + (ANY, VMEM),
+        in_specs=[smem] * 3 + [VMEM] * 4 + [ANY] * 4,
+        out_specs=(ANY,) * 10 + (VMEM, ANY, VMEM),
         scratch_shapes=[
+            *[pltpu.VMEM(array.shape, array.dtype) for array in (*states, *cache)],
             pltpu.VMEM((slots, BLOCK, BLOCK), bf16),
             pltpu.VMEM((N_DP, rows, width), bf16),
             pltpu.VMEM((3, 2, BLOCK, BLOCK), bf16),
@@ -1610,17 +1792,16 @@
             pltpu.VMEM((own, FF), bf16),
             pltpu.VMEM((own, D), bf16),
             pltpu.VMEM((2, 2, SIDE, SIDE, own, half), bf16),
-            pltpu.VMEM((count, D), bf16),
             pltpu.VMEM((rows, count), f32),
-            pltpu.VMEM((rows, count), bf16),
             pltpu.VMEM((N_VOCAB, 8, count // 4), f32),
             pltpu.VMEM((2, 2, SIDE, SIDE, own, half), bf16),
             pltpu.VMEM((2, SIDE, SIDE, own, half), bf16),
             pltpu.VMEM((2, 3, SIDE, own, half), bf16),
             pltpu.VMEM((2, 3, own, half), bf16),
-            pltpu.SemaphoreType.DMA((200,)),
-            pltpu.SemaphoreType.DMA((200,)),
-            pltpu.SemaphoreType.DMA((5,)),
+            pltpu.VMEM((2, 16, BLOCK, BLOCK), bf16),
+            pltpu.SemaphoreType.DMA((21,)),
+            pltpu.SemaphoreType.DMA((123,)),
+            pltpu.SemaphoreType.DMA((19,)),
         ],
         compiler_params=pltpu.CompilerParams(
             collective_id=1, has_side_effects=True, vmem_limit_bytes=VMEM_BYTES
@@ -1633,10 +1814,7 @@
         target_ids,
         positions,
         lengths.reshape(1, -1),
-        matrices,
-        vocab_table,
-        positions_table,
-        vectors,
+        *states,
     )
 
 
@@ -1650,19 +1828,24 @@
     where_ref,
     at_ref,
     full_ref,
-    hidden_ref,
-    vec_ref,
-    query_ref,
-    kv_ref,
-    probs_ref,
-    attended_ref,
-    middle_ref,
-    pre_act_ref,
-    last_ref,
-    d_head_ref,
-    grads_ref,
-    small_ref,
-    d_embed_ref,
+    out_blocks_ref,
+    *refs,
+):
+    sources, (grads_ref, small_ref, d_embed_ref), refs = refs[:10], refs[10:13], refs[13:]
+    held, refs = refs[:10], refs[10:]
+    (
+        d_head_ref,
+        last_ref,
+        vec_ref,
+        pre_act_ref,
+        middle_ref,
+        attended_ref,
+        query_ref,
+        kv_ref,
+        probs_ref,
+        hidden_ref,
+    ) = held
+    (
     blocks,
     grad_blocks,
     activated,
@@ -1675,8 +1858,19 @@
     vec_grads,
     sems,
     grad_sem,
-):
+    ) = refs
+    loads = [
+        pltpu.make_async_copy(source, target, sems.at[9 + index])
+        for index, (source, target) in enumerate(zip(sources, held))
+    ]
+    for copy in loads:
+        copy.start()
+    out_blocks = grad_blocks.at[pl.ds(0, out_blocks_ref.shape[0])]
+    out_load = pltpu.make_async_copy(out_blocks_ref, out_blocks, sems.at[8])
+    out_load.start()
     copies = load_blocks(full_ref, blocks, sems)
+    for copy in loads:
+        copy.wait()
     count = d_head_ref.shape[0]
     bf16 = jnp.bfloat16
     own = lax.axis_index("vocab")
@@ -1708,13 +1902,18 @@
     vec_grads[11:12] = jnp.sum(d_branch.astype(jnp.float32), 0, keepdims=True)
     activated[...] = gelu(pre_act_ref[...]).astype(bf16)
     weight_grad(OUT, 32, activated, d_branch)
-    for copy in copies:
-        copy.wait()
+    out_load.wait()
 
     @pl.loop(0, 16)
     def _(tile):
         at = lane_range(256 * tile, 256)
-        weight = weight_tiles(blocks, where_ref, OUT, 2 * tile, 2, 0, 8)
+        weight = jnp.concatenate(
+            [
+                jnp.concatenate([out_blocks[16 * tile + 8 * row + j] for j in range(8)], 1)
+                for row in range(2)
+            ],
+            0,
+        )
         lowered = (dot_nt(d_branch, weight) * gelu_slope(pre_act_ref[:, at])).astype(bf16)
         d_pre[:, at] = lowered
         vec_grads[pl.ds(7 + tile // 4, 1), lane_range(256 * (tile % 4), 256)] = jnp.sum(
@@ -1725,6 +1924,8 @@
     normed[pl.ds(0, count)] = (hat * vec_ref[5:6] + vec_ref[6:7]).astype(bf16)
     weight_grad(FC, 8, normed.at[pl.ds(0, count)], d_pre[...])
     rows_out[...] = jnp.zeros(rows_out.shape, jnp.float32)
+    for copy in copies:
+        copy.wait()
 
     @pl.loop(0, 16)
     def _(index):
@@ -1805,8 +2006,9 @@
     pltpu.make_async_copy(grad_blocks, grads_ref, grad_sem).wait()
 
 
-def backward_call(where, positions, full, hidden, vectors, cache, d_head):
+def backward_call(where, positions, full, out_blocks, states):
     count = positions.shape[0]
+    hidden = states[-1]
     bf16 = jnp.bfloat16
     shape = jax.ShapeDtypeStruct
     return pl.pallas_call(
@@ -1820,9 +2022,10 @@
         grid_spec=pltpu.PrefetchScalarGridSpec(
             num_scalar_prefetch=2,
             grid=(),
-            in_specs=[ANY] + [VMEM] * 10,
+            in_specs=[ANY] * 12,
             out_specs=(ANY, VMEM, VMEM),
             scratch_shapes=[
+                *[pltpu.VMEM(array.shape, array.dtype) for array in states],
                 pltpu.VMEM(full.shape, bf16),
                 pltpu.VMEM(full.shape, bf16),
                 pltpu.VMEM((count, FF), bf16),
@@ -1833,12 +2036,12 @@
                 pltpu.VMEM(hidden.shape, jnp.float32),
                 pltpu.VMEM((count, D), jnp.float32),
                 pltpu.VMEM((16, D), jnp.float32),
-                pltpu.SemaphoreType.DMA((8,)),
+                pltpu.SemaphoreType.DMA((19,)),
                 pltpu.SemaphoreType.DMA,
             ],
         ),
         compiler_params=pltpu.CompilerParams(vmem_limit_bytes=VMEM_BYTES),
-    )(where, positions, full, hidden, vectors, *cache, d_head)
+    )(where, positions, full, out_blocks, *states)
 
 
 def adam_step(weight, moment_one, moment_two, grad_in, rate, decay):
@@ -1852,80 +2055,66 @@
     return weight - rate * change, new_one, new_two
 
 
-def high_dot(left, right, contract=((1,), (0,))):
-    return lax.dot_general(
-        left, right, (contract, ((), ())), precision=HIGH, preferred_element_type=jnp.float32
-    )
+TABLE_PIECES = 2
 
 
 def update_kernel(*refs):
-    names = 18
+    names = 20
     sources, (loss_ref, norm_ref, *targets) = refs[:names], refs[names : names + 15]
     buffers = refs[names + 15 : 2 * names + 15]
     results = refs[2 * names + 15 : 2 * names + 28]
     vec_grad, load_sems, store_sems = refs[2 * names + 28 :]
-    loads = [
-        pltpu.make_async_copy(source, buffer, load_sems.at[index])
-        for index, (source, buffer) in enumerate(zip(sources, buffers))
-    ]
-    for copy in loads:
-        copy.start()
-    stores = []
+    loads, stores = [], []
+
+    def load(index, at=None):
+        source, target = sources[index], buffers[index]
+        if at is not None:
+            source, target = source.at[at], target.at[at]
+        loads.append(pltpu.make_async_copy(source, target, load_sems.at[len(loads)]))
+        loads[-1].start()
 
     def store(index, at=None):
         source, target = results[index], targets[index]
         if at is not None:
             source, target = source.at[at], target.at[at]
-        copy = pltpu.make_async_copy(source, target, store_sems.at[len(stores)])
-        copy.start()
-        stores.append(copy)
-
-    totals, final, grads, matrices, left_stats, right_stats, left_roots, right_roots = buffers[:8]
-    table_grad, table, table_m, table_v = buffers[8:12]
-    positions, pos_m, pos_v, vectors, vectors_m, vectors_v = buffers[12:]
+        stores.append(pltpu.make_async_copy(source, target, store_sems.at[len(stores)]))
+        stores[-1].start()
+
+    def await_loads(count):
+        for copy in loads[:count]:
+            copy.wait()
+        del loads[:count]
+
+    totals, final, table_grad, table, table_m, table_v = buffers[:6]
+    grads, left_gram, right_gram, left_part = buffers[6:10]
+    matrices, left_stats, right_stats, right_roots = buffers[10:14]
+    positions, pos_m, pos_v, vectors, vectors_m, vectors_v = buffers[14:]
     matrices_new, left_new, right_new, matrices_grad = results[:4]
-    for copy in loads[:2]:
-        copy.wait()
+    rows, width = table.shape
+    chunk = rows // TABLE_PIECES
+    for index in range(2):
+        load(index)
+    for piece in range(TABLE_PIECES):
+        for index in range(2, 6):
+            load(index, pl.ds(piece * chunk, chunk))
+    for index in range(6, names):
+        load(index)
+    await_loads(2)
     row_squares = jnp.zeros((8, 128), jnp.float32)
     for part in range(2):
         for core in range(2):
             values = final[part, core].reshape(SIDE**3, 8, 128)
             row_squares += jnp.sum(values * values, 0)
-    squares = jnp.sum(totals[0:1]) + jnp.sum(row_squares)
-    loss = jnp.sum(totals[1:2])
-    norm = jnp.sqrt(jnp.full((1, 128), squares, jnp.float32))
-    clip = CLIP_LEVEL / jnp.maximum(norm, CLIP_LEVEL)
-    loss_ref[0, 0] = loss
+    norm, clip = clip_for(jnp.sum(totals[0:1]) + jnp.sum(row_squares))
+    loss_ref[0, 0] = jnp.sum(totals[1:2])
     norm_ref[0, 0] = jnp.max(norm)
-    for copy in loads[2:8]:
-        copy.wait()
-
-    @pl.loop(0, SLOTS, unroll=3)
-    def _(slot):
-        grad = grads[slot // 2, slot % 2] * clip
-        matrices_grad[slot] = grad
-        left_new[slot] = STAT_DECAY * left_stats[slot] + (1.0 - STAT_DECAY) * high_dot(
-            grad, grad, ((1,), (1,))
-        )
-        right_new[slot] = STAT_DECAY * right_stats[slot] + (1.0 - STAT_DECAY) * high_dot(
-            grad, grad, ((0,), (0,))
-        )
-        stepped = high_dot(high_dot(left_roots[slot], grad), right_roots[slot])
-        weight = matrices[slot]
-        matrices_new[slot] = weight - SHAMPOO_RATE * (stepped + DECAY_RATE * weight)
-
-    for index in range(4):
-        store(index)
-    for copy in loads[8:12]:
-        copy.wait()
-    rows, width = table.shape
     wide_clip = jnp.concatenate([clip] * (width // 128), 1)
-    chunk = rows // 4
-    for index in range(4):
+    for piece in range(TABLE_PIECES):
+        await_loads(4)
 
         @pl.loop(0, chunk // 80)
         def _(inner):
-            at = pl.ds(pl.multiple_of(index * chunk + inner * 80, 80), 80)
+            at = pl.ds(pl.multiple_of(piece * chunk + inner * 80, 80), 80)
             grad = table_grad[at] * wide_clip
             stepped = adam_step(
                 table[at], table_m[at], table_v[at], grad, TABLE_RATE, DECAY_RATE
@@ -1934,9 +2123,31 @@
                 results[4 + order][at] = value
 
         for order in range(3):
-            store(4 + order, pl.ds(index * chunk, chunk))
-    for copy in loads[12:]:
-        copy.wait()
+            store(4 + order, pl.ds(piece * chunk, chunk))
+    await_loads(8)
+    own_squares = jnp.zeros((1, 128), jnp.float32)
+    for slot in range(SLOTS):
+        grad = grads[slot // 2, slot % 2]
+        own_squares += jnp.sum(grad * grad, 0, keepdims=True)
+    own_clip = clip_for(jnp.sum(own_squares))[1]
+    ratio = jnp.where(own_clip > 0.0, clip / own_clip, 0.0)
+
+    @pl.loop(0, SLOTS, unroll=3)
+    def _(slot):
+        matrices_grad[slot] = grads[slot // 2, slot % 2] * clip
+        left_new[slot] = STAT_DECAY * left_stats[slot] + (1.0 - STAT_DECAY) * (
+            left_gram[slot] * ratio * ratio
+        )
+        right_new[slot] = STAT_DECAY * right_stats[slot] + (1.0 - STAT_DECAY) * (
+            right_gram[slot] * ratio * ratio
+        )
+        stepped = fine_dot(left_part[slot] * ratio, right_roots[slot])
+        weight = matrices[slot]
+        matrices_new[slot] = weight - SHAMPOO_RATE * (stepped + DECAY_RATE * weight)
+
+    for index in range(4):
+        store(index)
+    await_loads(6)
     tiles = D // 128
     for index in range(N_DP * N_VOCAB):
         at_core, rest = index // 64, index % 64
@@ -1969,8 +2180,8 @@
         copy.wait()
 
 
-def update_call(totals, final, grads, blocks, table_grad, table, positions, vectors):
-    sources = [totals, final, grads, *blocks, table_grad, *table, *positions, *vectors]
+def update_call(totals, final, grads, products, blocks, table_grad, table, positions, vectors):
+    sources = [totals, final, table_grad, *table, grads, *products, *blocks, *positions, *vectors]
     shape = lambda array: jax.ShapeDtypeStruct(array.shape, jnp.float32)
     targets = [shape(blocks[0])] * 4
     targets += [shape(array) for array in (*table, *positions, *vectors)]
@@ -1986,8 +2197,8 @@
         + [pltpu.VMEM(target.shape, jnp.float32) for target in targets]
         + [
             pltpu.VMEM(vectors[0].shape, jnp.float32),
-            pltpu.SemaphoreType.DMA((len(sources),)),
-            pltpu.SemaphoreType.DMA((len(targets) + 9,)),
+            pltpu.SemaphoreType.DMA((len(sources) + 4 * (TABLE_PIECES - 1),)),
+            pltpu.SemaphoreType.DMA((len(targets) + 3 * (TABLE_PIECES - 1),)),
         ],
         compiler_params=pltpu.CompilerParams(vmem_limit_bytes=VMEM_BYTES),
     )(*sources)
@@ -2036,7 +2247,7 @@
         dtype=jnp.int32,
     )
     positions = loss_positions.T
-    full, hidden, *cache, d_head_in, head_grad, loss_row = forward_call(
+    full, out_blocks, *cache, d_head_in, head_grad, loss_row = forward_call(
         where,
         positions,
         seq_lengths,
@@ -2047,14 +2258,20 @@
         positions_table,
         vectors,
     )
+    hidden, query, key_value, probs, attended, middle, pre_act, last = cache
     grad_blocks, small, d_embed = backward_call(
-        where, positions, full, hidden, vectors, cache, d_head_in
-    )
-    owned_grads, table_grad_own, final, totals = finish_call(
+        where,
+        positions,
+        full,
+        out_blocks,
+        (d_head_in, last, vectors, pre_act, middle, attended, query, key_value, probs, hidden),
+    )
+    owned_grads, table_grad_own, final, *products, totals = finish_call(
         grad_blocks.reshape(3, 2, SIDE, 32, BLOCK, BLOCK),
         small.reshape(2, SIDE, 16, 16, 128),
         head_grad.reshape(N_DP, TABLE_CHUNKS, -1, head_grad.shape[1]),
         d_embed,
+        left_roots,
         token_ids,
         loss_row,
     )
@@ -2062,7 +2279,8 @@
         totals,
         final,
         owned_grads,
-        (matrices, left_stats, right_stats, left_roots, right_roots),
+        products,
+        (matrices, left_stats, right_stats, right_roots),
         table_grad_own,
         (vocab_table, table_m, table_v),
         (positions_table, pos_m, pos_v),

time: 287 us -> 278 us (0.969)
  Pallas kernels: 284 us -> 275 us
    pallas_call x1, Pallas kernels: 137 us -> 131 us  [forward_call(): pl.pallas_call(forward_kernel, name='forward_and_head', out_shape=(shape(...]
    pallas_call x1, Pallas kernels: 36.5 us -> 33.4 us  [backward_call(): pl.pallas_call(backward_kernel, name='layer_backward', out_shape=(shape(f...]
where the time goes in v4:
time: 278 us; the launch traced here: 277 us
  Pallas kernels  275 us (99%)
    pallas_call x1, Pallas kernels, forward_call(): pl.pallas_call(forward_kernel, name='forward_and_head', out_shape=(shape(...  131 us
    pallas_call x1, Pallas kernels, finish_call(): pl.pallas_call(finish_kernel, name='reduce_and_scatter', out_shape=(jax.S...  101 us
    pallas_call x1, Pallas kernels, backward_call(): pl.pallas_call(backward_kernel, name='layer_backward', out_shape=(shape(f...  33.4 us
    pallas_call x1, Pallas kernels, update_call(): pl.pallas_call(update_kernel, name='optimizer_update', out_shape=(scalar,...  8.66 us

profile of v4, /device:TPU:1, one launch (start us, length us, event | category | flops | bytes accessed | tf_op | source)
XLA Modules:
  0.0 277.1 jit_solution(1255557185138941690)
XLA Ops:
  0.6 1.6 select_reduce_fusion.where_ref
  2.3 131.4 %forward_and_head.1 = (bf16[768,128,128]{2,1,0:T(8,128)(2,1)}, bf16[256,128,128]{2,1,0:T(8,128)(2,1)}, f32[128,1024]{1,0:T(8,128)}, bf16[16,1024]{1,0:T(8,128)(2...) custom-call(s32[768]{0:T(1024)} %select_reduce_fusion.where_ref, ...), custom_call_target="tpu_custom_call" | custom-call | tf_op jit(solution)/shard_map/forward_and_head/pallas_call | solution.py:1764
  133.6 33.4 %layer_backward.1 = (bf16[768,128,128]{2,1,0:T(8,128)(2,1)}, bf16[128,16,128]{2,1,0:T(8,128)(2,1)}, bf16[128,1024]{1,0:T(8,128)(2,1)}) custom-call(s32[768]{0:T(1024)} %select_reduce_fusion.where_ref, s32[16,32]{1,0:T(8,128)} %bitcast.13, bf16[768,128,128]{2,1,0:T(8,128)(2,1)} %get-tuple-element.53.full_ref, ...), custom_call_target="tpu_custom_call" | custom-call | tf_op jit(solution)/shard_map/layer_backward/pallas_call | solution.py:2014
  167.0 101.2 %reduce_and_scatter.1 = (f32[3,2,128,128]{3,2,1,0:T(8,128)}, f32[1600,256]{1,0:T(8,128)}, f32[2,2,4,4,4,8,128]{6,5,4,3,2,1,0:T(8,128)}, f32[6,128,128]{2,1,0:T(8...) custom-call(bf16[3,2,4,32,128,128]{5,4,3,2,1,0:T(8,128)(2,1)} %bitcast.8, ...), custom_call_target="tpu_custom_call" | custom-call | tf_op jit(solution)/shard_map/reduce_and_scatter/pallas_call | solution.py:1357
  268.2 8.7 %optimizer_update.1 = (f32[1,1]{1,0:T(1,128)}, f32[1,1]{1,0:T(1,128)}, f32[6,128,128]{2,1,0:T(8,128)}, f32[6,128,128]{2,1,0:T(8,128)}, f32[6,128,128]{2,1,0:T(8,...) custom-call(f32[8,128]{1,0:T(8,128)} %get-tuple-element.69.refs_0_, ...), custom_call_target="tpu_custom_call" | custom-call | tf_op jit(solution)/shard_map/optimizer_update/pallas_call | solution.py:2190

commit v5 on v4

--- a/solution.py
+++ b/solution.py
@@ -653,6 +653,7 @@
     d_second,
     local_sems,
     arrange_out,
+    keeps,
 ):
     core = place[CORE]
     sibling = moved(place, CORE, 1)
@@ -905,6 +906,9 @@
         later.start()
     table_grad(2)
     table_grad(3)
+    for copy in keeps + stores[:3]:
+        copy.wait()
+    del stores[:3]
     for part in range(2):
         second_rings[part].arrive()
         first_axis, second_axis = reduce_axes[part]
@@ -1323,9 +1327,6 @@
     store(grads_out_ref, grads_out_target)
     loss = sum(loss_ref[:, 128 * index : 128 * (index + 1)] for index in range(4))
     totals = jnp.concatenate([squares, loss, jnp.zeros((6, 128), jnp.float32)], 0)
-    for copy in final_siblings:
-        copy.wait_recv()
-    store(final_ref, final_target)
     for phase, (own, others) in enumerate(
         ((2 * across + core, line), (SIDE * place[Z] + place[Y], plane))
     ):
@@ -1335,16 +1336,21 @@
         for other in others:
             wires.send_all(mine, mine, other, bundle)
         products(range(3 * phase, 3 * phase + 3))
+        if phase == 0:
+            for copy in final_siblings:
+                copy.wait_recv()
+            store(final_ref, final_target)
+            later_sends.settle(sums)
+        else:
+            store(left_gram, left_gram_target)
+            store(right_gram, right_gram_target)
+            store(left_part, left_part_target)
+            wires.settle()
         wires.whole(totals_all.at[phase, pl.ds(0, len(others))], sibling, bundle).wait()
         totals = totals_all[phase, 0]
         for index in range(1, len(others) + 1):
             totals += totals_all[phase, index]
     totals_ref[...] = totals
-    store(left_gram, left_gram_target)
-    store(right_gram, right_gram_target)
-    store(left_part, left_part_target)
-    later_sends.settle(sums)
-    wires.settle()
     for copy in stores:
         copy.wait()
 
@@ -1734,9 +1740,10 @@
         d_second,
         local_sems,
         arrange_out,
+        keeps,
     )
     sends.settle(blocks)
-    for copy in keeps + stores:
+    for copy in stores:
         copy.wait()
 
 

time: 278 us -> 275 us (0.989)
  no operation moved by 1% of the time
where the time goes in v5:
time: 275 us
  Pallas kernels  273 us (99%)
    pallas_call x1, Pallas kernels, forward_call(): pl.pallas_call(forward_kernel, name='forward_and_head', out_shape=(shape(...  131 us
    pallas_call x1, Pallas kernels, finish_call(): pl.pallas_call(finish_kernel, name='reduce_and_scatter', out_shape=(jax.S...  99.1 us
    pallas_call x1, Pallas kernels, backward_call(): pl.pallas_call(backward_kernel, name='layer_backward', out_shape=(shape(f...  33.4 us
    pallas_call x1, Pallas kernels, update_call(): pl.pallas_call(update_kernel, name='optimizer_update', out_shape=(scalar,...  8.66 us

profile of v5, /device:TPU:1, one launch (start us, length us, event | category | flops | bytes accessed | tf_op | source)
XLA Modules:
  0.0 275.0 jit_solution(17629971039195621737)
XLA Ops:
  0.6 1.6 select_reduce_fusion.where_ref
  2.3 131.5 %forward_and_head.1 = (bf16[768,128,128]{2,1,0:T(8,128)(2,1)}, bf16[256,128,128]{2,1,0:T(8,128)(2,1)}, f32[128,1024]{1,0:T(8,128)}, bf16[16,1024]{1,0:T(8,128)(2...) custom-call(s32[768]{0:T(1024)} %select_reduce_fusion.where_ref, ...), custom_call_target="tpu_custom_call" | custom-call | tf_op jit(solution)/shard_map/forward_and_head/pallas_call | solution.py:1771
  133.7 33.4 %layer_backward.1 = (bf16[768,128,128]{2,1,0:T(8,128)(2,1)}, bf16[128,16,128]{2,1,0:T(8,128)(2,1)}, bf16[128,1024]{1,0:T(8,128)(2,1)}) custom-call(s32[768]{0:T(1024)} %select_reduce_fusion.where_ref, s32[16,32]{1,0:T(8,128)} %bitcast.13, bf16[768,128,128]{2,1,0:T(8,128)(2,1)} %get-tuple-element.53.full_ref, ...), custom_call_target="tpu_custom_call" | custom-call | tf_op jit(solution)/shard_map/layer_backward/pallas_call | solution.py:2021
  167.1 99.1 %reduce_and_scatter.1 = (f32[3,2,128,128]{3,2,1,0:T(8,128)}, f32[1600,256]{1,0:T(8,128)}, f32[2,2,4,4,4,8,128]{6,5,4,3,2,1,0:T(8,128)}, f32[6,128,128]{2,1,0:T(8...) custom-call(bf16[3,2,4,32,128,128]{5,4,3,2,1,0:T(8,128)(2,1)} %bitcast.8, ...), custom_call_target="tpu_custom_call" | custom-call | tf_op jit(solution)/shard_map/reduce_and_scatter/pallas_call | solution.py:1363
  266.2 8.7 %optimizer_update.1 = (f32[1,1]{1,0:T(1,128)}, f32[1,1]{1,0:T(1,128)}, f32[6,128,128]{2,1,0:T(8,128)}, f32[6,128,128]{2,1,0:T(8,128)}, f32[6,128,128]{2,1,0:T(8,...) custom-call(f32[8,128]{1,0:T(8,128)} %get-tuple-element.69.refs_0_, ...), custom_call_target="tpu_custom_call" | custom-call | tf_op jit(solution)/shard_map/optimizer_update/pallas_call | solution.py:2197

commit v6 on v5

--- a/solution.py
+++ b/solution.py
@@ -1883,7 +1883,7 @@
     own = lax.axis_index("vocab")
     positions = [at_ref[i, own] for i in range(count)]
 
-    def weight_grad(matrix, rows, left_ref, right, together=4):
+    def weight_grad(matrix, rows, left_ref, right, together=8):
         first, in_row = matrix
 
         @pl.loop(0, rows // together)

time: 275 us -> 275 us (level)
  no operation moved by 1% of the time
where the time goes in v6:
time: 275 us
  Pallas kernels  272 us (99%)
    pallas_call x1, Pallas kernels, forward_call(): pl.pallas_call(forward_kernel, name='forward_and_head', out_shape=(shape(...  131 us
    pallas_call x1, Pallas kernels, finish_call(): pl.pallas_call(finish_kernel, name='reduce_and_scatter', out_shape=(jax.S...  99.4 us
    pallas_call x1, Pallas kernels, backward_call(): pl.pallas_call(backward_kernel, name='layer_backward', out_shape=(shape(f...  32.7 us
    pallas_call x1, Pallas kernels, update_call(): pl.pallas_call(update_kernel, name='optimizer_update', out_shape=(scalar,...  8.66 us

profile of v6, /device:TPU:1, one launch (start us, length us, event | category | flops | bytes accessed | tf_op | source)
XLA Modules:
  0.0 274.8 jit_solution(5776693396395668162)
XLA Ops:
  0.6 1.6 select_reduce_fusion.where_ref
  2.3 131.5 %forward_and_head.1 = (bf16[768,128,128]{2,1,0:T(8,128)(2,1)}, bf16[256,128,128]{2,1,0:T(8,128)(2,1)}, f32[128,1024]{1,0:T(8,128)}, bf16[16,1024]{1,0:T(8,128)(2...) custom-call(s32[768]{0:T(1024)} %select_reduce_fusion.where_ref, ...), custom_call_target="tpu_custom_call" | custom-call | tf_op jit(solution)/shard_map/forward_and_head/pallas_call | solution.py:1771
  133.7 32.7 %layer_backward.1 = (bf16[768,128,128]{2,1,0:T(8,128)(2,1)}, bf16[128,16,128]{2,1,0:T(8,128)(2,1)}, bf16[128,1024]{1,0:T(8,128)(2,1)}) custom-call(s32[768]{0:T(1024)} %select_reduce_fusion.where_ref, s32[16,32]{1,0:T(8,128)} %bitcast.13, bf16[768,128,128]{2,1,0:T(8,128)(2,1)} %get-tuple-element.53.full_ref, ...), custom_call_target="tpu_custom_call" | custom-call | tf_op jit(solution)/shard_map/layer_backward/pallas_call | solution.py:2021
  166.5 99.4 %reduce_and_scatter.1 = (f32[3,2,128,128]{3,2,1,0:T(8,128)}, f32[1600,256]{1,0:T(8,128)}, f32[2,2,4,4,4,8,128]{6,5,4,3,2,1,0:T(8,128)}, f32[6,128,128]{2,1,0:T(8...) custom-call(bf16[3,2,4,32,128,128]{5,4,3,2,1,0:T(8,128)(2,1)} %bitcast.8, ...), custom_call_target="tpu_custom_call" | custom-call | tf_op jit(solution)/shard_map/reduce_and_scatter/pallas_call | solution.py:1363
  265.9 8.7 %optimizer_update.1 = (f32[1,1]{1,0:T(1,128)}, f32[1,1]{1,0:T(1,128)}, f32[6,128,128]{2,1,0:T(8,128)}, f32[6,128,128]{2,1,0:T(8,128)}, f32[6,128,128]{2,1,0:T(8,...) custom-call(f32[8,128]{1,0:T(8,128)} %get-tuple-element.69.refs_0_, ...), custom_call_target="tpu_custom_call" | custom-call | tf_op jit(solution)/shard_map/optimizer_update/pallas_call | solution.py:2197
